TPU v7x, 32 devices: a whole 2x2x4 slice. The times are simulated.
32 devices in a mesh: row: 4 (over x, core), col: 8 (over z, y).
Axes of the slice: x: 2, y: 2, z: 4, core: 2. Of those that a mesh axis runs over, the one named last changes fastest.
Arguments:
- latents: bfloat16 [64, 64, 16], P('row', 'col'), may hold values from -6 to 6
- captions: bfloat16 [256, 4096], replicated, may hold values from -6 to 6
- item_heights: int32 [21], replicated, may hold values from 1 to 8, 64 in all
- item_bands: int32 [21], replicated, may hold values from 0 to 7
- embedding: bfloat16 [144, 1536], P(None, 'col'), may hold values from -0.5 to 0.5
- embed_bias: bfloat16 [1536], P('col'), may hold values from -2 to 2
- band_table: bfloat16 [8, 1536], P(None, 'col'), may hold values from -6 to 6
- adaptive: bfloat16 [1536, 6144], P('col'), may hold values from -0.15625 to 0.15625
- adaptive_bias: bfloat16 [6144], P('col'), may hold values from -2 to 2
- attention_gain: bfloat16 [1536], P('col'), may hold values from 0.5 to 1.5
- projection: bfloat16 [1536, 4608], P('col'), may hold values from -0.15625 to 0.15625
- query_gain: bfloat16 [1536], P('col'), may hold values from 0.5 to 1.5
- key_gain: bfloat16 [1536], P('col'), may hold values from 0.5 to 1.5
- cross_query: bfloat16 [1536, 1536], P('col'), may hold values from -0.15625 to 0.15625
- caption_weight: bfloat16 [4096, 3072], P('col'), may hold values from -0.09375 to 0.09375
- cross_gate: bfloat16 [1536], P('col'), may hold values from -1.5 to 1.5
- output_weight: bfloat16 [1536, 1536], P('col'), may hold values from -1.25 to 1.25
- feedforward_gain: bfloat16 [1536], P('col'), may hold values from 0.5 to 1.5
- gate_weight: bfloat16 [1536, 4096], P('col'), may hold values from -0.15625 to 0.15625
- up_weight: bfloat16 [1536, 4096], P('col'), may hold values from -0.15625 to 0.15625
- down_weight: bfloat16 [4096, 1536], P('col'), may hold values from -0.09375 to 0.09375
- unpatch_weight: bfloat16 [1536, 144], P('col'), may hold values from -0.15625 to 0.15625
- cotangent: bfloat16 [64, 64, 16], P('row', 'col'), may hold values from -6 to 6
Outputs:
- prediction: bfloat16 [64, 64, 16], P('row', 'col')
- latent_grad: bfloat16 [64, 64, 16], P('row', 'col')
- grad_embedding: float32 [144, 1536], P(None, ('row', 'col'))
- grad_embed_bias: float32 [1536], P(('row', 'col'))
- grad_band_table: float32 [8, 1536], P(None, ('row', 'col'))
- grad_adaptive: float32 [1536, 6144], P(('row', 'col'))
- grad_adaptive_bias: float32 [6144], P(('row', 'col'))
- grad_attention_gain: float32 [1536], P(('row', 'col'))
- grad_projection: float32 [1536, 4608], P(('row', 'col'))
- grad_query_gain: float32 [1536], P(('row', 'col'))
- grad_key_gain: float32 [1536], P(('row', 'col'))
- grad_cross_query: float32 [1536, 1536], P(('row', 'col'))
- grad_caption_weight: float32 [4096, 3072], P(('row', 'col'))
- grad_cross_gate: float32 [1536], P(('row', 'col'))
- grad_output_weight: float32 [1536, 1536], P(('row', 'col'))
- grad_feedforward_gain: float32 [1536], P(('row', 'col'))
- grad_gate_weight: float32 [1536, 4096], P(('row', 'col'))
- grad_up_weight: float32 [1536, 4096], P(('row', 'col'))
- grad_down_weight: float32 [4096, 1536], P(('row', 'col'))
- grad_unpatch_weight: float32 [1536, 144], P(('row', 'col'))
Inputs may be any that keep to these rules, and one draw needn't show every extreme that they name: `item_heights`: item heights in grid rows, summing to 64; the tallest item has exactly 8 rows.
All inputs are finite; a program needn't handle non-finite values.
Results may differ from a plain program's by a relative error of at most 0.025.
Values may be sent and summed in bfloat16 or wider, within the bound.
No kernel may reach another device: no remote copies, remote signals or barrier semaphores. Data moves between devices by JAX's collectives and lax.ppermute only.
A program may use at most 704 MiB of HBM per device.

v0:
```python
import math

import jax
import jax.numpy as jnp
import numpy as np
from jax import lax
from jax.sharding import PartitionSpec as P

HD = 64
TXT = 256
NBAND = 8
MOSTH = 8
RB = 4


EPS = 1e-06
THETA = 10000.0
NEG = -1e30
HIGH = lax.Precision.HIGHEST
OFFSETS = ((-1, -1), (-1, 0), (-1, 1), (0, -1), (0, 0), (0, 1), (1, -1), (1, 0), (1, 1))


def with_halo(cells, sides, width):
    for axis, dim in sides:
        count = lax.axis_size(axis)
        ends = count - 1
        head = lax.slice_in_dim(cells, 0, width, axis=dim)
        tail = lax.slice_in_dim(cells, cells.shape[dim] - width, cells.shape[dim], axis=dim)
        cells = jnp.concatenate(
            [
                lax.ppermute(tail, axis, [(i, (i + 1) % count) for i in range(ends)]),
                cells,
                lax.ppermute(head, axis, [((i + 1) % count, i) for i in range(ends)]),
            ],
            axis=dim,
        )
    return cells


def norm_rows(values):
    return values * lax.rsqrt(jnp.mean(values * values, axis=-1, keepdims=True) + EPS)


def norm_back(source, grad_normed, gain_full):
    inverse = lax.rsqrt(jnp.mean(source * source, axis=-1, keepdims=True) + EPS)
    unit = source * inverse
    grad_unit = grad_normed * gain_full
    return (inverse * (grad_unit - unit * jnp.mean(grad_unit * unit, axis=-1, keepdims=True)), unit)


def silu_slope(values):
    sigmoid = jax.nn.sigmoid(values)
    return sigmoid * (1.0 + values * (1.0 - sigmoid))


def contract(left_mat, right_mat, precision=None):
    flat_left = left_mat.reshape(-1, left_mat.shape[-1])
    flat_right = right_mat.reshape(-1, right_mat.shape[-1])
    return lax.dot_general(
        flat_left,
        flat_right,
        (((0,), (0,)), ((), ())),
        precision=precision,
        preferred_element_type=jnp.float32,
    )


def back_dot(grad_in, weight):
    return lax.dot_general(
        grad_in, weight, (((grad_in.ndim - 1,), (1,)), ((), ())), preferred_element_type=jnp.float32
    )


def gather_cells(padded, row_count, col_count):
    return jnp.concatenate(
        [
            padded[1 + row_off : 1 + row_off + row_count, 1 + col_off : 1 + col_off + col_count]
            for row_off, col_off in OFFSETS
        ],
        axis=-1,
    )


def spread_cells(padded, row_count, col_count, channels):
    summed = jnp.zeros((row_count, col_count, channels), jnp.float32)
    for offset_index, (row_off, col_off) in enumerate(OFFSETS):
        summed = summed + padded[
            1 - row_off : 1 - row_off + row_count,
            1 - col_off : 1 - col_off + col_count,
            offset_index * channels : (offset_index + 1) * channels,
        ].astype(jnp.float32)
    return summed


def row_items(heights, band_ids, row_count):
    item_ends = jnp.cumsum(heights)
    row_ids = jnp.arange(row_count, dtype=jnp.int32)
    item_of_row = jnp.sum((item_ends[None, :] <= row_ids[:, None]).astype(jnp.int32), axis=1)
    picked = item_of_row[:, None] == jnp.arange(heights.shape[0], dtype=jnp.int32)[None, :]
    item_top = jnp.sum(jnp.where(picked, (item_ends - heights)[None, :], 0), axis=1)
    row_band = jnp.sum(jnp.where(picked, band_ids[None, :], 0), axis=1)
    band_onehot = (row_band[:, None] == jnp.arange(NBAND, dtype=jnp.int32)[None, :]).astype(
        jnp.float32
    )
    return (item_of_row, row_ids - item_top, band_onehot)


def rope_tables(row_place, col_place, head_dim):
    quarter = head_dim // 4
    frequency = THETA ** (-jnp.arange(quarter, dtype=jnp.float32) / quarter)
    angle_rows = row_place.astype(jnp.float32)[:, None] * frequency
    angle_cols = col_place.astype(jnp.float32)[:, None] * frequency
    return (jnp.cos(angle_rows), jnp.sin(angle_rows), jnp.cos(angle_cols), jnp.sin(angle_cols))


def rotate(values, tables):
    cos_rows, sin_rows, cos_cols, sin_cols = tables
    quarter = values.shape[-1] // 4
    first, second, third, fourth = (
        values[..., segment * quarter : (segment + 1) * quarter] for segment in range(4)
    )
    cos_r = cos_rows[:, None, None, :]
    sin_r = sin_rows[:, None, None, :]
    cos_c = cos_cols[None, :, None, :]
    sin_c = sin_cols[None, :, None, :]
    return jnp.concatenate(
        [
            first * cos_r - second * sin_r,
            first * sin_r + second * cos_r,
            third * cos_c - fourth * sin_c,
            third * sin_c + fourth * cos_c,
        ],
        axis=-1,
    )


def head_norm(raw_heads, gain_vec, tables):
    shaped = gain_vec.reshape(raw_heads.shape[2], raw_heads.shape[3])
    return rotate(norm_rows(raw_heads) * shaped, tables)


def on_device(
    latents,
    captions,
    item_heights,
    item_bands,
    embedding,
    embed_bias,
    band_table,
    adaptive,
    adaptive_bias,
    attention_gain,
    projection,
    query_gain,
    key_gain,
    cross_query,
    caption_weight,
    cross_gate,
    output_weight,
    feedforward_gain,
    gate_weight,
    up_weight,
    down_weight,
    unpatch_weight,
    cotangent,
):
    whole = (
        lax.all_gather(embedding, "col", axis=1, tiled=True),
        lax.all_gather(embed_bias, "col", axis=0, tiled=True),
        lax.all_gather(band_table, "col", axis=1, tiled=True),
        lax.all_gather(adaptive, "col", axis=0, tiled=True),
        lax.all_gather(adaptive_bias, "col", axis=0, tiled=True),
        lax.all_gather(attention_gain, "col", axis=0, tiled=True),
        lax.all_gather(projection, "col", axis=0, tiled=True),
        lax.all_gather(query_gain, "col", axis=0, tiled=True),
        lax.all_gather(key_gain, "col", axis=0, tiled=True),
        lax.all_gather(cross_query, "col", axis=0, tiled=True),
        lax.all_gather(caption_weight, "col", axis=0, tiled=True),
        lax.all_gather(cross_gate, "col", axis=0, tiled=True),
        lax.all_gather(output_weight, "col", axis=0, tiled=True),
        lax.all_gather(feedforward_gain, "col", axis=0, tiled=True),
        lax.all_gather(gate_weight, "col", axis=0, tiled=True),
        lax.all_gather(up_weight, "col", axis=0, tiled=True),
        lax.all_gather(down_weight, "col", axis=0, tiled=True),
        lax.all_gather(unpatch_weight, "col", axis=0, tiled=True),
    )
    (
        full_embedding,
        full_embed_bias,
        full_band_table,
        full_adaptive,
        full_adaptive_bias,
        full_attention_gain,
        full_projection,
        full_query_gain,
        full_key_gain,
        full_cross_query,
        full_caption_weight,
        full_cross_gate,
        full_output_weight,
        full_feedforward_gain,
        full_gate_weight,
        full_up_weight,
        full_down_weight,
        full_unpatch_weight,
    ) = whole
    f32 = jnp.float32
    bf16 = jnp.bfloat16
    tile_rows, tile_cols, channels = (latents.shape[0], latents.shape[1], latents.shape[2])
    row_index = lax.axis_index("row")
    col_index = lax.axis_index("col")
    grid_rows = tile_rows * lax.axis_size("row")
    model_width = full_embed_bias.shape[0]
    score_scale = 1.0 / math.sqrt(HD)
    item_of_row, row_place, band_onehot = row_items(item_heights, item_bands, grid_rows)
    band_wide = full_band_table.astype(f32)
    modulations = jnp.dot(
        jax.nn.silu(band_wide), full_adaptive.astype(f32), precision=HIGH
    ) + full_adaptive_bias.astype(f32)
    tile_onehot = lax.dynamic_slice_in_dim(band_onehot, row_index * tile_rows, tile_rows, 0)
    tile_modulation = jnp.dot(tile_onehot, modulations, precision=HIGH)[:, None, :]
    first_scale = tile_modulation[..., 0:model_width]
    first_gate = tile_modulation[..., model_width : 2 * model_width]
    second_scale = tile_modulation[..., 2 * model_width : 3 * model_width]
    second_gate = tile_modulation[..., 3 * model_width : 4 * model_width]
    joined = jnp.concatenate([latents, cotangent], axis=-1)
    bordered = with_halo(joined, (("row", 0), ("col", 1)), 1)
    neighbours = gather_cells(bordered[..., 0:channels], tile_rows, tile_cols)
    patch_grads = gather_cells(bordered[..., channels : 2 * channels], tile_rows, tile_cols)
    embedded = jnp.dot(
        neighbours, full_embedding, preferred_element_type=f32
    ) + full_embed_bias.astype(f32)
    attn_gain = full_attention_gain.astype(f32)
    normed = (norm_rows(embedded) * attn_gain * (1.0 + first_scale)).astype(bf16)
    triple = jnp.dot(normed, full_projection, preferred_element_type=f32)
    queries_raw = triple[..., 0:model_width].astype(bf16)
    keys_raw = triple[..., model_width : 2 * model_width].astype(bf16)
    values_raw = triple[..., 2 * model_width : 3 * model_width].astype(bf16)
    cross_raw = jnp.dot(normed, full_cross_query, preferred_element_type=f32).astype(bf16)
    heads_query, heads_key, heads_value, heads_cross = (
        lax.all_to_all(queries_raw, "row", split_axis=2, concat_axis=0, tiled=True),
        lax.all_to_all(keys_raw, "row", split_axis=2, concat_axis=0, tiled=True),
        lax.all_to_all(values_raw, "row", split_axis=2, concat_axis=0, tiled=True),
        lax.all_to_all(cross_raw, "row", split_axis=2, concat_axis=0, tiled=True),
    )
    head_width = heads_query.shape[2]
    head_count = head_width // HD
    slice_start = row_index * head_width
    col_place = col_index * tile_cols + jnp.arange(tile_cols, dtype=jnp.int32)
    tables = rope_tables(row_place, col_place, HD)

    def shape_heads(values):
        return values.reshape(grid_rows, tile_cols, head_count, HD)

    gain_query = lax.dynamic_slice_in_dim(full_query_gain.astype(f32), slice_start, head_width, 0)
    gain_key = lax.dynamic_slice_in_dim(full_key_gain.astype(f32), slice_start, head_width, 0)
    query_source = shape_heads(heads_query).astype(f32)
    key_source = shape_heads(heads_key).astype(f32)
    queries = head_norm(query_source, gain_query, tables).astype(bf16)
    keys = head_norm(key_source, gain_key, tables).astype(bf16)
    values = shape_heads(heads_value)
    block_count = grid_rows // RB
    window = RB + 2 * (MOSTH - 1)
    query_len = RB * tile_cols
    window_rows = (
        np.clip(np.arange(block_count) * RB - (MOSTH - 1), 0, grid_rows - window)[:, None]
        + np.arange(window)[None, :]
    )
    row_blocks = item_of_row.reshape(block_count, RB)
    window_items = item_of_row[window_rows]

    def in_blocks(source):
        return source.reshape(block_count, RB * source.shape[1], source.shape[2], source.shape[3])

    def in_windows(source):
        return source[window_rows].reshape(
            block_count, window * source.shape[1], source.shape[2], source.shape[3]
        )

    def same_item(query_cols, key_cols):
        return (
            jnp.repeat(row_blocks, query_cols, axis=1)[:, :, None]
            == jnp.repeat(window_items, key_cols, axis=1)[:, None, :]
        )[:, None]

    def stats_blocks(source):
        return source.reshape(block_count, RB * source.shape[1], source.shape[2]).transpose(0, 2, 1)

    block_queries = in_blocks(queries)
    start_best = jnp.full((block_count, head_count, query_len), NEG, f32)
    start_sum = jnp.zeros((block_count, head_count, query_len), f32)
    start_acc = jnp.zeros((block_count, head_count, query_len, HD), f32)
    part_keys = lax.all_gather(keys, "col", axis=1, tiled=True)
    part_values = lax.all_gather(values, "col", axis=1, tiled=True)
    part_cols = part_keys.shape[1]
    same_mask = same_item(tile_cols, part_cols)
    scores = (
        jnp.einsum(
            "bqhd,bkhd->bhqk", block_queries, in_windows(part_keys), preferred_element_type=f32
        )
        * score_scale
    )
    scores = jnp.where(same_mask, scores, NEG)
    best_score = start_best
    summed = start_sum
    gathered = start_acc
    newest = jnp.maximum(best_score, jnp.max(scores, axis=-1))
    weights = jnp.where(same_mask, jnp.exp(scores - newest[..., None]), 0.0)
    factor = jnp.exp(best_score - newest)
    summed = summed * factor + jnp.sum(weights, axis=-1)
    gathered = gathered * factor[..., None] + jnp.einsum(
        "bhqk,bkhd->bhqd", weights.astype(bf16), in_windows(part_values), preferred_element_type=f32
    )
    best_score, summed, gathered = (newest, summed, gathered)
    log_total = best_score + jnp.log(summed)
    self_out = (
        (gathered / summed[..., None])
        .transpose(0, 2, 1, 3)
        .reshape(grid_rows, tile_cols, head_width)
    )
    caption_keys = (
        jnp.dot(
            captions,
            lax.dynamic_slice_in_dim(full_caption_weight, slice_start, head_width, 1),
            preferred_element_type=f32,
        )
        .astype(bf16)
        .reshape(TXT, head_count, HD)
    )
    caption_values = (
        jnp.dot(
            captions,
            lax.dynamic_slice_in_dim(full_caption_weight, model_width + slice_start, head_width, 1),
            preferred_element_type=f32,
        )
        .astype(bf16)
        .reshape(TXT, head_count, HD)
    )
    cross_tokens = heads_cross.reshape(grid_rows * tile_cols, head_count, HD)
    cross_scores = (
        jnp.einsum("qhd,khd->hqk", cross_tokens, caption_keys, preferred_element_type=f32)
        * score_scale
    )
    cross_weights = jnp.exp(cross_scores - jnp.max(cross_scores, axis=-1, keepdims=True))
    cross_probability = cross_weights / jnp.sum(cross_weights, axis=-1, keepdims=True)
    cross_low = cross_probability.astype(bf16)
    crossed = jnp.einsum(
        "hqk,khd->qhd", cross_low, caption_values, preferred_element_type=f32
    ).reshape(grid_rows, tile_cols, head_width)
    gate_slice = jnp.tanh(
        lax.dynamic_slice_in_dim(full_cross_gate.astype(f32), slice_start, head_width, 0)
    )
    mixed = (self_out + gate_slice * crossed).astype(bf16)
    mixed_tile = lax.all_to_all(mixed, "row", split_axis=0, concat_axis=2, tiled=True)
    branch = jnp.dot(mixed_tile, full_output_weight, preferred_element_type=f32)
    tanh_one = jnp.tanh(first_gate)
    residual = embedded + tanh_one * branch
    ff_gain = full_feedforward_gain.astype(f32)
    inner = (norm_rows(residual) * ff_gain * (1.0 + second_scale)).astype(bf16)
    gate = jnp.dot(inner, full_gate_weight, preferred_element_type=f32)
    upward = jnp.dot(inner, full_up_weight, preferred_element_type=f32)
    hidden = (jax.nn.silu(gate) * upward).astype(bf16)
    feed = jnp.dot(hidden, full_down_weight, preferred_element_type=f32)
    tanh_two = jnp.tanh(second_gate)
    result_low = (residual + tanh_two * feed).astype(bf16)
    patches = jnp.dot(result_low, full_unpatch_weight, preferred_element_type=f32).astype(bf16)
    patch_border = with_halo(patches, (("row", 0), ("col", 1)), 1)
    prediction = spread_cells(patch_border, tile_rows, tile_cols, channels).astype(bf16)
    again_set = (
        lax.all_gather(embedding, "col", axis=1, tiled=True),
        lax.all_gather(embed_bias, "col", axis=0, tiled=True),
        lax.all_gather(band_table, "col", axis=1, tiled=True),
        lax.all_gather(adaptive, "col", axis=0, tiled=True),
        lax.all_gather(adaptive_bias, "col", axis=0, tiled=True),
        lax.all_gather(attention_gain, "col", axis=0, tiled=True),
        lax.all_gather(projection, "col", axis=0, tiled=True),
        lax.all_gather(query_gain, "col", axis=0, tiled=True),
        lax.all_gather(key_gain, "col", axis=0, tiled=True),
        lax.all_gather(cross_query, "col", axis=0, tiled=True),
        lax.all_gather(caption_weight, "col", axis=0, tiled=True),
        lax.all_gather(cross_gate, "col", axis=0, tiled=True),
        lax.all_gather(output_weight, "col", axis=0, tiled=True),
        lax.all_gather(feedforward_gain, "col", axis=0, tiled=True),
        lax.all_gather(gate_weight, "col", axis=0, tiled=True),
        lax.all_gather(up_weight, "col", axis=0, tiled=True),
        lax.all_gather(down_weight, "col", axis=0, tiled=True),
        lax.all_gather(unpatch_weight, "col", axis=0, tiled=True),
    )
    (
        full_embedding,
        full_embed_bias,
        full_band_table,
        full_adaptive,
        full_adaptive_bias,
        full_attention_gain,
        full_projection,
        full_query_gain,
        full_key_gain,
        full_cross_query,
        full_caption_weight,
        full_cross_gate,
        full_output_weight,
        full_feedforward_gain,
        full_gate_weight,
        full_up_weight,
        full_down_weight,
        full_unpatch_weight,
    ) = again_set
    grad_unpatch = contract(result_low, patch_grads)
    grad_result = back_dot(patch_grads, full_unpatch_weight)
    grad_feed = (tanh_two * grad_result).astype(bf16)
    grad_second_gate = grad_result * feed * (1.0 - tanh_two * tanh_two)
    grad_down = contract(hidden, grad_feed)
    grad_hidden = back_dot(grad_feed, full_down_weight)
    grad_gate = (grad_hidden * upward * silu_slope(gate)).astype(bf16)
    grad_upward = (grad_hidden * jax.nn.silu(gate)).astype(bf16)
    grad_gate_weight = contract(inner, grad_gate)
    grad_up_weight = contract(inner, grad_upward)
    grad_inner = back_dot(grad_gate, full_gate_weight) + back_dot(grad_upward, full_up_weight)
    grad_residual_norm, unit_two = norm_back(residual, grad_inner, ff_gain * (1.0 + second_scale))
    grad_ff_gain = jnp.sum(grad_inner * (1.0 + second_scale) * unit_two, axis=(0, 1))
    grad_second_scale = grad_inner * ff_gain * unit_two
    grad_residual = grad_result + grad_residual_norm
    grad_branch = (tanh_one * grad_residual).astype(bf16)
    grad_first_gate = grad_residual * branch * (1.0 - tanh_one * tanh_one)
    grad_output = contract(mixed_tile, grad_branch)
    grad_mixed = back_dot(grad_branch, full_output_weight).astype(bf16)
    grad_heads = lax.all_to_all(grad_mixed, "row", split_axis=2, concat_axis=0, tiled=True)
    grad_heads_wide = grad_heads.astype(f32)
    grad_gate_part = jnp.sum(
        grad_heads_wide * crossed * (1.0 - gate_slice * gate_slice), axis=(0, 1)
    )
    grad_crossed = (
        (gate_slice * grad_heads_wide).astype(bf16).reshape(grid_rows * tile_cols, head_count, HD)
    )
    grad_cross_prob = jnp.einsum(
        "qhd,khd->hqk", grad_crossed, caption_values, preferred_element_type=f32
    )
    grad_cross_scores = (
        cross_probability
        * (grad_cross_prob - jnp.sum(cross_probability * grad_cross_prob, axis=-1, keepdims=True))
    ).astype(bf16)
    grad_cross_tokens = (
        (
            jnp.einsum("hqk,khd->qhd", grad_cross_scores, caption_keys, preferred_element_type=f32)
            * score_scale
        )
        .astype(bf16)
        .reshape(grid_rows, tile_cols, head_width)
    )
    grad_caption_keys = (
        jnp.einsum(
            "hqk,qhd->khd", grad_cross_scores, cross_tokens, preferred_element_type=f32
        ).reshape(TXT, head_width)
        * score_scale
    )
    grad_caption_values = jnp.einsum(
        "hqk,qhd->khd", cross_low, grad_crossed, preferred_element_type=f32
    ).reshape(TXT, head_width)
    captions_wide = captions.astype(f32)
    grad_heads_split = shape_heads(grad_heads)
    delta_tokens = jnp.sum(
        grad_heads_wide.reshape(grid_rows, tile_cols, head_count, HD)
        * self_out.reshape(grid_rows, tile_cols, head_count, HD),
        axis=-1,
    )
    lse_tokens = log_total.transpose(0, 2, 1).reshape(grid_rows, tile_cols, head_count)
    all_lse, all_delta = (
        lax.all_gather(lse_tokens, "col", axis=1, tiled=True),
        lax.all_gather(delta_tokens, "col", axis=1, tiled=True),
    )
    block_grads = in_blocks(grad_heads_split)
    delta_blocks = stats_blocks(delta_tokens)
    part_keys = lax.all_gather(keys, "col", axis=1, tiled=True)
    part_values = lax.all_gather(values, "col", axis=1, tiled=True)
    part_cols = part_keys.shape[1]
    same_mask = same_item(tile_cols, part_cols)
    window_keys = in_windows(part_keys)
    scores = (
        jnp.einsum("bqhd,bkhd->bhqk", block_queries, window_keys, preferred_element_type=f32)
        * score_scale
    )
    probability = jnp.where(same_mask, jnp.exp(scores - log_total[..., None]), 0.0)
    grad_prob = jnp.einsum(
        "bqhd,bkhd->bhqk", block_grads, in_windows(part_values), preferred_element_type=f32
    )
    grad_scores = (probability * (grad_prob - delta_blocks[..., None])).astype(bf16)
    grad_query_blocks = start_acc + jnp.einsum(
        "bhqk,bkhd->bhqd", grad_scores, window_keys, preferred_element_type=f32
    )
    local_keys = in_windows(keys)
    local_values = in_windows(values)
    window_zero = jnp.zeros((block_count, window * tile_cols, head_count, HD), f32)
    part_queries = lax.all_gather(queries, "col", axis=1, tiled=True)
    part_grads = lax.all_gather(grad_heads_split, "col", axis=1, tiled=True)
    part_cols = part_queries.shape[1]
    part_lse = stats_blocks(all_lse)
    part_delta = stats_blocks(all_delta)
    same_mask = same_item(part_cols, tile_cols)
    queries_part = in_blocks(part_queries)
    grads_part = in_blocks(part_grads)
    scores = (
        jnp.einsum("bqhd,bkhd->bhqk", queries_part, local_keys, preferred_element_type=f32)
        * score_scale
    )
    probability = jnp.where(same_mask, jnp.exp(scores - part_lse[..., None]), 0.0)
    grad_values_part = jnp.einsum(
        "bhqk,bqhd->bkhd", probability.astype(bf16), grads_part, preferred_element_type=f32
    )
    grad_prob = jnp.einsum("bqhd,bkhd->bhqk", grads_part, local_values, preferred_element_type=f32)
    grad_scores = (probability * (grad_prob - part_delta[..., None])).astype(bf16)
    grad_keys_part = jnp.einsum(
        "bhqk,bqhd->bkhd", grad_scores, queries_part, preferred_element_type=f32
    )
    window_keys_grad = window_zero + grad_keys_part
    window_values_grad = window_zero + grad_values_part

    def from_windows(source):
        shaped = source.reshape(block_count, window, tile_cols, head_count, HD)
        return jnp.zeros((grid_rows, tile_cols, head_count, HD), f32).at[window_rows].add(shaped)

    grad_key_norm = (from_windows(window_keys_grad) * score_scale).astype(bf16)
    grad_value_heads = (
        from_windows(window_values_grad).astype(bf16).reshape(grid_rows, tile_cols, head_width)
    )
    grad_query_norm = (
        grad_query_blocks.transpose(0, 2, 1, 3).reshape(grid_rows, tile_cols, head_count, HD)
        * score_scale
    ).astype(bf16)
    normed_query, query_pull = jax.vjp(
        lambda source, gain_vec: head_norm(source, gain_vec, tables), query_source, gain_query
    )
    normed_key, key_pull = jax.vjp(
        lambda source, gain_vec: head_norm(source, gain_vec, tables), key_source, gain_key
    )
    grad_query_source, grad_query_gain_part = query_pull(grad_query_norm.astype(f32))
    grad_key_source, grad_key_gain_part = key_pull(grad_key_norm.astype(f32))
    grad_query_tile, grad_key_tile, grad_value_tile, grad_cross_tile = (
        lax.all_to_all(
            grad_query_source.astype(bf16).reshape(grid_rows, tile_cols, head_width),
            "row",
            split_axis=0,
            concat_axis=2,
            tiled=True,
        ),
        lax.all_to_all(
            grad_key_source.astype(bf16).reshape(grid_rows, tile_cols, head_width),
            "row",
            split_axis=0,
            concat_axis=2,
            tiled=True,
        ),
        lax.all_to_all(grad_value_heads, "row", split_axis=0, concat_axis=2, tiled=True),
        lax.all_to_all(grad_cross_tokens, "row", split_axis=0, concat_axis=2, tiled=True),
    )
    grad_triple = jnp.concatenate([grad_query_tile, grad_key_tile, grad_value_tile], axis=-1)
    grad_projection = contract(normed, grad_triple)
    grad_cross_weight = contract(normed, grad_cross_tile)
    grad_normed = back_dot(grad_triple, full_projection) + back_dot(
        grad_cross_tile, full_cross_query
    )
    attn_gain = full_attention_gain.astype(f32)
    grad_embedded_norm, unit_one = norm_back(embedded, grad_normed, attn_gain * (1.0 + first_scale))
    grad_attn_gain = jnp.sum(grad_normed * (1.0 + first_scale) * unit_one, axis=(0, 1))
    grad_first_scale = grad_normed * attn_gain * unit_one
    grad_embedded = (grad_residual + grad_embedded_norm).astype(bf16)
    grad_embedding = contract(neighbours, grad_embedded)
    grad_embed_bias = jnp.sum(grad_embedded.astype(f32), axis=(0, 1))
    grad_cells = back_dot(grad_embedded, full_embedding).astype(bf16)
    cell_border = with_halo(grad_cells, (("row", 0), ("col", 1)), 1)
    latent_grad = spread_cells(cell_border, tile_rows, tile_cols, channels).astype(bf16)
    grad_rows_mod = jnp.sum(
        jnp.concatenate(
            [grad_first_scale, grad_first_gate, grad_second_scale, grad_second_gate], axis=-1
        ),
        axis=1,
    )
    grad_modulations = contract(tile_onehot, grad_rows_mod, HIGH)
    band_wide = full_band_table.astype(f32)
    silu_band = jax.nn.silu(band_wide)
    zero_width = jnp.zeros((model_width,), f32)
    grad_query_gain = lax.dynamic_update_slice_in_dim(
        zero_width, grad_query_gain_part, slice_start, 0
    )
    grad_key_gain = lax.dynamic_update_slice_in_dim(zero_width, grad_key_gain_part, slice_start, 0)
    grad_cross_gate = lax.dynamic_update_slice_in_dim(zero_width, grad_gate_part, slice_start, 0)
    grad_caption = jnp.zeros((captions.shape[1], 2 * model_width), f32)
    grad_caption = lax.dynamic_update_slice_in_dim(
        grad_caption, contract(captions_wide, grad_caption_keys, HIGH), slice_start, 1
    )
    grad_caption = lax.dynamic_update_slice_in_dim(
        grad_caption,
        contract(captions_wide, grad_caption_values, HIGH),
        model_width + slice_start,
        1,
    )
    grad_adaptive = contract(silu_band, grad_modulations, HIGH)
    grad_adaptive_bias = jnp.sum(grad_modulations, axis=0)
    grad_band_table = lax.dot_general(
        grad_modulations, full_adaptive.astype(f32), (((1,), (1,)), ((), ())), precision=HIGH
    ) * silu_slope(band_wide)
    summed_grads = (
        lax.psum_scatter(grad_embedding, ("row", "col"), scatter_dimension=1, tiled=True),
        lax.psum_scatter(grad_embed_bias, ("row", "col"), scatter_dimension=0, tiled=True),
        lax.psum_scatter(grad_band_table, ("row", "col"), scatter_dimension=1, tiled=True),
        lax.psum_scatter(grad_adaptive, ("row", "col"), scatter_dimension=0, tiled=True),
        lax.psum_scatter(grad_adaptive_bias, ("row", "col"), scatter_dimension=0, tiled=True),
        lax.psum_scatter(grad_attn_gain, ("row", "col"), scatter_dimension=0, tiled=True),
        lax.psum_scatter(grad_projection, ("row", "col"), scatter_dimension=0, tiled=True),
        lax.psum_scatter(grad_query_gain, ("row", "col"), scatter_dimension=0, tiled=True),
        lax.psum_scatter(grad_key_gain, ("row", "col"), scatter_dimension=0, tiled=True),
        lax.psum_scatter(grad_cross_weight, ("row", "col"), scatter_dimension=0, tiled=True),
        lax.psum_scatter(grad_caption, ("row", "col"), scatter_dimension=0, tiled=True),
        lax.psum_scatter(grad_cross_gate, ("row", "col"), scatter_dimension=0, tiled=True),
        lax.psum_scatter(grad_output, ("row", "col"), scatter_dimension=0, tiled=True),
        lax.psum_scatter(grad_ff_gain, ("row", "col"), scatter_dimension=0, tiled=True),
        lax.psum_scatter(grad_gate_weight, ("row", "col"), scatter_dimension=0, tiled=True),
        lax.psum_scatter(grad_up_weight, ("row", "col"), scatter_dimension=0, tiled=True),
        lax.psum_scatter(grad_down, ("row", "col"), scatter_dimension=0, tiled=True),
        lax.psum_scatter(grad_unpatch, ("row", "col"), scatter_dimension=0, tiled=True),
    )
    return (prediction, latent_grad) + tuple(summed_grads)


def solution(mesh):
    in_specs = (
        P("row", "col", None),
        P(),
        P(),
        P(),
        P(None, "col"),
        P("col"),
        P(None, "col"),
        P("col", None),
        P("col"),
        P("col"),
        P("col", None),
        P("col"),
        P("col"),
        P("col", None),
        P("col", None),
        P("col"),
        P("col", None),
        P("col"),
        P("col", None),
        P("col", None),
        P("col", None),
        P("col", None),
        P("row", "col", None),
    )
    out_specs = (
        P("row", "col", None),
        P("row", "col", None),
        P(None, ("row", "col")),
        P(("row", "col")),
        P(None, ("row", "col")),
        P(("row", "col"), None),
        P(("row", "col")),
        P(("row", "col")),
        P(("row", "col"), None),
        P(("row", "col")),
        P(("row", "col")),
        P(("row", "col"), None),
        P(("row", "col"), None),
        P(("row", "col")),
        P(("row", "col"), None),
        P(("row", "col")),
        P(("row", "col"), None),
        P(("row", "col"), None),
        P(("row", "col"), None),
        P(("row", "col"), None),
    )
    return jax.shard_map(
        on_device, mesh=mesh, in_specs=in_specs, out_specs=out_specs, check_vma=False
    )
```

profile of v0, /device:TPU:0, one launch (start us, length us, event | category | flops | bytes accessed | tf_op | source)
XLA Modules:
  0.0 4922.9 jit_solution(18091565780785944020)
XLA Ops:
  14.1 54.4 %all-gather.2 = bf16[8,1,768]{2,1,0:T(2,128)(2,1)S(1)} all-gather(bf16[1,1,768]{2,1,0:T(2,128)(2,1)S(1)} %reshape.582), channel_id=1, replica_groups=mesh['row'=4,'col'=8] {'col'}, dimensions={0}, use_global_device_ids=true | all-gather | bytes 13824 | tf_op jit(solution)/shard_map/all_gather | solution.py:172
  69.1 39.2 all-gather.1
  111.4 50.3 %all-reduce.22 = (bf16[1536]{0:T(1024)(128)(2,1)S(1)}, bf16[1536]{0:T(1024)(128)(2,1)S(1)}, bf16[1536]{0:T(1024)(128)(2,1)S(1)}, bf16[1536]{0:T(1024)(128)(2,1)S...) all-reduce(bf16[1536]{0:T(1024)(128)(2,1)S(1)} %dynamic-update-slic, ...), channel_id=1, replica_groups=mesh['row'=4,'col'=8] {'col'}, use_global_device_ids=true, to_apply=%add.8 | all-reduce | flops 9216 | bytes 36864
  162.0 40.9 all-gather
  217.0 171.5 %all-gather.17.cloned.1.call-done = bf16[1536,6144]{1,0:T(8,128)(2,1)} async-done(((bf16[192,6144]{1,0:T(8,128)(2,1)}), bf16[1536,6144]{1,0:T(8,128)(2,1)}) %all-gather.17.cloned.1.call-update) | async-done | bytes 18874384 | tf_op jit(solution)/shard_map/all_gather | solution.py:171
  401.3 185.1 %all-gather.19.cloned.1.call-done = bf16[1536,4608]{1,0:T(8,128)(2,1)} async-done(((bf16[192,4608]{1,0:T(8,128)(2,1)}), bf16[1536,4608]{1,0:T(8,128)(2,1)}) %all-gather.19.cloned.1.call-update) | async-done | bytes 14155792 | tf_op jit(solution)/shard_map/all_gather | solution.py:174
  663.7 32.8 all-gather.3
  733.8 11.9 all-to-all-start.3
  773.5 21.1 all-gather.23.cloned.1.call-done
  794.6 18.9 gather_fusion.2
  813.6 34.7 copy.559
  848.2 47.0 all-gather.21.cloned.1.call-done
  895.2 16.5 gather_fusion.1
  911.7 38.2 copy.554
  949.9 38.3 reshape.454
  988.2 19.1 select_reduce_fusion
  1015.4 11.5 fusion.89
  1033.1 342.1 %all-gather.25.cloned.1.call-done = bf16[4096,3072]{1,0:T(8,128)(2,1)} async-done(((bf16[512,3072]{1,0:T(8,128)(2,1)}), bf16[4096,3072]{1,0:T(8,128)(2,1)}) %all-gather.25.cloned.1.call-update) | async-done | bytes 25165840 | tf_op jit(solution)/shard_map/all_gather | solution.py:178
  1396.7 157.3 %all-gather.35.cloned.1.call-done = bf16[4096,1536]{1,0:T(8,128)(2,1)} async-done(((bf16[512,1536]{1,0:T(8,128)(2,1)}), bf16[4096,1536]{1,0:T(8,128)(2,1)}) %all-gather.35.cloned.1.call-update) | async-done | bytes 12582928 | tf_op jit(solution)/shard_map/all_gather | solution.py:184
  1568.0 66.2 %all-gather.29.cloned.1.call-done = bf16[1536,1536]{1,0:T(8,128)(2,1)} async-done(((bf16[192,1536]{1,0:T(8,128)(2,1)}), bf16[1536,1536]{1,0:T(8,128)(2,1)}) %all-gather.29.cloned.1.call-update) | async-done | bytes 4718608 | tf_op jit(solution)/shard_map/all_gather | solution.py:180
  1639.4 171.6 %all-gather.33.cloned.1.call-done = bf16[1536,4096]{1,0:T(8,128)(2,1)} async-done(((bf16[192,4096]{1,0:T(8,128)(2,1)}), bf16[1536,4096]{1,0:T(8,128)(2,1)}) %all-gather.33.cloned.1.call-update) | async-done | bytes 12582928 | tf_op jit(solution)/shard_map/all_gather | solution.py:183
  1818.7 169.0 %all-gather.31.cloned.1.call-done = bf16[1536,4096]{1,0:T(8,128)(2,1)} async-done(((bf16[192,4096]{1,0:T(8,128)(2,1)}), bf16[1536,4096]{1,0:T(8,128)(2,1)}) %all-gather.31.cloned.1.call-update) | async-done | bytes 12582928 | tf_op jit(solution)/shard_map/all_gather | solution.py:182
  2008.1 11.1 multiply_reduce_fusion.9
  2057.3 31.6 all-gather.37.cloned.1.call-done
  2108.0 31.2 all_gather.106
  2163.7 21.1 convert_bitcast_fusion
  2187.8 31.8 all_gather.108
  2243.9 29.8 all-gather.39.cloned.1.call-done
  2282.3 11.6 fusion.64
  2309.8 41.2 scatter_fusion.1
  2354.2 13.6 fusion.67
  2383.7 41.2 scatter_fusion
  2476.6 11.1 fusion.1
  2494.8 17.7 convolution_multiply_fusion
  2556.5 11.5 convolution_bitcast_fusion.1
  2569.2 12.3 convolution_bitcast_fusion
  2582.5 33.9 fusion.131
  2644.2 16.6 broadcast_in_dim.210
  2698.3 44.9 all-reduce.21
  2749.6 60.9 %reduce-scatter.14.cloned.1.call-done = f32[144,48]{0,1:T(8,128)} async-done(((f32[144,1536]{0,1:T(8,128)}), f32[144,48]{0,1:T(8,128)}) %reduce-scatter.14.cloned.1.call-update) | async-done | bytes 27664 | tf_op jit(solution)/shard_map/reduce_scatter | solution.py:603
  2810.5 140.9 %reduce-scatter.24.cloned.1.call-done = f32[48,1536]{1,0:T(8,128)} async-done(((f32[1536,1536]{1,0:T(8,128)}), f32[48,1536]{1,0:T(8,128)}) %reduce-scatter.24.cloned.1.call-update) | async-done | bytes 294928 | tf_op jit(solution)/shard_map/reduce_scatter | solution.py:615
  2951.5 142.0 %reduce-scatter.20.cloned.1.call-done = f32[48,1536]{1,0:T(8,128)} async-done(((f32[1536,1536]{1,0:T(8,128)}), f32[48,1536]{1,0:T(8,128)}) %reduce-scatter.20.cloned.1.call-update) | async-done | bytes 294928 | tf_op jit(solution)/shard_map/reduce_scatter | solution.py:612
  3093.4 251.3 %reduce-scatter.26.cloned.1.call-done = f32[48,4096]{1,0:T(8,128)} async-done(((f32[1536,4096]{1,0:T(8,128)}), f32[48,4096]{1,0:T(8,128)}) %reduce-scatter.26.cloned.1.call-update) | async-done | bytes 786448 | tf_op jit(solution)/shard_map/reduce_scatter | solution.py:617
  3344.7 253.2 %reduce-scatter.28.cloned.1.call-done = f32[48,4096]{1,0:T(8,128)} async-done(((f32[1536,4096]{1,0:T(8,128)}), f32[48,4096]{1,0:T(8,128)}) %reduce-scatter.28.cloned.1.call-update) | async-done | bytes 786448 | tf_op jit(solution)/shard_map/reduce_scatter | solution.py:618
  3597.9 251.9 %reduce-scatter.30.cloned.1.call-done = f32[128,1536]{1,0:T(8,128)} async-done(((f32[4096,1536]{1,0:T(8,128)}), f32[128,1536]{1,0:T(8,128)}) %reduce-scatter.30.cloned.1.call-update) | async-done | bytes 786448 | tf_op jit(solution)/shard_map/reduce_scatter | solution.py:619
  3849.8 271.7 %reduce-scatter.18.cloned.1.call-done = f32[48,4608]{1,0:T(8,128)} async-done(((f32[1536,4608]{1,0:T(8,128)}), f32[48,4608]{1,0:T(8,128)}) %reduce-scatter.18.cloned.1.call-update) | async-done | bytes 884752 | tf_op jit(solution)/shard_map/reduce_scatter | solution.py:609
  4121.5 356.7 %reduce-scatter.16.cloned.1.call-done = f32[48,6144]{1,0:T(8,128)} async-done(((f32[1536,6144]{1,0:T(8,128)}), f32[48,6144]{1,0:T(8,128)}) %reduce-scatter.16.cloned.1.call-update) | async-done | bytes 1179664 | tf_op jit(solution)/shard_map/reduce_scatter | solution.py:606
  4478.2 437.7 %reduce-scatter.22.cloned.1.call-done = f32[128,3072]{1,0:T(8,128)} async-done(((f32[4096,3072]{1,0:T(8,128)}), f32[128,3072]{1,0:T(8,128)}) %reduce-scatter.22.cloned.1.call-update) | async-done | bytes 1572880 | tf_op jit(solution)/shard_map/reduce_scatter | solution.py:613
  (665 shorter events, 589.6 us)
Async XLA Ops:
  7.2 1368.1 %copy-start = (bf16[256,4096]{1,0:T(8,128)(2,1)S(1)}, bf16[256,4096]{1,0:T(8,128)(2,1)}, u32[]{:S(2)}) copy-start(bf16[256,4096]{1,0:T(8,128)(2,1)} %param.34) | copy-start | bytes 6291460
  7.4 381.1 %all-gather.17.cloned.1.call-start = ((), (), s32[]{:S(2)}) async-start(), calls=%async_computation.21 | async-start | bytes 21233664 | tf_op jit(solution)/shard_map/all_gather | solution.py:171
  8.1 578.4 %all-gather.19.cloned.1.call-start = ((), (), s32[]{:S(2)}) async-start(), calls=%async_computation.22 | async-start | bytes 15925248 | tf_op jit(solution)/shard_map/all_gather | solution.py:174
  8.8 712.3 %all-gather.27.cloned.1.call-start = ((), (), s32[]{:S(2)}) async-start(), calls=%async_computation.26 | async-start | bytes 5308416 | tf_op jit(solution)/shard_map/all_gather | solution.py:177
  9.6 785.1 %all-gather.23.cloned.1.call-start = ((), (), s32[]{:S(2)}) async-start(), calls=%async_computation.24 | async-start | bytes 9437184 | tf_op jit(solution)/shard_map/all_gather | solution.py:294
  9.7 194.0 %collective-permute-start.1 = (bf16[1,8,32]{2,1,0:T(8,128)(2,1)S(1)}, bf16[1,8,32]{2,1,0:T(8,128)(2,1)S(1)}, u32[]{:S(2)}, u32[]{:S(2)}) collective-permute-start(bf16[1,8,32]{2,1,0:T(8,128)(2,1)S(1)} %get-tuple-element.129), channel_id=1, source_target_pairs={{8,0},{16,8},{24,16},{9,1},{17,9},{25,17},{10,2},{18,10},{26,18},{... | collective-permute-start | bytes 1544 | tf_op jit(solution)/shard_map/ppermute | solution.py:33
  11.0 192.7 %collective-permute-start = (bf16[1,8,32]{2,1,0:T(8,128)(2,1)S(1)}, bf16[1,8,32]{2,1,0:T(8,128)(2,1)S(1)}, u32[]{:S(2)}, u32[]{:S(2)}) collective-permute-start(bf16[1,8,32]{2,1,0:T(8,128)(2,1)S(1)} %get-tuple-element.128), channel_id=1, source_target_pairs={{0,8},{8,16},{16,24},{1,9},{9,17},{17,25},{2,10},{10,18},{18,26},{... | collective-permute-start | bytes 1544 | tf_op jit(solution)/shard_map/ppermute | solution.py:31
  203.8 11.7 collective-permute-start.3
  205.1 10.4 collective-permute-start.2
  401.3 319.8 %copy-start.12 = (bf16[16,8,1536]{2,1,0:T(8,128)(2,1)}, bf16[16,8,1536]{2,1,0:T(8,128)(2,1)S(1)}, u32[]{:S(2)}) copy-start(bf16[16,8,1536]{2,1,0:T(8,128)(2,1)S(1)} %multiply_convert_fusion.12) | copy-start | bytes 1179652
  632.4 10.9 all-to-all-start.1
  635.9 259.4 %all-gather.21.cloned.1.call-start = ((), (), s32[]{:S(2)}) async-start(), calls=%async_computation.23 | async-start | bytes 7077888 | tf_op jit(solution)/shard_map/all_gather | solution.py:293
  660.2 715.1 %all-gather.25.cloned.1.call-start = ((), (), s32[]{:S(2)}) async-start(), calls=%async_computation.25 | async-start | bytes 28311552 | tf_op jit(solution)/shard_map/all_gather | solution.py:178
  660.8 893.2 %all-gather.35.cloned.1.call-start = ((), (), s32[]{:S(2)}) async-start(), calls=%async_computation.30 | async-start | bytes 14155776 | tf_op jit(solution)/shard_map/all_gather | solution.py:184
  661.5 972.7 %all-gather.29.cloned.1.call-start = ((), (), s32[]{:S(2)}) async-start(), calls=%async_computation.27 | async-start | bytes 5308416 | tf_op jit(solution)/shard_map/all_gather | solution.py:180
  662.3 1148.7 %all-gather.33.cloned.1.call-start = ((), (), s32[]{:S(2)}) async-start(), calls=%async_computation.29 | async-start | bytes 14155776 | tf_op jit(solution)/shard_map/all_gather | solution.py:183
  663.0 1324.7 %all-gather.31.cloned.1.call-start = ((), (), s32[]{:S(2)}) async-start(), calls=%async_computation.28 | async-start | bytes 14155776 | tf_op jit(solution)/shard_map/all_gather | solution.py:182
  717.6 16.2 all-to-all-start
  733.8 31.3 all-to-all-start.3
  773.5 604.7 %copy-start.59 = (bf16[512,6,64]{0,2,1:T(8,128)(2,1)}, bf16[512,6,64]{0,2,1:T(8,128)(2,1)S(1)}, u32[]{:S(2)}) copy-start(bf16[512,6,64]{0,2,1:T(8,128)(2,1)S(1)} %copy.563) | copy-start | bytes 1179652
  1393.0 173.2 %all-to-all-start.4 = ((bf16[64,8,384]{2,1,0:T(8,128)(2,1)}), bf16[64,8,384]{2,1,0:T(8,128)(2,1)S(1)}, u32[]{:S(2)}, u32[]{:S(2)}) async-start(bf16[64,8,384]{2,1,0:T(8,128)(2,1)} %add_convert_fusion.6), calls=%async_computation.4 | async-start | bytes 786432 | tf_op jit(solution)/shard_map/all_to_all | solution.py:354
  1396.4 692.4 %all-gather.37.cloned.1.call-start = ((), (), s32[]{:S(2)}) async-start(), calls=%async_computation.31 | async-start | bytes 7077888 | tf_op jit(solution)/shard_map/all_gather | solution.py:494
  1639.4 348.3 %copy-start.63 = (bf16[16,8,1536]{2,1,0:T(8,128)(2,1)}, bf16[16,8,1536]{2,1,0:T(8,128)(2,1)S(1)}, u32[]{:S(2)}) copy-start(bf16[16,8,1536]{2,1,0:T(8,128)(2,1)S(1)} %multiply_convert_fusion.11) | copy-start | bytes 1179652
  2039.4 101.3 %all-to-all-start.5 = ((bf16[4,2,24576]{2,1,0:T(2,128)(2,1)}), bf16[4,2,24576]{2,1,0:T(2,128)(2,1)S(1)}, u32[]{:S(2)}, u32[]{:S(2)}) async-start(bf16[4,2,24576]{2,1,0:T(2,128)(2,1)} %reshape.627), calls=%async_computation.5 | async-start | bytes 786432 | tf_op jit(solution)/shard_map/all_to_all | solution.py:428
  2042.9 230.7 %all-gather.39.cloned.1.call-start = ((), (), s32[]{:S(2)}) async-start(), calls=%async_computation.32 | async-start | bytes 9437184 | tf_op jit(solution)/shard_map/all_gather | solution.py:495
  2232.5 207.5 %all-to-all-start.9 = ((bf16[64,8,384]{2,1,0:T(8,128)(2,1)}), bf16[64,8,384]{2,1,0:T(8,128)(2,1)}, u32[]{:S(2)}, u32[]{:S(2)}) async-start(bf16[64,8,384]{2,1,0:T(8,128)(2,1)} %reshape.477), calls=%async_computation.9 | async-start | bytes 786432 | tf_op jit(solution)/shard_map/all_to_all | solution.py:554
  2440.0 14.0 all-to-all-start.8
  2454.0 10.9 all-to-all-start.7
  2464.9 10.9 all-to-all-start.6
  2468.4 279.8 %reduce-scatter.34.cloned.1.call-start = ((), (), s32[]{:S(2)}) async-start(), calls=%async_computation.43 | async-start | bytes 811008
  2513.8 235.8 %reduce-scatter.32.cloned.1.call-start = ((), (), s32[]{:S(2)}) async-start(), calls=%async_computation.42 | async-start | bytes 1622016 | tf_op jit(solution)/shard_map/reduce_scatter | solution.py:620
  2515.5 295.0 %reduce-scatter.14.cloned.1.call-start = ((), (), s32[]{:S(2)}) async-start(), calls=%async_computation.33 | async-start | bytes 1622016 | tf_op jit(solution)/shard_map/reduce_scatter | solution.py:603
  2521.1 430.4 %reduce-scatter.24.cloned.1.call-start = ((), (), s32[]{:S(2)}) async-start(), calls=%async_computation.38 | async-start | bytes 9732096 | tf_op jit(solution)/shard_map/reduce_scatter | solution.py:615
  2526.2 567.2 %reduce-scatter.20.cloned.1.call-start = ((), (), s32[]{:S(2)}) async-start(), calls=%async_computation.36 | async-start | bytes 9732096 | tf_op jit(solution)/shard_map/reduce_scatter | solution.py:612
  2532.3 812.5 %reduce-scatter.26.cloned.1.call-start = ((), (), s32[]{:S(2)}) async-start(), calls=%async_computation.39 | async-start | bytes 25952256 | tf_op jit(solution)/shard_map/reduce_scatter | solution.py:617
  2543.8 1054.1 %reduce-scatter.28.cloned.1.call-start = ((), (), s32[]{:S(2)}) async-start(), calls=%async_computation.40 | async-start | bytes 25952256 | tf_op jit(solution)/shard_map/reduce_scatter | solution.py:618
  2555.4 1294.5 %reduce-scatter.30.cloned.1.call-start = ((), (), s32[]{:S(2)}) async-start(), calls=%async_computation.41 | async-start | bytes 25952256 | tf_op jit(solution)/shard_map/reduce_scatter | solution.py:619
  2568.0 1553.5 %reduce-scatter.18.cloned.1.call-start = ((), (), s32[]{:S(2)}) async-start(), calls=%async_computation.35 | async-start | bytes 29196288 | tf_op jit(solution)/shard_map/reduce_scatter | solution.py:609
  2581.6 1896.7 %reduce-scatter.16.cloned.1.call-start = ((), (), s32[]{:S(2)}) async-start(), calls=%async_computation.34 | async-start | bytes 38928384 | tf_op jit(solution)/shard_map/reduce_scatter | solution.py:606
  2616.4 2299.5 %reduce-scatter.22.cloned.1.call-start = ((), (), s32[]{:S(2)}) async-start(), calls=%async_computation.37 | async-start | bytes 51904512 | tf_op jit(solution)/shard_map/reduce_scatter | solution.py:613
  2672.4 4.4 collective-permute-start.5
  2673.7 3.8 collective-permute-start.4
  2677.6 8.7 collective-permute-start.7
  2680.0 6.3 collective-permute-start.6
  2681.7 8.6 collective-permute-start.9
  2683.1 7.1 collective-permute-start.8
  2690.3 57.1 %collective-permute-start.11 = (bf16[18,1,144]{2,1,0:T(2,128)(2,1)S(1)}, bf16[18,1,144]{2,1,0:T(2,128)(2,1)S(1)}, u32[]{:S(2)}, u32[]{:S(2)}) collective-permute-start(bf16[18,1,144]{2,1,0:T(2,128)(2,1)S(1)} %get-tuple-element.100), channel_id=1, source_target_pairs={{0,1},{1,2},{2,3},{3,4},{4,5},{5,6},{6,7},{8,9},{9,10},{10,11},{11... | collective-permute-start | bytes 15560 | tf_op jit(solution)/shard_map/ppermute | solution.py:31
  2694.7 52.7 %collective-permute-start.10 = (bf16[18,1,144]{2,1,0:T(2,128)(2,1)S(1)}, bf16[18,1,144]{2,1,0:T(2,128)(2,1)S(1)}, u32[]{:S(2)}, u32[]{:S(2)}) collective-permute-start(bf16[18,1,144]{2,1,0:T(2,128)(2,1)S(1)} %get-tuple-element.99), channel_id=1, source_target_pairs={{1,0},{2,1},{3,2},{4,3},{5,4},{6,5},{7,6},{9,8},{10,9},{11,10},{12... | collective-permute-start | bytes 15560 | tf_op jit(solution)/shard_map/ppermute | solution.py:33
  (156 other events, 4973.0 us)
Sparse Core Ops, SparseCore 0:
  9.7 378.7 all-gather.16
  390.7 195.7 all-gather.18
  588.6 78.0 all-gather.26
  669.4 125.2 all-gather.22
  797.1 98.0 all-gather.20
  896.6 478.6 all-gather.24
  1377.5 176.3 all-gather.34
  1556.1 78.0 all-gather.28
  1636.4 174.5 all-gather.32
  1813.0 174.6 all-gather.30
  1989.8 99.0 all-gather.36
  2149.6 124.0 all-gather.38
  2513.9 93.0 reduce-scatter.33
  2612.6 96.0 reduce-scatter.31
  2714.4 96.0 reduce-scatter.13
  2816.8 134.5 reduce-scatter.23
  2958.8 134.5 reduce-scatter.19
  3100.3 244.4 reduce-scatter.25
  3352.9 244.9 reduce-scatter.27
  3604.7 245.0 reduce-scatter.29
  3858.0 263.5 reduce-scatter.17
  4129.7 348.5 reduce-scatter.15
  4485.2 430.6 reduce-scatter.21
where the time goes:
time: 4940 us; the launch traced here: 4920 us
  waiting for transfers between devices  3580 us (72%)
  local copies, waits for them, and re-layouts  440 us (9%)
  blocking collectives  336 us (7%)
  matrix products  328 us (7%)
  other arithmetic  149 us (3%)
  starting transfers between devices  71.5 us (1%)
    reduce_scatter x1, waiting for transfers between devices, on_device(): lax.psum_scatter(grad_caption, ('row', 'col'), scatter_dimension=0, tiled...  438 us
    reduce_scatter x1, waiting for transfers between devices, on_device(): lax.psum_scatter(grad_adaptive, ('row', 'col'), scatter_dimension=0, tile...  357 us
    all_gather x1, waiting for transfers between devices, on_device(): lax.all_gather(caption_weight, 'col', axis=0, tiled=True)  342 us
    reduce_scatter x1, waiting for transfers between devices, on_device(): lax.psum_scatter(grad_projection, ('row', 'col'), scatter_dimension=0, ti...  272 us
    reduce_scatter x1, waiting for transfers between devices, on_device(): lax.psum_scatter(grad_up_weight, ('row', 'col'), scatter_dimension=0, til...  253 us
    reduce_scatter x1, waiting for transfers between devices, on_device(): lax.psum_scatter(grad_down, ('row', 'col'), scatter_dimension=0, tiled=True)  252 us
    reduce_scatter x1, waiting for transfers between devices, on_device(): lax.psum_scatter(grad_gate_weight, ('row', 'col'), scatter_dimension=0, t...  251 us
    all_gather x1, waiting for transfers between devices, on_device(): lax.all_gather(projection, 'col', axis=0, tiled=True)  185 us
  transfers between devices with their start and end apart: 44, of which 25 were waited for; matrix products, arithmetic and copies ran while one was open for 17% of the time, Pallas kernels for 0%

commit v1 on v0

v1 whole, which is shorter than its diff:
```python
import functools
import math

import jax
import jax.numpy as jnp
import numpy as np
from jax import lax
from jax.experimental import pallas as pl
from jax.experimental.pallas import tpu as pltpu
from jax.sharding import Mesh, PartitionSpec as P

HD = 64
NBAND = 8
MOSTH = 8
HALO = 8
LANES = 256

EPS = 1e-06
THETA = 10000.0
NEG = -1e30
HIGH = lax.Precision.HIGHEST
OFFSETS = ((-1, -1), (-1, 0), (-1, 1), (0, -1), (0, 0), (0, 1), (1, -1), (1, 0), (1, 1))
ALL = ("row", "sub", "tp")
COL = ("sub", "tp")
f32 = jnp.float32
bf16 = jnp.bfloat16


def spread_all(value, axes):
    count = lax.axis_size(axes)
    return lax.all_to_all(
        jnp.broadcast_to(value[None], (count,) + value.shape), axes, 0, 0, tiled=True
    )


def swap(value, axes):
    return lax.all_to_all(value, axes, 0, 0, tiled=True)


def dot(left, right, left_dim, right_dim, precision=None):
    return lax.dot_general(
        left,
        right,
        (((left_dim,), (right_dim,)), ((), ())),
        precision=precision,
        preferred_element_type=f32,
    )


def shift(cells, axis, up):
    count = lax.axis_size(axis)
    pairs = [(i, i + 1) if up else (i + 1, i) for i in range(count - 1)]
    return lax.ppermute(cells, axis, pairs)


def with_halo(cells, sides, width):
    for axis, dim in sides:
        head = lax.slice_in_dim(cells, 0, width, axis=dim)
        tail = lax.slice_in_dim(cells, cells.shape[dim] - width, cells.shape[dim], axis=dim)
        cells = jnp.concatenate([shift(tail, axis, True), cells, shift(head, axis, False)], axis=dim)
    return cells


def silu_slope(values):
    sigmoid = jax.nn.sigmoid(values)
    return sigmoid * (1.0 + values * (1.0 - sigmoid))


def gather_cells(padded, row_count, col_count):
    return jnp.concatenate(
        [
            padded[1 + row_off : 1 + row_off + row_count, 1 + col_off : 1 + col_off + col_count]
            for row_off, col_off in OFFSETS
        ],
        axis=-1,
    )


def spread_cells(padded, row_count, col_count, channels):
    summed = jnp.zeros((row_count, col_count, channels), f32)
    for offset_index, (row_off, col_off) in enumerate(OFFSETS):
        summed = summed + padded[
            1 - row_off : 1 - row_off + row_count,
            1 - col_off : 1 - col_off + col_count,
            offset_index * channels : (offset_index + 1) * channels,
        ].astype(f32)
    return summed


def row_items(heights, band_ids, row_count):
    count = heights.shape[0]
    below = jnp.arange(count)[:, None] >= jnp.arange(count)[None, :]
    item_ends = jnp.sum(jnp.where(below, heights[None, :], 0), axis=1)
    row_ids = jnp.arange(row_count, dtype=jnp.int32)
    item_of_row = jnp.sum((item_ends[None, :] <= row_ids[:, None]).astype(jnp.int32), axis=1)
    picked = item_of_row[:, None] == jnp.arange(count, dtype=jnp.int32)[None, :]
    item_top = jnp.sum(jnp.where(picked, (item_ends - heights)[None, :], 0), axis=1)
    row_band = jnp.sum(jnp.where(picked, band_ids[None, :], 0), axis=1)
    band_onehot = (row_band[:, None] == jnp.arange(NBAND, dtype=jnp.int32)[None, :]).astype(f32)
    return (item_of_row, row_ids - item_top, band_onehot)


def rotate(values, tables):
    cos_rows, sin_rows, cos_cols, sin_cols = tables
    first, second, third, fourth = (values[:, i] for i in range(4))
    return jnp.stack(
        [
            first * cos_rows - second * sin_rows,
            first * sin_rows + second * cos_rows,
            third * cos_cols - fourth * sin_cols,
            third * sin_cols + fourth * cos_cols,
        ],
        axis=1,
    )


def head_norm(raw, gain, tables):
    heads, _, tokens = raw.shape
    normed = raw * lax.rsqrt(jnp.mean(raw * raw, axis=1, keepdims=True) + EPS) * gain
    return rotate(normed.reshape(heads, 4, HD // 4, tokens), tables).reshape(raw.shape)


def head_norm_back(raw, gain, tables, grad):
    heads, _, tokens = raw.shape
    cos_rows, sin_rows, cos_cols, sin_cols = tables
    turned = rotate(
        grad.reshape(heads, 4, HD // 4, tokens), (cos_rows, -sin_rows, cos_cols, -sin_cols)
    ).reshape(raw.shape)
    inverse = lax.rsqrt(jnp.mean(raw * raw, axis=1, keepdims=True) + EPS)
    unit = raw * inverse
    grad_gain = jnp.sum(turned * unit, axis=2)
    weighted = turned * gain
    grad_raw = inverse * (weighted - unit * jnp.mean(weighted * unit, axis=1, keepdims=True))
    return grad_raw, grad_gain


def tn(left, right):
    return dot(left, right, 0, 0)


def nt(left, right):
    return dot(left, right, 1, 1)


def nn(left, right):
    return dot(left, right, 1, 0)


def masked_scores(key_block, query_block, bias):
    return tn(key_block, query_block) + bias


def block_bias(items_ref, item_query, chunk, key_rows, width):
    rows = []
    for key_row in range(key_rows):
        item = items_ref[chunk * key_rows + key_row]
        rows.append(
            jnp.broadcast_to(jnp.where(item_query == item, 0.0, NEG), (width, item_query.shape[1]))
        )
    return rows[0] if len(rows) == 1 else jnp.concatenate(rows, axis=0)


def attend_kernel(
    heads,
    key_rows,
    key_width,
    items_ref,
    low_ref,
    high_ref,
    item_query_ref,
    query_ref,
    key_ref,
    value_ref,
    cross_ref,
    caption_key_ref,
    caption_value_ref,
    gate_ref,
    mixed_ref,
    self_ref,
    crossed_ref,
    stats_ref,
    total_ref,
):
    block = pl.program_id(0)
    item_query = item_query_ref[0:1, :]
    self_ref[...] = jnp.zeros_like(self_ref)
    total_ref[...] = jnp.zeros_like(total_ref)

    def chunk_step(chunk, carry):
        lanes = pl.ds(pl.multiple_of(chunk * LANES, LANES), LANES)
        bias = block_bias(items_ref, item_query, chunk, key_rows, key_width)
        for head in range(heads):
            part = slice(head * HD, (head + 1) * HD)
            scores = masked_scores(key_ref[part, lanes], query_ref[part, :], bias)
            weights = jnp.exp(scores)
            total_ref[head : head + 1, :] += jnp.sum(weights, axis=0, keepdims=True)
            self_ref[part, :] += nn(value_ref[part, lanes], weights.astype(bf16))
        return carry

    lax.fori_loop(low_ref[block], high_ref[block], chunk_step, 0)
    stats_ref[...] = jnp.zeros_like(stats_ref)
    for head in range(heads):
        part = slice(head * HD, (head + 1) * HD)
        total = total_ref[head : head + 1, :]
        attended = self_ref[part, :] / total
        self_ref[part, :] = attended
        stats_ref[head : head + 1, :] = jnp.log(total)
        scores = tn(caption_key_ref[part, :], cross_ref[part, :])
        best = jnp.max(scores, axis=0, keepdims=True)
        weights = jnp.exp(scores - best)
        total = jnp.sum(weights, axis=0, keepdims=True)
        crossed = nn(caption_value_ref[part, :], (weights / total).astype(bf16))
        crossed_ref[part, :] = crossed
        stats_ref[heads + head : heads + head + 1, :] = best + jnp.log(total)
        mixed_ref[part, :] = (attended + gate_ref[part, 0:1] * crossed).astype(bf16)


def cross_back_kernel(
    heads,
    cross_ref,
    caption_key_ref,
    caption_value_ref,
    gate_ref,
    grad_ref,
    crossed_ref,
    stats_ref,
    grad_cross_ref,
    grad_key_ref,
    grad_value_ref,
    grad_gate_ref,
):
    @pl.when(pl.program_id(0) == 0)
    def _():
        grad_key_ref[...] = jnp.zeros_like(grad_key_ref)
        grad_value_ref[...] = jnp.zeros_like(grad_value_ref)
        grad_gate_ref[...] = jnp.zeros_like(grad_gate_ref)

    for head in range(heads):
        part = slice(head * HD, (head + 1) * HD)
        gate = gate_ref[part, 0:1]
        grad_wide = grad_ref[part, :].astype(f32)
        grad_crossed = (gate * grad_wide).astype(bf16)
        grad_gate_ref[part, 0:1] += jnp.sum(
            grad_wide * crossed_ref[part, :], axis=1, keepdims=True
        ) * (1.0 - gate * gate)
        scores = tn(caption_key_ref[part, :], cross_ref[part, :])
        weights = jnp.exp(scores - stats_ref[heads + head : heads + head + 1, :])
        grad_weights = tn(caption_value_ref[part, :], grad_crossed)
        delta = jnp.sum(weights * grad_weights, axis=0, keepdims=True)
        grad_scores = (weights * (grad_weights - delta)).astype(bf16)
        grad_cross_ref[part, :] = (
            nn(caption_key_ref[part, :], grad_scores) * (1.0 / math.sqrt(HD))
        ).astype(bf16)
        grad_key_ref[part, :] += nt(cross_ref[part, :], grad_scores)
        grad_value_ref[part, :] += nt(grad_crossed, weights.astype(bf16))


def attend_back_kernel(
    heads,
    key_rows,
    key_width,
    items_ref,
    low_ref,
    high_ref,
    item_query_ref,
    query_ref,
    key_ref,
    value_ref,
    grad_ref,
    self_ref,
    stats_ref,
    grad_query_ref,
    grad_key_ref,
    grad_value_ref,
    delta_ref,
):
    block = pl.program_id(0)

    @pl.when(block == 0)
    def _():
        grad_key_ref[...] = jnp.zeros_like(grad_key_ref)
        grad_value_ref[...] = jnp.zeros_like(grad_value_ref)

    item_query = item_query_ref[0:1, :]
    grad_query_ref[...] = jnp.zeros_like(grad_query_ref)
    for head in range(heads):
        part = slice(head * HD, (head + 1) * HD)
        delta_ref[head : head + 1, :] = jnp.sum(
            grad_ref[part, :].astype(f32) * self_ref[part, :], axis=0, keepdims=True
        )

    def chunk_step(chunk, carry):
        lanes = pl.ds(pl.multiple_of(chunk * LANES, LANES), LANES)
        bias = block_bias(items_ref, item_query, chunk, key_rows, key_width)
        for head in range(heads):
            part = slice(head * HD, (head + 1) * HD)
            key_block = key_ref[part, lanes]
            query_block = query_ref[part, :]
            grad_block = grad_ref[part, :]
            scores = masked_scores(key_block, query_block, bias)
            weights = jnp.exp(scores - stats_ref[head : head + 1, :])
            grad_weights = tn(value_ref[part, lanes], grad_block)
            grad_scores = (weights * (grad_weights - delta_ref[head : head + 1, :])).astype(bf16)
            grad_query_ref[part, :] += nn(key_block, grad_scores)
            grad_key_ref[part, lanes] += nt(query_block, grad_scores)
            grad_value_ref[part, lanes] += nt(grad_block, weights.astype(bf16))
        return carry

    lax.fori_loop(low_ref[block], high_ref[block], chunk_step, 0)


def on_device(
    latents,
    captions,
    item_heights,
    item_bands,
    embedding,
    embed_bias,
    band_table,
    adaptive,
    adaptive_bias,
    attention_gain,
    projection,
    query_gain,
    key_gain,
    cross_query,
    caption_weight,
    cross_gate,
    output_weight,
    feedforward_gain,
    gate_weight,
    up_weight,
    down_weight,
    unpatch_weight,
    cotangent,
):
    rows_n, sub_n, tp_n = (lax.axis_size(a) for a in ALL)
    col_n = sub_n * tp_n
    all_n = rows_n * col_n
    row = lax.axis_index("row")
    sub = lax.axis_index("sub")
    tp = lax.axis_index("tp")
    tile_rows, tile_cols, channels = latents.shape
    grid_rows = tile_rows * rows_n
    grid_cols = tile_cols * col_n
    span = tile_cols * tp_n
    tokens = tile_rows * span
    own = tile_rows * tile_cols
    width = embed_bias.shape[0]
    model = width * col_n
    head_width = model // tp_n
    heads = head_width // HD
    owned = model // all_n
    quarter = width // rows_n
    ff = gate_weight.shape[1]
    ff_part = ff // col_n
    ff_mine = ff // tp_n
    text = captions.shape[0]
    patch = 9 * channels

    grid = spread_all(jnp.concatenate([latents, cotangent], axis=-1), ALL)
    grid = (
        grid.reshape(rows_n, col_n, tile_rows, tile_cols, 2 * channels)
        .transpose(0, 2, 1, 3, 4)
        .reshape(grid_rows, grid_cols, 2 * channels)
    )
    grid = jnp.pad(grid, ((1, 1), (1, 1), (0, 0)))
    bordered = lax.dynamic_slice(
        grid,
        (row * tile_rows, sub * span, 0),
        (tile_rows + 2, span + 2, 2 * channels),
    )
    packed = jnp.concatenate(
        [
            embedding,
            unpatch_weight.T,
            embed_bias[None],
            attention_gain[None],
            feedforward_gain[None],
            band_table,
            adaptive_bias.reshape(-1, width),
        ],
        axis=0,
    )
    packed = spread_all(packed, COL)
    parts = packed.shape[1]
    bias_all = packed[:, 2 * patch + 3 + NBAND :].reshape(-1).astype(f32)
    packed = packed.transpose(1, 0, 2).reshape(parts, model)
    full_embedding = packed[0:patch]
    full_unpatch = packed[patch : 2 * patch]
    full_bias, attn_gain, ff_gain = (packed[2 * patch + i].astype(f32) for i in range(3))
    full_band = packed[2 * patch + 3 : 2 * patch + 3 + NBAND].astype(f32)

    mod_width = adaptive.shape[1] // rows_n
    mod_part = jnp.dot(
        jax.nn.silu(band_table.astype(f32)),
        lax.dynamic_slice_in_dim(adaptive, row * mod_width, mod_width, 1).astype(f32),
        precision=HIGH,
    )
    mod_part = jnp.sum(spread_all(mod_part, COL), axis=0)
    modulations = (
        spread_all(mod_part, "row").transpose(1, 0, 2).reshape(NBAND, adaptive.shape[1]) + bias_all
    )
    item_of_row, row_place, band_onehot = row_items(item_heights, item_bands, grid_rows)
    tile_onehot = lax.dynamic_slice_in_dim(band_onehot, row * tile_rows, tile_rows, 0)
    tile_modulation = jnp.dot(tile_onehot, modulations, precision=HIGH)[:, None, :]
    first_scale, first_gate, second_scale, second_gate = (
        tile_modulation[..., i * model : (i + 1) * model] for i in range(4)
    )

    def fetch(weight):
        piece = lax.dynamic_slice_in_dim(weight, row * quarter, quarter, 0).transpose(1, 0, 2)
        piece = jnp.broadcast_to(piece[None], (sub_n,) + piece.shape).reshape(
            col_n, quarter, weight.shape[2]
        )
        piece = swap(piece, COL)
        whole = lax.all_gather(piece, "row", axis=0, tiled=False)
        return whole.transpose(1, 0, 2, 3).reshape(model, weight.shape[2])

    weight_qkvc = fetch(
        jnp.concatenate(
            [
                projection.reshape(width, 3, tp_n, head_width),
                cross_query.reshape(width, 1, tp_n, head_width),
            ],
            axis=1,
        )
        .transpose(0, 2, 1, 3)
        .reshape(width, tp_n, 4 * head_width)
    )

    text_part = text // rows_n
    cap_part = jnp.dot(
        lax.dynamic_slice(
            captions,
            (row * text_part, (sub * tp_n + tp) * caption_weight.shape[0]),
            (text_part, caption_weight.shape[0]),
        ),
        caption_weight,
        preferred_element_type=f32,
    ).astype(bf16)
    cap_part = cap_part.reshape(text_part, 2, tp_n, head_width).transpose(2, 0, 1, 3)
    cap_part = jnp.broadcast_to(cap_part[None], (sub_n,) + cap_part.shape).reshape(
        col_n, text_part, 2 * head_width
    )
    cap_part = jnp.sum(swap(cap_part, COL).astype(f32), axis=0).astype(bf16)
    caption_heads = spread_all(cap_part, "row").reshape(text, 2 * head_width).T
    caption_keys = caption_heads[:head_width]
    caption_values = caption_heads[head_width:]

    neighbours = gather_cells(bordered[..., 0:channels], tile_rows, span)
    patch_grads = gather_cells(bordered[..., channels : 2 * channels], tile_rows, span)
    embedded = (
        jnp.dot(neighbours, full_embedding, preferred_element_type=f32) + full_bias
    )
    inverse_one = lax.rsqrt(jnp.mean(embedded * embedded, axis=-1, keepdims=True) + EPS)
    normed = (embedded * inverse_one * (attn_gain * (1.0 + first_scale))).astype(bf16)
    normed = normed.reshape(tokens, model)
    raw = dot(weight_qkvc, normed, 0, 1).astype(bf16)
    raw_query = raw[0:head_width].reshape(heads, HD, tokens)
    raw_key = raw[head_width : 2 * head_width].reshape(heads, HD, tokens)
    values = raw[2 * head_width : 3 * head_width]
    score_scale = 1.0 / math.sqrt(HD)
    raw_cross = raw[3 * head_width :] * jnp.asarray(score_scale, bf16)

    frequency = THETA ** (-jnp.arange(HD // 4, dtype=f32) / (HD // 4))
    tile_place = lax.dynamic_slice_in_dim(row_place, row * tile_rows, tile_rows, 0)
    row_angles = frequency[:, None] * tile_place.astype(f32)[None, :]
    col_angles = frequency[:, None] * (sub * span + jnp.arange(span)).astype(f32)[None, :]

    def on_rows(table):
        return jnp.repeat(table, span, axis=1)

    def on_cols(table):
        return jnp.tile(table, (1, tile_rows))

    tables = (
        on_rows(jnp.cos(row_angles)),
        on_rows(jnp.sin(row_angles)),
        on_cols(jnp.cos(col_angles)),
        on_cols(jnp.sin(col_angles)),
    )
    gain_query = _mine(query_gain, tp, sub_n).astype(f32).reshape(heads, HD, 1)
    gain_key = _mine(key_gain, tp, sub_n).astype(f32).reshape(heads, HD, 1)
    gate_cross = jnp.tanh(_mine(cross_gate, tp, sub_n).astype(f32))
    query_wide = raw_query.astype(f32)
    key_wide = raw_key.astype(f32)
    queries = head_norm(query_wide, gain_query, tables).astype(bf16) * jnp.asarray(
        score_scale, bf16
    )
    queries = queries.reshape(head_width, tokens)
    keys = head_norm(key_wide, gain_key, tables).astype(bf16).reshape(head_width, tokens)

    both = jnp.concatenate([keys, values], axis=0)
    if sub_n > 1:
        both = (
            lax.all_gather(both, "sub", axis=0)
            .reshape(sub_n, 2 * head_width, tile_rows, span)
            .transpose(1, 2, 0, 3)
            .reshape(2 * head_width, tile_rows * grid_cols)
        )
    edge = HALO * grid_cols
    both = jnp.concatenate(
        [
            shift(both[:, both.shape[1] - edge :], "row", True),
            both,
            shift(both[:, :edge], "row", False),
        ],
        axis=1,
    )
    keys_near, values_near = both[:head_width], both[head_width:]

    near_rows = tile_rows + 2 * HALO
    key_rows = max(1, LANES // grid_cols)
    key_width = LANES // key_rows
    block_rows = LANES // span
    blocks = tile_rows // block_rows
    items_padded = jnp.concatenate(
        [
            jnp.full((HALO,), -1, jnp.int32),
            item_of_row.astype(jnp.int32),
            jnp.full((HALO,), item_heights.shape[0] + 1, jnp.int32),
        ]
    )
    items_near = lax.dynamic_slice_in_dim(items_padded, row * tile_rows, near_rows, 0)
    item_query = jnp.repeat(items_near[HALO : HALO + tile_rows], span)[None, :]
    chunk_items = jnp.repeat(items_near, grid_cols // (key_width)).reshape(-1, key_rows)
    query_items = items_near[HALO : HALO + tile_rows].reshape(blocks, block_rows)
    before = chunk_items[None, :, -1] < query_items[:, None, 0]
    after = chunk_items[None, :, 0] <= query_items[:, None, -1]
    low = jnp.sum(before.astype(jnp.int32), axis=1)
    high = jnp.sum(after.astype(jnp.int32), axis=1)
    chunk_items = chunk_items.reshape(-1)
    near = near_rows * grid_cols

    def by_block(count):
        return pl.BlockSpec((count, LANES), lambda i, *_: (0, i))

    def whole(*shape):
        return pl.BlockSpec(shape, lambda i, *_: (0, 0))

    vmem = pltpu.CompilerParams(vmem_limit_bytes=48 * 2**20)
    gate_column = gate_cross[:, None]
    mixed, self_out, crossed, stats = pl.pallas_call(
        functools.partial(attend_kernel, heads, key_rows, key_width),
        grid_spec=pltpu.PrefetchScalarGridSpec(
            num_scalar_prefetch=3,
            grid=(blocks,),
            in_specs=[
                by_block(1),
                by_block(head_width),
                whole(head_width, near),
                whole(head_width, near),
                by_block(head_width),
                whole(head_width, text),
                whole(head_width, text),
                whole(head_width, 1),
            ],
            out_specs=[by_block(head_width), by_block(head_width), by_block(head_width), by_block(8)],
            scratch_shapes=[pltpu.VMEM((8, LANES), f32)],
        ),
        out_shape=[
            jax.ShapeDtypeStruct((head_width, tokens), bf16),
            jax.ShapeDtypeStruct((head_width, tokens), f32),
            jax.ShapeDtypeStruct((head_width, tokens), f32),
            jax.ShapeDtypeStruct((8, tokens), f32),
        ],
        compiler_params=vmem,
        name="attend",
    )(
        chunk_items,
        low,
        high,
        item_query,
        queries,
        keys_near,
        values_near,
        raw_cross,
        caption_keys,
        caption_values,
        gate_column,
    )

    full_output = lax.all_gather(output_weight, COL, axis=0, tiled=True)
    mixed_all = lax.all_gather(mixed, "tp", axis=0, tiled=True)
    branch = dot(mixed_all, full_output, 0, 0).reshape(tile_rows, span, model)
    tanh_one = jnp.tanh(first_gate)
    residual = embedded + tanh_one * branch
    inverse_two = lax.rsqrt(jnp.mean(residual * residual, axis=-1, keepdims=True) + EPS)
    inner = (residual * inverse_two * (ff_gain * (1.0 + second_scale))).astype(bf16)
    inner = inner.reshape(tokens, model)

    def ff_slices(weight):
        return weight.reshape(width, sub_n, tp_n, ff_part).transpose(0, 2, 1, 3)

    weight_gu = fetch(
        jnp.stack([ff_slices(gate_weight), ff_slices(up_weight)], axis=2).reshape(
            width, tp_n, 2 * ff_mine
        )
    )
    down_mine = down_weight
    if sub_n > 1:
        down_mine = lax.all_gather(down_weight, "sub", axis=0, tiled=True)
    gate_up = dot(inner, weight_gu, 1, 0)
    gate = gate_up[:, :ff_mine]
    upward = gate_up[:, ff_mine:]
    sigmoid = jax.nn.sigmoid(gate)
    hidden = (gate * sigmoid * upward).astype(bf16)

    def to_tiles(partial):
        count = partial.shape[-1]
        return (
            partial.astype(bf16)
            .reshape(tile_rows, tp_n, tile_cols, count)
            .transpose(1, 0, 2, 3)
            .reshape(tokens, count)
        )

    def scatter(partial):
        return lax.psum_scatter(to_tiles(partial), "tp", scatter_dimension=0, tiled=True).astype(f32)

    def own_tile(values):
        return lax.dynamic_slice_in_dim(
            values.reshape(tile_rows, span, -1), tp * tile_cols, tile_cols, 1
        )

    tanh_two = jnp.tanh(second_gate)
    grad_result = jnp.dot(patch_grads, full_unpatch, preferred_element_type=f32)
    grad_feed = (tanh_two * grad_result).astype(bf16).reshape(tokens, model)
    grad_hidden = dot(grad_feed, down_mine, 1, 1)
    grad_gate = (
        grad_hidden * upward * (sigmoid * (1.0 + gate * (1.0 - sigmoid)))
    ).astype(bf16)
    grad_upward = (grad_hidden * (gate * sigmoid)).astype(bf16)
    grad_gu = jnp.concatenate([grad_gate, grad_upward], axis=1)
    grad_inner = scatter(dot(grad_gu, weight_gu, 1, 1))
    feed = scatter(dot(hidden, down_mine, 1, 0))

    own_residual = own_tile(residual)
    own_embedded = own_tile(embedded)
    own_branch = own_tile(branch)
    own_patch_grads = own_tile(patch_grads)
    tile3 = (tile_rows, tile_cols, model)
    grad_inner = grad_inner.reshape(tile3)
    feed = feed.reshape(tile3)
    own_grad_result = jnp.dot(own_patch_grads, full_unpatch, preferred_element_type=f32)
    own_inverse = lax.rsqrt(jnp.mean(own_residual * own_residual, axis=-1, keepdims=True) + EPS)
    unit_two = own_residual * own_inverse
    grad_unit = grad_inner * (ff_gain * (1.0 + second_scale))
    grad_residual = own_grad_result + own_inverse * (
        grad_unit - unit_two * jnp.mean(grad_unit * unit_two, axis=-1, keepdims=True)
    )
    grad_inner_unit = grad_inner * unit_two
    grad_branch = (tanh_one * grad_residual).astype(bf16)
    grad_mixed_own = dot(grad_branch.reshape(own, model), full_output, 1, 1).astype(bf16)
    grad_mixed = swap(
        grad_mixed_own.reshape(own, tp_n, head_width).transpose(1, 0, 2), "tp"
    )
    grad_mixed = (
        grad_mixed.reshape(tp_n, tile_rows, tile_cols, head_width)
        .transpose(1, 0, 2, 3)
        .reshape(tokens, head_width)
        .T
    )

    result_low = (own_residual + tanh_two * feed).astype(bf16)
    patches = dot(result_low.reshape(own, model), full_unpatch, 1, 1).astype(bf16)
    patches = patches.reshape(tile_rows, tile_cols, patch)
    patch_border = with_halo(patches, (("row", 0), (COL, 1)), 1)
    prediction = spread_cells(patch_border, tile_rows, tile_cols, channels).astype(bf16)
    grad_unpatch = dot(result_low.reshape(own, model), own_patch_grads.reshape(own, patch), 0, 0)

    rows_second_scale = jnp.sum(grad_inner_unit * ff_gain, axis=1)
    grad_ff_gain = jnp.sum(grad_inner_unit * (1.0 + second_scale), axis=(0, 1))
    rows_second_gate = jnp.sum(
        own_grad_result * feed * (1.0 - tanh_two * tanh_two), axis=1
    )
    rows_first_gate = jnp.sum(
        grad_residual * own_branch * (1.0 - tanh_one * tanh_one), axis=1
    )

    mixed_own = (
        lax.dynamic_slice_in_dim(
            mixed_all.reshape(model, tile_rows, span), tp * tile_cols, tile_cols, 2
        )
        .reshape(model, own)
        .T
    )
    mixed_rows = swap(
        mixed_own.reshape(own, rows_n, model // rows_n).transpose(1, 0, 2), "row"
    ).reshape(rows_n * own, model // rows_n)
    branch_rows = lax.all_gather(grad_branch.reshape(own, model), "row", axis=0, tiled=True)
    grad_output = lax.psum_scatter(
        dot(mixed_rows, branch_rows, 0, 0).astype(bf16), COL, scatter_dimension=0, tiled=True
    ).astype(f32)

    grad_cross, grad_cap_keys, grad_cap_values, grad_gate_part = pl.pallas_call(
        functools.partial(cross_back_kernel, heads),
        grid=(blocks,),
        in_specs=[
            by_block(head_width),
            whole(head_width, text),
            whole(head_width, text),
            whole(head_width, 1),
            by_block(head_width),
            by_block(head_width),
            by_block(8),
        ],
        out_specs=[
            by_block(head_width),
            whole(head_width, text),
            whole(head_width, text),
            whole(head_width, 128),
        ],
        out_shape=[
            jax.ShapeDtypeStruct((head_width, tokens), bf16),
            jax.ShapeDtypeStruct((head_width, text), f32),
            jax.ShapeDtypeStruct((head_width, text), f32),
            jax.ShapeDtypeStruct((head_width, 128), f32),
        ],
        compiler_params=vmem,
        name="cross_back",
    )(raw_cross, caption_keys, caption_values, gate_column, grad_mixed, crossed, stats)

    grad_queries, grad_keys, grad_values = pl.pallas_call(
        functools.partial(attend_back_kernel, heads, key_rows, key_width),
        grid_spec=pltpu.PrefetchScalarGridSpec(
            num_scalar_prefetch=3,
            grid=(blocks,),
            in_specs=[
                by_block(1),
                by_block(head_width),
                whole(head_width, near),
                whole(head_width, near),
                by_block(head_width),
                by_block(head_width),
                by_block(8),
            ],
            out_specs=[by_block(head_width), whole(head_width, near), whole(head_width, near)],
            scratch_shapes=[pltpu.VMEM((8, LANES), f32)],
        ),
        out_shape=[
            jax.ShapeDtypeStruct((head_width, tokens), f32),
            jax.ShapeDtypeStruct((head_width, near), f32),
            jax.ShapeDtypeStruct((head_width, near), f32),
        ],
        compiler_params=vmem,
        name="attend_back",
    )(chunk_items, low, high, item_query, queries, keys_near, values_near, grad_mixed, self_out, stats)

    grad_cap = jnp.concatenate([grad_cap_keys, grad_cap_values], axis=0).astype(bf16)
    share = 2 * head_width // rows_n
    if sub_n > 1:
        grad_cap = lax.psum_scatter(
            grad_cap.reshape(rows_n, sub_n, share // sub_n, text).reshape(-1, text),
            ("row", "sub"),
            scatter_dimension=0,
            tiled=True,
        )
    else:
        grad_cap = jnp.sum(
            swap(grad_cap.reshape(rows_n, share, text), "row").astype(f32), axis=0
        ).astype(bf16)
    grad_cap = lax.all_gather(grad_cap, ALL, axis=0, tiled=True)
    grad_cap = (
        grad_cap.reshape(rows_n * sub_n, tp_n, share // sub_n, text)
        .transpose(1, 0, 2, 3)
        .reshape(tp_n, 2, head_width, text)
        .transpose(1, 0, 2, 3)
        .reshape(2 * model, text)
    )
    index = (row * sub_n + sub) * tp_n + tp
    cap_own = captions.shape[1] // all_n
    own_captions = lax.dynamic_slice_in_dim(captions, index * cap_own, cap_own, 1)
    grad_caption = dot(own_captions, grad_cap, 0, 1)

    grad_both = jnp.concatenate([grad_keys, grad_values], axis=0)
    upper = grad_both[:, :edge].astype(bf16)
    lower = grad_both[:, near - edge :].astype(bf16)
    middle = grad_both[:, edge : near - edge]
    from_above = shift(lower, "row", True).astype(f32)
    from_below = shift(upper, "row", False).astype(f32)
    side = middle.shape[1] - edge
    middle = (
        middle
        + jnp.pad(from_above, ((0, 0), (0, side)))
        + jnp.pad(from_below, ((0, 0), (side, 0)))
    )
    if sub_n > 1:
        middle = (
            middle.astype(bf16)
            .reshape(2 * head_width, tile_rows, sub_n, span)
            .transpose(2, 0, 1, 3)
            .reshape(sub_n, 2 * head_width, tokens)
        )
        middle = jnp.sum(swap(middle, "sub").astype(f32), axis=0)
    grad_keys = middle[:head_width].astype(bf16).astype(f32).reshape(heads, HD, tokens)
    grad_values = middle[head_width:].astype(bf16)
    grad_queries = (grad_queries * score_scale).astype(bf16).astype(f32).reshape(heads, HD, tokens)
    grad_raw_query, part_query_gain = head_norm_back(query_wide, gain_query, tables, grad_queries)
    grad_raw_key, part_key_gain = head_norm_back(key_wide, gain_key, tables, grad_keys)
    grad_raw = jnp.concatenate(
        [
            grad_raw_query.astype(bf16).reshape(head_width, tokens),
            grad_raw_key.astype(bf16).reshape(head_width, tokens),
            grad_values,
            grad_cross,
        ],
        axis=0,
    )

    grad_normed = dot(grad_raw, weight_qkvc, 0, 1).reshape(tile_rows, span, model)
    unit_one = embedded * inverse_one
    normed_unit = grad_normed * unit_one
    grad_unit_one = grad_normed * (attn_gain * (1.0 + first_scale))
    part_embedded = inverse_one * (
        grad_unit_one - unit_one * jnp.mean(grad_unit_one * unit_one, axis=-1, keepdims=True)
    )
    part_attn_gain = jnp.sum(normed_unit * (1.0 + first_scale), axis=(0, 1))
    rows_first_scale = jnp.sum(normed_unit * attn_gain, axis=1)
    mine = (jnp.arange(span) // tile_cols == tp)[None, :, None]
    spread_residual = jnp.where(mine, jnp.tile(grad_residual, (1, tp_n, 1)), 0.0)
    part_embedded = (part_embedded + spread_residual).astype(bf16)
    part_flat = part_embedded.reshape(tokens, model)
    grad_embedding = dot(neighbours.reshape(tokens, patch), part_flat, 0, 0)
    grad_embed_bias = jnp.sum(part_embedded.astype(f32), axis=(0, 1))
    cells = dot(part_flat, full_embedding, 1, 1).reshape(tile_rows, span, patch)
    around = spread_cells(
        jnp.pad(cells, ((2, 2), (2, 2), (0, 0))), tile_rows + 2, span + 2, channels
    )
    inside = around[:, 1 : span + 1]
    if sub_n > 1:
        from_left = shift(around[:, span + 1 :].astype(bf16), "sub", True).astype(f32)
        from_right = shift(around[:, :1].astype(bf16), "sub", False).astype(f32)
        inside = (
            inside
            + jnp.pad(from_left, ((0, 0), (0, span - 1), (0, 0)))
            + jnp.pad(from_right, ((0, 0), (span - 1, 0), (0, 0)))
        )
    inside = (
        inside.astype(bf16)
        .reshape(tile_rows + 2, tp_n, tile_cols, channels)
        .transpose(1, 0, 2, 3)
    )
    inside = jnp.sum(swap(inside, "tp").astype(f32), axis=0)
    from_above = shift(inside[tile_rows + 1 :].astype(bf16), "row", True).astype(f32)
    from_below = shift(inside[:1].astype(bf16), "row", False).astype(f32)
    latent_grad = (
        inside[1 : tile_rows + 1]
        + jnp.pad(from_above, ((0, tile_rows - 1), (0, 0), (0, 0)))
        + jnp.pad(from_below, ((tile_rows - 1, 0), (0, 0), (0, 0)))
    ).astype(bf16)

    def to_owner(partial):
        count = partial.shape[1]
        summed = lax.psum_scatter(
            partial.astype(bf16), ("row", "sub"), scatter_dimension=0, tiled=True
        )
        moved = swap(summed.reshape(tp_n, owned, count), "tp")
        return moved.transpose(1, 0, 2).astype(f32)

    grad_qkvc = to_owner(dot(normed, grad_raw, 0, 1))
    grad_qkvc = grad_qkvc.reshape(owned, tp_n, 4, head_width).transpose(0, 2, 1, 3)
    grad_projection = grad_qkvc[:, 0:3].reshape(owned, 3 * model)
    grad_cross_query = grad_qkvc[:, 3].reshape(owned, model)
    grad_gu_weight = to_owner(dot(inner, grad_gu, 0, 0))
    grad_gu_weight = grad_gu_weight.reshape(owned, tp_n, 2, sub_n, ff_part).transpose(2, 0, 3, 1, 4)
    grad_gu_weight = grad_gu_weight.reshape(2, owned, ff)
    grad_down = dot(hidden, grad_feed, 0, 0).astype(bf16)
    ff_own = ff // all_n
    grad_down = (
        grad_down.reshape(sub_n, rows_n, ff_own, model).transpose(1, 0, 2, 3).reshape(-1, model)
    )
    grad_down = lax.psum_scatter(grad_down, ("row", "sub"), scatter_dimension=0, tiled=True)
    moves = []
    for source in range(all_n):
        source_row, rest = divmod(source, col_n)
        moves.append((source, rest * rows_n + source_row))
    grad_down = lax.ppermute(grad_down, ALL, moves).astype(f32)

    def place(vector):
        return lax.dynamic_update_slice_in_dim(
            jnp.zeros((model,), f32), vector.reshape(-1), tp * head_width, 0
        )

    onehot = tile_onehot
    mod_grads = jnp.concatenate(
        [
            dot(onehot, rows, 0, 0, HIGH)
            for rows in (rows_first_scale, rows_first_gate, rows_second_scale, rows_second_gate)
        ],
        axis=0,
    )
    small = jnp.concatenate(
        [
            grad_embedding,
            grad_unpatch.T,
            mod_grads,
            grad_embed_bias[None],
            part_attn_gain[None],
            place(part_query_gain)[None],
            place(part_key_gain)[None],
            place(grad_gate_part[:, 0])[None],
            grad_ff_gain[None],
        ],
        axis=0,
    )
    count = small.shape[0]
    small = small.astype(bf16).reshape(count, all_n, owned).transpose(1, 0, 2)
    small = jnp.sum(swap(small, ALL).astype(f32), axis=0)
    grad_embedding = small[0:patch]
    grad_unpatch = small[patch : 2 * patch].T
    mods = 4 * NBAND
    vectors = small[2 * patch + mods :]
    all_mods = spread_all(small[2 * patch : 2 * patch + mods].astype(bf16), ALL).astype(f32)
    all_mods = (
        all_mods.reshape(all_n, 4, NBAND, owned).transpose(2, 1, 0, 3).reshape(NBAND, 4 * model)
    )
    own_band = lax.dynamic_slice_in_dim(full_band, index * owned, owned, 1)
    grad_adaptive = dot(jax.nn.silu(own_band), all_mods, 0, 0, HIGH)
    bias_own = 4 * owned
    grad_adaptive_bias = lax.dynamic_slice_in_dim(
        jnp.sum(all_mods, axis=0), index * bias_own, bias_own, 0
    )
    local_rows = lax.dynamic_slice_in_dim(adaptive, row * quarter, quarter, 0)
    local_band = lax.dynamic_slice_in_dim(band_table, row * quarter, quarter, 1).astype(f32)
    grad_band = dot(all_mods, local_rows.astype(f32), 1, 1, HIGH) * silu_slope(local_band)
    grad_band = lax.ppermute(grad_band, ALL, moves)

    return (
        prediction,
        latent_grad,
        grad_embedding,
        vectors[0],
        grad_band,
        grad_adaptive,
        grad_adaptive_bias,
        vectors[1],
        grad_projection,
        vectors[2],
        vectors[3],
        grad_cross_query,
        grad_caption,
        vectors[4],
        grad_output,
        vectors[5],
        grad_gu_weight[0],
        grad_gu_weight[1],
        grad_down,
        grad_unpatch,
    )


def _mine(vector, tp, sub_n):
    if sub_n == 1:
        return vector
    size = vector.shape[0] * sub_n
    whole = lax.all_gather(vector, COL, axis=0, tiled=True)
    return lax.dynamic_slice_in_dim(whole, tp * size, size, 0)


def solution(mesh):
    rows_n, col_n = mesh.shape["row"], mesh.shape["col"]

    def run(*args):
        heads = args[5].shape[0] // HD
        tp_n = math.gcd(heads, col_n)
        split = Mesh(mesh.devices.reshape(rows_n, col_n // tp_n, tp_n), ALL)
        in_specs = (
            P("row", COL, None),
            P(),
            P(),
            P(),
            P(None, COL),
            P(COL),
            P(None, COL),
            P(COL, None),
            P(COL),
            P(COL),
            P(COL, None),
            P(COL),
            P(COL),
            P(COL, None),
            P(COL, None),
            P(COL),
            P(COL, None),
            P(COL),
            P(COL, None),
            P(COL, None),
            P(COL, None),
            P(COL, None),
            P("row", COL, None),
        )
        out_specs = (
            P("row", COL, None),
            P("row", COL, None),
            P(None, ALL),
            P(ALL),
            P(None, ALL),
            P(ALL, None),
            P(ALL),
            P(ALL),
            P(ALL, None),
            P(ALL),
            P(ALL),
            P(ALL, None),
            P(ALL, None),
            P(ALL),
            P(ALL, None),
            P(ALL),
            P(ALL, None),
            P(ALL, None),
            P(ALL, None),
            P(ALL, None),
        )
        return jax.shard_map(
            on_device, mesh=split, in_specs=in_specs, out_specs=out_specs, check_vma=False
        )(*args)

    return run
```

time: 4940 us -> 863 us (0.17)
  waiting for transfers between devices: 3580 us -> 331 us
  blocking collectives: 336 us -> 46.6 us
  local copies, waits for them, and re-layouts: 440 us -> 173 us
  matrix products: 328 us -> 94.3 us
  other arithmetic: 149 us -> 55.7 us
    reduce_scatter x10 -> x6, waiting for transfers between devices: 2170 us -> 162 us  [the longest x2 128 us: scatter(): lax.psum_scatter(to_tiles(partial), 'tp', scatter_dimension=0, tiled=True)]
    all_gather x12 -> x6, waiting for transfers between devices: 1390 us -> 49.2 us  [the longest x1 49.2 us: on_device(): mixed_all = lax.all_gather(mixed, 'tp', axis=0, tiled=True)]
    dot_general x43 -> x28, matrix products: 325 us -> 92.9 us  [the longest x23 80.3 us: dot(): lax.dot_general(left, right, (((left_dim,), (right_dim,)), ((), ())), pre...]
    all_gather x6 -> x0, blocking collectives: 230 us -> none  [the longest x1 54.4 us: on_device(): lax.all_gather(adaptive_bias, 'col', axis=0, tiled=True)]
    all_to_all x9 -> x14, waiting for transfers between devices: 10.6 us -> 115 us  [the longest x6 82.5 us: spread_all(): lax.all_to_all(jnp.broadcast_to(value[None], (count,) + value.shape), axe...]
    unnamed x2 -> x0, blocking collectives: 95.2 us -> none
    reshape x24 -> x15, local copies, waits for them, and re-layouts: 122 us -> 32.2 us  [the longest x2 7.94 us: on_device(): projection.reshape(width, 3, tp_n, head_width)]
    gather x9 -> x0, local copies, waits for them, and re-layouts: 88.5 us -> none  [the longest x6 86 us: in_windows(): source[window_rows]]
  transfers between devices with their start and end apart: 44 -> 38, of which waited for: 25 -> 17; matrix products, arithmetic and copies ran while one was open for 17% -> 29% of each run, Pallas kernels for 0% -> 4%
where the time goes in v1:
time: 863 us; the launch traced here: 852 us
  waiting for transfers between devices  331 us (38%)
  local copies, waits for them, and re-layouts  173 us (20%)
  starting transfers between devices  97.2 us (11%)
  matrix products  94.3 us (11%)
  other arithmetic  55.7 us (6%)
  blocking collectives  46.6 us (5%)
  Pallas kernels  38 us (4%)
  between operations  16.9 us (2%)
    reduce_scatter x2, waiting for transfers between devices, scatter(): lax.psum_scatter(to_tiles(partial), 'tp', scatter_dimension=0, tiled=True)  128 us
    all_to_all x6, waiting for transfers between devices, spread_all(): lax.all_to_all(jnp.broadcast_to(value[None], (count,) + value.shape), axe...  82.5 us
    dot_general x23, matrix products, dot(): lax.dot_general(left, right, (((left_dim,), (right_dim,)), ((), ())), pre...  80.3 us
    all_gather x1, waiting for transfers between devices, on_device(): mixed_all = lax.all_gather(mixed, 'tp', axis=0, tiled=True)  49.2 us
    all_to_all x2, blocking collectives, swap(): return lax.all_to_all(value, axes, 0, 0, tiled=True)  46.6 us
    all_to_all x8, starting transfers between devices, swap(): return lax.all_to_all(value, axes, 0, 0, tiled=True)  43.4 us
    reduce_scatter x1, waiting for transfers between devices, on_device(): lax.psum_scatter(dot(mixed_rows, branch_rows, 0, 0).astype(bf16), COL, sc...  33.8 us
    all_to_all x8, waiting for transfers between devices, swap(): return lax.all_to_all(value, axes, 0, 0, tiled=True)  32.3 us
  transfers between devices with their start and end apart: 38, of which 17 were waited for; matrix products, arithmetic and copies ran while one was open for 29% of the time, Pallas kernels for 4%

profile of v1, /device:TPU:0, one launch (start us, length us, event | category | flops | bytes accessed | tf_op | source)
XLA Modules:
  0.0 852.0 jit_solution(16787071404097700181)
XLA Ops:
  7.3 5.0 reshape.615
  12.2 4.5 reshape.547
  20.2 4.7 maximum_bitcast_fusion
  24.9 6.4 reshape.549
  32.6 23.8 %all_to_all.80 = bf16[8,48,768]{2,1,0:T(8,128)(2,1)} all-to-all(bf16[8,48,768]{2,1,0:T(8,128)(2,1)S(1)} %copy.399), channel_id=1, replica_groups=mesh['row'=4,'col'=8] {'col'}, dimensions={0} | all-to-all | bytes 1179648 | tf_op jit(solution)/shard_map/all_to_all | solution.py:37
  56.4 8.7 %stack_transpose_reshape.8 = bf16[192,8,1,1,512]{4,2,1,0,3:T(2,128)(2,1)} reshape(bf16[192,4096]{1,0:T(8,128)(2,1)} %param.41) | data formatting | bytes 3145728 | tf_op jit(solution)/shard_map/stack;transpose;reshape | solution.py:597
  65.1 8.6 %stack_transpose_reshape.9 = bf16[192,8,1,1,512]{4,2,1,0,3:T(2,128)(2,1)} reshape(bf16[192,4096]{1,0:T(8,128)(2,1)} %param.42) | data formatting | bytes 3145728 | tf_op jit(solution)/shard_map/stack;transpose;reshape | solution.py:597
  73.7 9.7 %pad_maximum_fusion = bf16[192,8,2,1,512]{4,2,1,0,3:T(2,128)(2,1)} fusion(bf16[192,8,1,1,512]{4,2,1,0,3:T(2,128)(2,1)} %stack_transpose_reshape.9, bf16[192,8,1,1,512]{4,2,1,0,3:T(2,128)(2,1)} %stack_transpose_reshape.8), kind=kLoop, calls=%fused_computation.21 | loop fusion | flops 6291456 | bytes 6291456 | tf_op jit(solution)/shard_map/stack | solution.py:597
  83.4 6.1 reshape.556
  91.1 22.8 %all_to_all.81 = bf16[8,48,1024]{2,1,0:T(8,128)(2,1)} all-to-all(bf16[8,48,1024]{2,1,0:T(8,128)(2,1)S(1)} %copy.406), channel_id=1, replica_groups=mesh['row'=4,'col'=8] {'col'}, dimensions={0} | all-to-all | bytes 1572864 | tf_op jit(solution)/shard_map/all_to_all | solution.py:37
  125.8 6.9 all-to-all-done
  138.7 9.5 %all-to-all-done.5 = bf16[8,64,384]{2,1,0:T(8,128)(2,1)S(1)} async-done(((bf16[8,64,384]{2,1,0:T(8,128)(2,1)}), bf16[8,64,384]{2,1,0:T(8,128)(2,1)S(1)}, u32[]{:S(2)}, u32[]{:S(2)}) %all-to-all-start.5) | async-done | bytes 393248 | tf_op jit(solution)/shard_map/all_to_all | solution.py:37
  153.0 19.4 %all-to-all-done.2 = f32[8,8,1536]{2,1,0:T(8,128)S(1)} async-done(((f32[8,8,1536]{2,1,0:T(8,128)}), f32[8,8,1536]{2,1,0:T(8,128)S(1)}, u32[]{:S(2)}, u32[]{:S(2)}) %all-to-all-start.2) | async-done | bytes 393248 | tf_op jit(solution)/shard_map/all_to_all | solution.py:31
  182.9 6.0 all-to-all-start.1
  198.7 4.2 concatenate.79
  203.1 45.9 %all-to-all-done.1 = bf16[8,303,192]{1,2,0:T(8,128)(2,1)S(1)} async-done(((bf16[8,303,192]{1,2,0:T(8,128)(2,1)}), bf16[8,303,192]{1,2,0:T(8,128)(2,1)S(1)}, u32[]{:S(2)}, u32[]{:S(2)}) %all-to-all-start.1) | async-done | bytes 930848 | tf_op jit(solution)/shard_map/all_to_all | solution.py:31
  284.5 16.1 %attend.1 = (bf16[192,1024]{1,0:T(8,128)(2,1)}, f32[192,1024]{1,0:T(8,128)S(1)}, f32[192,1024]{1,0:T(8,128)S(1)}, f32[8,1024]{1,0:T(8,128)S(1)}) custom-call(s32[32]{0:T(128)S(1)} %dynamic_slice.55.items_ref, s32[4]{0:T(128)S(1)} %get-tuple-element.236.low_ref, s32[4]{0:T(128)S(1)} %get-tuple-element.235.high_ref, ...), custom_call_target="tpu_custom_call" | custom-call | tf_op jit(solution)/shard_map/attend/pallas_call | solution.py:544
  311.6 4.2 copy.407
  315.8 49.2 %all-gather.9.cloned.1.call-done = bf16[1536,1024]{1,0:T(8,128)(2,1)} async-done(((bf16[192,1024]{1,0:T(8,128)(2,1)}), bf16[1536,1024]{1,0:T(8,128)(2,1)}) %all-gather.9.cloned.1.call-update) | async-done | bytes 3145744 | tf_op jit(solution)/shard_map/all_gather | solution.py:585
  365.0 11.1 %multiply_add_fusion = (f32[16,64,1536]{2,1,0:T(8,128)S(1)}, f32[1024,1536]{1,0:T(8,128)}) fusion(f32[16,64,1536]{2,1,0:T(8,128)} %copy-done.12, f32[16,1536]{1,0:T(8,128)S(1)} %get-tuple-element.215, f32[1536]{0:T(1024)S(1)} %copy-done.69, bf16[1536,1024]{1,0:T(8,128)(2,1)} %all-gather.9.cloned.1.call-done, ...), kind=kOutput, calls=%fused_computation.10 | convolution fusion | flops 4836556800 | bytes 26843136 | tf_op jit(solution)/shard_map/dot_general | solution.py:41
  388.3 4.0 convolution_convert_fusion.2
  399.9 5.2 convolution_convert_fusion.5
  405.2 7.8 convolution_convert_fusion.1
  414.3 53.3 %reduce-scatter.9.cloned.1.call-done = bf16[128,1536]{1,0:T(8,128)(2,1)} async-done(((bf16[1024,1536]{1,0:T(8,128)(2,1)}), bf16[128,1536]{1,0:T(8,128)(2,1)}) %reduce-scatter.9.cloned.1.call-update) | async-done | bytes 393232 | tf_op jit(solution)/shard_map/reduce_scatter | solution.py:620
  470.0 74.6 %reduce-scatter.7.cloned.1.call-done = bf16[128,1536]{1,0:T(8,128)(2,1)} async-done(((bf16[1024,1536]{1,0:T(8,128)(2,1)}), bf16[128,1536]{1,0:T(8,128)(2,1)}) %reduce-scatter.7.cloned.1.call-update) | async-done | bytes 393232 | tf_op jit(solution)/shard_map/reduce_scatter | solution.py:620
  544.7 3.9 multiply_reduce_fusion.9
  549.6 4.4 convolution_convert_fusion.7
  561.7 8.3 all-to-all-done.8
  575.3 5.7 cross_back.1
  583.6 16.3 %attend_back.1 = (f32[192,1024]{1,0:T(8,128)S(1)}, f32[192,2048]{1,0:T(8,128)S(1)}, f32[192,2048]{1,0:T(8,128)}) custom-call(s32[32]{0:T(128)S(1)} %dynamic_slice.55.items_ref, s32[4]{0:T(128)S(1)} %get-tuple-element.236.low_ref, s32[4]{0:T(128)S(1)} %get-tuple-element.235.high_ref, s32[1,1024]{1,0:T(1,128)S(1)} %broadcast_in_dim_reshape.2.item_query_ref, ...), custom_call_target="tpu_custom_call" | custom-call | tf_op jit(solution)/shard_map/attend_back/pallas_call | solution.py:725
  611.0 4.0 convolution_convert_fusion.4
  616.2 4.8 copy.445
  622.8 4.5 collective-permute-start.11
  636.0 9.3 %all-to-all-start.13 = ((bf16[4,96,256]{2,1,0:T(8,128)(2,1)}), bf16[4,96,256]{2,1,0:T(8,128)(2,1)S(1)}, u32[]{:S(2)}, u32[]{:S(2)}) async-start(bf16[4,96,256]{2,1,0:T(8,128)(2,1)} %bitcast.96), calls=%async_computation.16 | async-start | bytes 393216 | tf_op jit(solution)/shard_map/all_to_all | solution.py:37
  646.4 7.6 all-to-all-done.13
  654.0 4.1 all-to-all-start.14
  664.1 9.5 %multiply_reduce_fusion = (bf16[1536]{0:T(1024)(128)(2,1)S(1)}, f32[16,1536]{1,0:T(8,128)}, f32[16,64]{1,0:T(8,128)S(1)}, f32[16,64,1536]{2,1,0:T(8,128)S(1)}) fusion(f32[16,1536]{1,0:T(8,128)S(1)} %copy-done.73, f32[16,64]{1,0:T(8,128)S(1)} %copy-done.75, f32[16,64,1536]{2,1,0:T(8,128)} %copy-done.12, f32[1536]{0:T(1024)S(1)} %copy-done.70, ...), kind=kOutput, calls=%fused_computation.4 | convolution fusion | flops 2431620608 | bytes 16833536 | tf_op jit(solution)/shard_map/dot_general | solution.py:41
  680.6 5.3 all-to-all-start.9
  692.6 5.9 all-to-all-start.15
  716.2 6.7 concatenate.102
  722.9 7.0 all-to-all-start.10
  738.7 4.5 collective-permute-start.5
  744.1 4.5 collective-permute-start.8
  758.6 6.3 all-to-all-done.10
  767.6 7.3 all-to-all-start.11
  777.7 5.4 all-to-all-done.11
  783.1 4.2 all-to-all-start.12
  798.5 33.8 %reduce-scatter.13.cloned.1.call-done = bf16[48,1536]{1,0:T(8,128)(2,1)} async-done(((bf16[384,1536]{1,0:T(8,128)(2,1)}), bf16[48,1536]{1,0:T(8,128)(2,1)}) %reduce-scatter.13.cloned.1.call-update) | async-done | bytes 147472 | tf_op jit(solution)/shard_map/reduce_scatter | solution.py:693
  (525 shorter events, 244.5 us)
Async XLA Ops:
  7.2 114.9 %copy-start = (bf16[512,3072]{1,0:T(8,128)(2,1)S(1)}, bf16[512,3072]{1,0:T(8,128)(2,1)}, u32[]{:S(2)}) copy-start(bf16[512,3072]{1,0:T(8,128)(2,1)} %param.37) | copy-start | bytes 9437188
  7.2 260.8 %all-gather.17.cloned.1.call-start = ((), (), s32[]{:S(2)}) async-start(), calls=%async_computation.32 | async-start | bytes 2949120 | tf_op jit(solution)/shard_map/all_gather | solution.py:417
  56.3 255.3 %all-gather.19.cloned.1.call-start = ((), (), s32[]{:S(2)}) async-start(), calls=%async_computation.33 | async-start | bytes 3932160 | tf_op jit(solution)/shard_map/all_gather | solution.py:417
  118.3 14.4 %all-to-all-start = ((bf16[32,2,2048]{2,1,0:T(2,128)(2,1)}), bf16[32,2,2048]{2,1,0:T(2,128)(2,1)}, u32[]{:S(2)}, u32[]{:S(2)}) async-start(bf16[32,2,2048]{2,1,0:T(2,128)(2,1)} %reshape.632), calls=%async_computation | async-start | bytes 524288 | tf_op jit(solution)/shard_map/all_to_all | solution.py:31
  124.3 54.4 %copy-start.78 = (bf16[144,192]{1,0:T(8,128)(2,1)S(1)}, bf16[144,192]{1,0:T(8,128)(2,1)}, u32[]{:S(2)}) copy-start(bf16[144,192]{1,0:T(8,128)(2,1)} %param.27) | copy-start | bytes 165892
  124.3 54.4 %copy-start.79 = (bf16[192,144]{0,1:T(8,128)(2,1)S(1)}, bf16[192,144]{0,1:T(8,128)(2,1)}, u32[]{:S(2)}) copy-start(bf16[192,144]{0,1:T(8,128)(2,1)} %param.44) | copy-start | bytes 165892
  132.7 15.6 %all-to-all-start.5 = ((bf16[8,64,384]{2,1,0:T(8,128)(2,1)}), bf16[8,64,384]{2,1,0:T(8,128)(2,1)S(1)}, u32[]{:S(2)}, u32[]{:S(2)}) async-start(bf16[8,64,384]{2,1,0:T(8,128)(2,1)} %reshape_broadcast_in_dim.3), calls=%async_computation.5 | async-start | bytes 786432 | tf_op jit(solution)/shard_map/all_to_all | solution.py:37
  136.5 179.3 %all-gather.11.cloned.1.call-start = ((), (), s32[]{:S(2)}) async-start(), calls=%async_computation.23 | async-start | bytes 5308416 | tf_op jit(solution)/shard_map/all_gather | solution.py:584
  149.0 23.3 %all-to-all-start.2 = ((f32[8,8,1536]{2,1,0:T(8,128)}), f32[8,8,1536]{2,1,0:T(8,128)S(1)}, u32[]{:S(2)}, u32[]{:S(2)}) async-start(f32[8,8,1536]{2,1,0:T(8,128)} %broadcast_in_dim.83), calls=%async_computation.2 | async-start | bytes 786432 | tf_op jit(solution)/shard_map/all_to_all | solution.py:31
  173.1 8.7 %all-to-all-start.6 = ((bf16[4,64,384]{2,1,0:T(8,128)(2,1)}), bf16[4,64,384]{2,1,0:T(8,128)(2,1)S(1)}, u32[]{:S(2)}, u32[]{:S(2)}) async-start(bf16[4,64,384]{2,1,0:T(8,128)(2,1)} %broadcast_in_dim.90), calls=%async_computation.6 | async-start | bytes 393216 | tf_op jit(solution)/shard_map/all_to_all | solution.py:31
  182.9 66.1 %all-to-all-start.1 = ((bf16[8,303,192]{1,2,0:T(8,128)(2,1)}), bf16[8,303,192]{1,2,0:T(8,128)(2,1)S(1)}, u32[]{:S(2)}, u32[]{:S(2)}) async-start(bf16[8,303,192]{1,2,0:T(8,128)(2,1)} %broadcast_in_dim.78), calls=%async_computation.1 | async-start | bytes 2359296 | tf_op jit(solution)/shard_map/all_to_all | solution.py:31
  189.2 92.4 %copy-start.36 = (f32[16,1024]{1,0:T(8,128)}, f32[16,1024]{1,0:T(8,128)S(1)}, u32[]{:S(2)}) copy-start(f32[16,1024]{1,0:T(8,128)S(1)} %mul.928) | copy-start | bytes 196612
  189.5 92.2 %copy-start.38 = (f32[16,1024]{1,0:T(8,128)}, f32[16,1024]{1,0:T(8,128)S(1)}, u32[]{:S(2)}) copy-start(f32[16,1024]{1,0:T(8,128)S(1)} %tile.83) | copy-start | bytes 196612
  189.7 92.0 %copy-start.50 = (f32[16,1024]{1,0:T(8,128)}, f32[16,1024]{1,0:T(8,128)S(1)}, u32[]{:S(2)}) copy-start(f32[16,1024]{1,0:T(8,128)S(1)} %mul.931) | copy-start | bytes 196612
  189.8 91.9 %copy-start.51 = (f32[16,1024]{1,0:T(8,128)}, f32[16,1024]{1,0:T(8,128)S(1)}, u32[]{:S(2)}) copy-start(f32[16,1024]{1,0:T(8,128)S(1)} %tile.85) | copy-start | bytes 196612
  190.4 68.7 %copy-start.89 = (pred[64,8]{0,1:T(8,128)(4,1)}, pred[64,8]{0,1:T(8,128)(4,1)S(1)}, u32[]{:S(2)}) copy-start(pred[64,8]{0,1:T(8,128)(4,1)S(1)} %iota_compare_fusion.3) | copy-start | bytes 1540
  249.7 8.7 %all-to-all-start.3 = ((f32[4,8,1536]{2,1,0:T(8,128)}), f32[4,8,1536]{2,1,0:T(8,128)S(1)}, u32[]{:S(2)}, u32[]{:S(2)}) async-start(f32[4,8,1536]{2,1,0:T(8,128)} %broadcast_in_dim.84), calls=%async_computation.3 | async-start | bytes 393216 | tf_op jit(solution)/shard_map/all_to_all | solution.py:31
  253.1 111.8 %all-gather.9.cloned.1.call-start = ((), (), s32[]{:S(2)}) async-start(), calls=%async_computation.22 | async-start | bytes 3538944 | tf_op jit(solution)/shard_map/all_gather | solution.py:585
  278.6 3.3 collective-permute-start
  280.2 3.9 collective-permute-start.1
  302.3 165.3 %reduce-scatter.9.cloned.1.call-start = ((), (), s32[]{:S(2)}) async-start(), calls=%async_computation.25 | async-start | bytes 3538944 | tf_op jit(solution)/shard_map/reduce_scatter | solution.py:620
  394.2 150.4 %reduce-scatter.7.cloned.1.call-start = ((), (), s32[]{:S(2)}) async-start(), calls=%async_computation.24 | async-start | bytes 3538944 | tf_op jit(solution)/shard_map/reduce_scatter | solution.py:620
  399.8 223.0 %reduce-scatter.17.cloned.1.call-start = ((), (), s32[]{:S(2)}) async-start(), calls=%async_computation.31 | async-start | bytes 1966080 | tf_op jit(solution)/shard_map/reduce_scatter | solution.py:874
  405.1 287.0 %reduce-scatter.15.cloned.1.call-start = ((), (), s32[]{:S(2)}) async-start(), calls=%async_computation.30 | async-start | bytes 3932160 | tf_op jit(solution)/shard_map/reduce_scatter | solution.py:856
  412.9 54.6 %copy-start.77 = (f32[1536]{0:T(1024)S(1)}, f32[1536]{0:T(1024)}, u32[]{:S(2)}) copy-start(f32[1536]{0:T(1024)} %copy-done.76) | copy-start | bytes 18436
  412.9 131.7 %copy-start.63 = (f32[16,1536]{1,0:T(8,128)S(1)}, f32[16,1536]{1,0:T(8,128)}, u32[]{:S(2)}) copy-start(f32[16,1536]{1,0:T(8,128)} %get-tuple-element.208) | copy-start | bytes 294916
  554.9 15.2 %all-to-all-start.8 = ((bf16[8,128,192]{1,2,0:T(8,128)(2,1)}), bf16[8,128,192]{1,2,0:T(8,128)(2,1)S(1)}, u32[]{:S(2)}, u32[]{:S(2)}) async-start(bf16[8,128,192]{1,2,0:T(8,128)(2,1)} %bitcast.50), calls=%async_computation.10 | async-start | bytes 786432 | tf_op jit(solution)/shard_map/all_to_all | solution.py:37
  558.7 191.2 %all-gather.15.cloned.1.call-start = ((), (), s32[]{:S(2)}) async-start(), calls=%async_computation.28 | async-start | bytes 1966080 | tf_op jit(solution)/shard_map/all_gather | solution.py:692
  561.7 221.4 %reduce-scatter.11.cloned.1.call-start = ((), (), s32[]{:S(2)}) async-start(), calls=%async_computation.26 | async-start | bytes 2949120 | tf_op jit(solution)/shard_map/reduce_scatter | solution.py:856
  601.8 3.2 collective-permute-start.6
  603.2 3.6 collective-permute-start.7
  622.8 112.3 %collective-permute-start.11 = (bf16[128,1536]{1,0:T(8,128)(2,1)}, bf16[128,1536]{1,0:T(8,128)(2,1)}, u32[]{:S(2)}, u32[]{:S(2)}) collective-permute-start(bf16[128,1536]{1,0:T(8,128)(2,1)} %reduce-scatter.17.cloned.1.call-done), channel_id=1, source_target_pairs={{0,0},{1,4},{2,8},{3,12},{4,16},{5,20},{6,24},{7,28},{8,1},{9,5},{... | collective-permute-start | bytes 1179656 | tf_op jit(solution)/shard_map/ppermute | solution.py:879
  636.0 18.0 %all-to-all-start.13 = ((bf16[4,96,256]{2,1,0:T(8,128)(2,1)}), bf16[4,96,256]{2,1,0:T(8,128)(2,1)S(1)}, u32[]{:S(2)}, u32[]{:S(2)}) async-start(bf16[4,96,256]{2,1,0:T(8,128)(2,1)} %bitcast.96), calls=%async_computation.16 | async-start | bytes 393216 | tf_op jit(solution)/shard_map/all_to_all | solution.py:37
  654.0 26.6 %all-to-all-start.14 = ((bf16[4,128,384]{2,1,0:T(8,128)(2,1)}), bf16[4,128,384]{2,1,0:T(8,128)(2,1)}, u32[]{:S(2)}, u32[]{:S(2)}) async-start(bf16[4,128,384]{2,1,0:T(8,128)(2,1)} %bitcast.338), calls=%async_computation.17 | async-start | bytes 786432 | tf_op jit(solution)/shard_map/all_to_all | solution.py:37
  658.1 136.1 %all-gather.13.cloned.1.call-start = ((), (), s32[]{:S(2)}) async-start(), calls=%async_computation.27 | async-start | bytes 1622016 | tf_op jit(solution)/shard_map/all_gather | solution.py:764
  680.6 12.0 %all-to-all-start.9 = ((bf16[8,2,1152]{2,1,0:T(2,128)(2,1)}), bf16[8,2,1152]{2,1,0:T(2,128)(2,1)S(1)}, u32[]{:S(2)}, u32[]{:S(2)}) async-start(bf16[8,2,1152]{2,1,0:T(2,128)(2,1)} %reshape.634), calls=%async_computation.11 | async-start | bytes 73728 | tf_op jit(solution)/shard_map/all_to_all | solution.py:37
  692.6 30.3 %all-to-all-start.15 = ((bf16[8,48,1024]{2,1,0:T(8,128)(2,1)}), bf16[8,48,1024]{2,1,0:T(8,128)(2,1)}, u32[]{:S(2)}, u32[]{:S(2)}) async-start(bf16[8,48,1024]{2,1,0:T(8,128)(2,1)} %bitcast.344), calls=%async_computation.20 | async-start | bytes 1572864 | tf_op jit(solution)/shard_map/all_to_all | solution.py:37
  722.9 42.0 %all-to-all-start.10 = ((bf16[32,326,48]{1,2,0:T(8,128)(2,1)}), bf16[32,326,48]{1,2,0:T(8,128)(2,1)}, u32[]{:S(2)}, u32[]{:S(2)}) async-start(bf16[32,326,48]{1,2,0:T(8,128)(2,1)} %bitcast.89), calls=%async_computation.12 | async-start | bytes 2359296 | tf_op jit(solution)/shard_map/all_to_all | solution.py:37
  729.9 102.4 %reduce-scatter.13.cloned.1.call-start = ((), (), s32[]{:S(2)}) async-start(), calls=%async_computation.29 | async-start | bytes 1327104 | tf_op jit(solution)/shard_map/reduce_scatter | solution.py:693
  730.9 6.3 collective-permute-start.2
  733.0 4.3 collective-permute-start.3
  737.4 15.9 %collective-permute-start.4 = (bf16[18,1,144]{2,1,0:T(2,128)(2,1)S(1)}, bf16[18,1,144]{2,1,0:T(2,128)(2,1)S(1)}, u32[]{:S(2)}, u32[]{:S(2)}) collective-permute-start(bf16[18,1,144]{2,1,0:T(2,128)(2,1)S(1)} %get-tuple-element.220), channel_id=1, source_target_pairs={{1,0},{2,1},{3,2},{4,3},{5,4},{6,5},{7,6},{9,8},{10,9},{11,10},{12... | collective-permute-start | bytes 15560 | tf_op jit(solution)/shard_map/ppermute | solution.py:53
  738.7 14.6 %collective-permute-start.5 = (bf16[18,1,144]{2,1,0:T(2,128)(2,1)S(1)}, bf16[18,1,144]{2,1,0:T(2,128)(2,1)S(1)}, u32[]{:S(2)}, u32[]{:S(2)}) collective-permute-start(bf16[18,1,144]{2,1,0:T(2,128)(2,1)S(1)} %get-tuple-element.221), channel_id=1, source_target_pairs={{0,1},{1,2},{2,3},{3,4},{4,5},{5,6},{6,7},{8,9},{9,10},{10,11},{11... | collective-permute-start | bytes 15560 | tf_op jit(solution)/shard_map/ppermute | solution.py:53
  744.1 10.2 %collective-permute-start.8 = (bf16[1,8,16]{0,2,1:T(8,128)(2,1)S(1)}, bf16[1,8,16]{0,2,1:T(8,128)(2,1)S(1)}, u32[]{:S(2)}, u32[]{:S(2)}) collective-permute-start(bf16[1,8,16]{0,2,1:T(8,128)(2,1)S(1)} %get-tuple-element.224), channel_id=1, source_target_pairs={{0,8},{8,16},{16,24},{1,9},{9,17},{17,25},{2,10},{10,18},{18,26},{... | collective-permute-start | bytes 776 | tf_op jit(solution)/shard_map/ppermute | solution.py:53
  748.6 5.6 collective-permute-start.9
  767.6 15.5 %all-to-all-start.11 = ((bf16[32,2,768]{2,1,0:T(2,128)(2,1)}), bf16[32,2,768]{2,1,0:T(2,128)(2,1)S(1)}, u32[]{:S(2)}, u32[]{:S(2)}) async-start(bf16[32,2,768]{2,1,0:T(2,128)(2,1)} %reshape.636), calls=%async_computation.13 | async-start | bytes 196608 | tf_op jit(solution)/shard_map/all_to_all | solution.py:31
  783.1 50.8 %all-to-all-start.12 = ((bf16[8,48,768]{2,1,0:T(8,128)(2,1)}), bf16[8,48,768]{2,1,0:T(8,128)(2,1)}, u32[]{:S(2)}, u32[]{:S(2)}) async-start(bf16[8,48,768]{2,1,0:T(8,128)(2,1)} %bitcast.350), calls=%async_computation.15 | async-start | bytes 1179648 | tf_op jit(solution)/shard_map/all_to_all | solution.py:37
  790.8 3.4 collective-permute-start.10
  (99 other events, 1051.3 us)
Sparse Core Ops, SparseCore 0:
  56.5 22.4 all-gather.16
  114.0 30.3 all-gather.18
  146.6 108.2 all-gather.10
  302.4 62.4 all-gather.8
  394.3 73.1 reduce-scatter.8
  471.0 73.6 reduce-scatter.6
  547.2 27.3 reduce-scatter.16
  577.3 42.1 reduce-scatter.14
  621.0 32.0 all-gather.14
  655.5 37.4 reduce-scatter.10
  696.3 63.7 all-gather.12
  763.8 68.4 reduce-scatter.12

commit v2 on v1

v2 whole, which is shorter than its diff:
```python
import functools
import math

import jax
import jax.numpy as jnp
import numpy as np
from jax import lax
from jax.experimental import pallas as pl
from jax.experimental.pallas import tpu as pltpu
from jax.sharding import Mesh, PartitionSpec as P

HD = 64
NBAND = 8
MOSTH = 8
HALO = 8
LANES = 256

EPS = 1e-06
THETA = 10000.0
NEG = -1e30
HIGH = lax.Precision.HIGHEST
OFFSETS = ((-1, -1), (-1, 0), (-1, 1), (0, -1), (0, 0), (0, 1), (1, -1), (1, 0), (1, 1))
ALL = ("row", "sub", "tp")
COL = ("sub", "tp")
f32 = jnp.float32
bf16 = jnp.bfloat16


def spread_all(value, axes):
    count = lax.axis_size(axes)
    return lax.all_to_all(
        jnp.broadcast_to(value[None], (count,) + value.shape), axes, 0, 0, tiled=True
    )


def swap(value, axes):
    return lax.all_to_all(value, axes, 0, 0, tiled=True)


def nothing(*others):
    return sum(other[(0,) * other.ndim].astype(f32) * 0.0 for other in others)


def after(value, *others):
    return value + nothing(*others).astype(value.dtype)


def waits_for(kernel, at, count):
    def run(*refs):
        return kernel(*refs[:at], *refs[at + count :])

    return run


def cost(microseconds):
    return pl.CostEstimate(
        flops=int(microseconds * 1e9), bytes_accessed=int(microseconds * 3e6), transcendentals=0
    )


ANYWHERE = pl.BlockSpec(memory_space=pl.ANY)


def pairwise(value, flip):
    return lax.ppermute(value, "row", [(i, i ^ flip) for i in range(4)])


def row_gather(value):
    if lax.axis_size("row") != 4:
        return lax.all_gather(value, "row", axis=0)
    row = lax.axis_index("row")
    chip, core = row // 2, row % 2
    other = pairwise(value, 2)
    pair = jnp.stack([jnp.where(chip == 0, value, other), jnp.where(chip == 0, other, value)])
    far = pairwise(pair, 1)
    both = jnp.stack([jnp.where(core == 0, pair, far), jnp.where(core == 0, far, pair)], axis=1)
    return both.reshape((4,) + value.shape)


def row_scatter(value):
    count = lax.axis_size("row")
    if count != 4:
        return lax.psum_scatter(value, "row", scatter_dimension=0, tiled=True)
    row = lax.axis_index("row")
    chip, core = row // 2, row % 2
    parts = value.astype(bf16).reshape((2, 2, value.shape[0] // 4) + value.shape[1:])

    def pick(array, which, axis):
        return lax.dynamic_index_in_dim(array, which, axis, keepdims=False)

    near = pairwise(pick(parts, 1 - core, 1), 1)
    kept = (pick(parts, core, 1).astype(f32) + near.astype(f32)).astype(bf16)
    far = pairwise(pick(kept, 1 - chip, 0), 2)
    return pick(kept, chip, 0).astype(f32) + far.astype(f32)


def row_sums(value, rows):
    if lax.axis_size("row") != 4:
        return row_scatter(value), lax.psum(rows.astype(bf16), "row").astype(f32)
    row = lax.axis_index("row")
    chip, core = row // 2, row % 2
    size = value.shape[0] // 4
    parts = value.astype(bf16).reshape((2, 2, size) + value.shape[1:])
    rows = rows.astype(bf16)

    def pick(array, which, axis):
        return lax.dynamic_index_in_dim(array, which, axis, keepdims=False)

    sent = pick(parts, 1 - core, 1).reshape((2 * size,) + value.shape[1:])
    near = pairwise(jnp.concatenate([sent, rows], axis=0), 1).astype(f32)
    kept = pick(parts, core, 1).astype(f32) + near[: 2 * size].reshape((2, size) + value.shape[1:])
    kept = kept.astype(bf16)
    rows = (rows.astype(f32) + near[2 * size :]).astype(bf16)
    far = pairwise(jnp.concatenate([pick(kept, 1 - chip, 0), rows], axis=0), 2).astype(f32)
    return pick(kept, chip, 0).astype(f32) + far[:size], rows.astype(f32) + far[size:]


def ring_of(count):
    return list(range(0, count, 2)) + list(range(count - 1, 0, -2))


def look_up(table, index):
    ids = jnp.arange(len(table))
    return jnp.sum(jnp.where(ids == index, jnp.asarray(table, jnp.int32), 0)).astype(jnp.int32)


def ring_steps(axis):
    count = lax.axis_size(axis)
    ring = ring_of(count)
    place = look_up([ring.index(i) for i in range(count)], lax.axis_index(axis))

    def member(step):
        return look_up(ring, lax.rem(place + (step + count), count))

    def onward(value):
        return lax.ppermute(value, axis, [(ring[i], ring[(i + 1) % count]) for i in range(count)])

    def back(value):
        return lax.ppermute(value, axis, [(ring[(i + 1) % count], ring[i]) for i in range(count)])

    return member, onward, back


def ring_gather(value, axis):
    count = lax.axis_size(axis)
    member, onward, back = ring_steps(axis)
    rows = value.shape[0]
    pieces, starts = [value], [member(0) * rows]
    right = left = value
    for step in range(1, count // 2):
        right, left = onward(right), back(left)
        pieces += [right, left]
        starts += [member(-step) * rows, member(step) * rows]
    half = rows // 2
    far = member(count // 2) * rows
    pieces += [onward(right[:half]), back(left[half:])]
    starts += [far, far + half]
    return pieces, jnp.stack(starts)


def ring_scatter(block, axis, beside):
    count = lax.axis_size(axis)
    member, onward, back = ring_steps(axis)
    beside, done = list(beside), []

    def step_on(right, left):
        held = (right, left)
        right, left = onward(right.astype(bf16)), back(left.astype(bf16))
        if beside:
            done.append(beside.pop(0)(held))
            right, left = after(right.astype(f32), *done[-1]), left.astype(f32)
        return right.astype(f32), left.astype(f32)

    far = block(member(count // 2)).astype(bf16)
    half = far.shape[0] // 2
    far_right, far_left = onward(far[:half]), back(far[half:])
    right = block(member(count // 2 - 1))
    left = block(member(1 - count // 2))
    right = jnp.concatenate([right[:half] + far_right.astype(f32), right[half:]], axis=0)
    left = jnp.concatenate([left[:half], left[half:] + far_left.astype(f32)], axis=0)
    for step in range(count // 2 - 2, 0, -1):
        right, left = step_on(right, left)
        right = right + block(member(step))
        left = left + block(member(-step))
    own = block(member(0))
    right, left = step_on(right, left)
    return right + left + own, done


def pack_kernel(copies, *refs):
    for source, source_lead, source_at, target, target_lead, target_at, size in copies:
        taken = slice(source_at, source_at + size)
        given = slice(target_at, target_at + size)
        value = refs[source][:, taken] if source_lead is None else refs[source][source_lead, :, taken]
        value = value.astype(refs[target].dtype)
        if target_lead is None:
            refs[target][:, given] = value
        else:
            refs[target][target_lead, :, given] = value


def pack(copies, out_shapes, *sources):
    return pl.pallas_call(
        functools.partial(pack_kernel, copies),
        out_shape=out_shapes,
        compiler_params=pltpu.CompilerParams(vmem_limit_bytes=48 * 2**20),
        name="pack",
        cost_estimate=cost(1),
    )(*sources)


def dot(left, right, left_dim, right_dim, precision=None):
    return lax.dot_general(
        left,
        right,
        (((left_dim,), (right_dim,)), ((), ())),
        precision=precision,
        preferred_element_type=f32,
    )


def shift(cells, axis, up):
    count = lax.axis_size(axis)
    pairs = [(i, i + 1) if up else (i + 1, i) for i in range(count - 1)]
    return lax.ppermute(cells, axis, pairs)


def silu_slope(values):
    sigmoid = jax.nn.sigmoid(values)
    return sigmoid * (1.0 + values * (1.0 - sigmoid))


def gather_cells(padded, row_count, col_count):
    return jnp.concatenate(
        [
            padded[1 + row_off : 1 + row_off + row_count, 1 + col_off : 1 + col_off + col_count]
            for row_off, col_off in OFFSETS
        ],
        axis=-1,
    )


def spread_cells(padded, row_count, col_count, channels):
    summed = jnp.zeros((row_count, col_count, channels), f32)
    for offset_index, (row_off, col_off) in enumerate(OFFSETS):
        summed = summed + padded[
            1 - row_off : 1 - row_off + row_count,
            1 - col_off : 1 - col_off + col_count,
            offset_index * channels : (offset_index + 1) * channels,
        ].astype(f32)
    return summed


def row_items(heights, band_ids, row_count):
    count = heights.shape[0]
    below = jnp.arange(count)[:, None] >= jnp.arange(count)[None, :]
    item_ends = jnp.sum(jnp.where(below, heights[None, :], 0), axis=1)
    row_ids = jnp.arange(row_count, dtype=jnp.int32)
    item_of_row = jnp.sum((item_ends[None, :] <= row_ids[:, None]).astype(jnp.int32), axis=1)
    picked = item_of_row[:, None] == jnp.arange(count, dtype=jnp.int32)[None, :]
    item_top = jnp.sum(jnp.where(picked, (item_ends - heights)[None, :], 0), axis=1)
    row_band = jnp.sum(jnp.where(picked, band_ids[None, :], 0), axis=1)
    band_onehot = (row_band[:, None] == jnp.arange(NBAND, dtype=jnp.int32)[None, :]).astype(f32)
    return (item_of_row, row_ids - item_top, band_onehot)


def tn(left, right):
    return dot(left, right, 0, 0)


def nt(left, right):
    return dot(left, right, 1, 1)


def nn(left, right):
    return dot(left, right, 1, 0)


def masked_scores(key_block, query_block, bias):
    return tn(key_block, query_block) + bias


def block_bias(items_ref, item_query, chunk, key_rows, width):
    rows = []
    for key_row in range(key_rows):
        item = items_ref[chunk * key_rows + key_row]
        rows.append(
            jnp.broadcast_to(jnp.where(item_query == item, 0.0, NEG), (width, item_query.shape[1]))
        )
    return rows[0] if len(rows) == 1 else jnp.concatenate(rows, axis=0)


def lay_out(block, near_ref, *parts):
    @pl.when(block == 0)
    def _():
        at = 0
        for part in parts:
            near_ref[:, at : at + part.shape[1]] = part[...]
            at += part.shape[1]


def attend_kernel(
    heads,
    key_rows,
    key_width,
    items_ref,
    low_ref,
    high_ref,
    item_query_ref,
    query_ref,
    above_ref,
    both_ref,
    below_ref,
    cross_ref,
    caption_key_ref,
    caption_value_ref,
    gate_ref,
    mixed_ref,
    self_ref,
    crossed_ref,
    stats_ref,
    total_ref,
    near_ref,
):
    block = pl.program_id(0)
    head_width = heads * HD
    lay_out(block, near_ref, above_ref, both_ref, below_ref)
    item_query = item_query_ref[0:1, :]
    self_ref[...] = jnp.zeros_like(self_ref)
    total_ref[...] = jnp.zeros_like(total_ref)

    def chunk_step(chunk, carry):
        lanes = pl.ds(pl.multiple_of(chunk * LANES, LANES), LANES)
        bias = block_bias(items_ref, item_query, chunk, key_rows, key_width)
        for head in range(heads):
            part = slice(head * HD, (head + 1) * HD)
            value_part = slice(head_width + head * HD, head_width + (head + 1) * HD)
            scores = masked_scores(near_ref[part, lanes], query_ref[part, :], bias)
            weights = jnp.exp(scores)
            total_ref[head : head + 1, :] += jnp.sum(weights, axis=0, keepdims=True)
            self_ref[part, :] += nn(near_ref[value_part, lanes], weights.astype(bf16))
        return carry

    lax.fori_loop(low_ref[block], high_ref[block], chunk_step, 0)
    stats_ref[...] = jnp.zeros_like(stats_ref)
    for head in range(heads):
        part = slice(head * HD, (head + 1) * HD)
        total = total_ref[head : head + 1, :]
        attended = self_ref[part, :] / total
        self_ref[part, :] = attended
        stats_ref[head : head + 1, :] = jnp.log(total)
        scores = tn(caption_key_ref[part, :], cross_ref[part, :])
        best = jnp.max(scores, axis=0, keepdims=True)
        weights = jnp.exp(scores - best)
        total = jnp.sum(weights, axis=0, keepdims=True)
        crossed = nn(caption_value_ref[part, :], (weights / total).astype(bf16))
        crossed_ref[part, :] = crossed
        stats_ref[heads + head : heads + head + 1, :] = best + jnp.log(total)
        mixed_ref[part, :] = (attended + gate_ref[part, 0:1] * crossed).astype(bf16)


def cross_back_kernel(
    heads,
    cross_ref,
    caption_key_ref,
    caption_value_ref,
    gate_ref,
    grad_ref,
    crossed_ref,
    stats_ref,
    grad_cross_ref,
    grad_key_ref,
    grad_value_ref,
    grad_gate_ref,
):
    @pl.when(pl.program_id(0) == 0)
    def _():
        grad_key_ref[...] = jnp.zeros_like(grad_key_ref)
        grad_value_ref[...] = jnp.zeros_like(grad_value_ref)
        grad_gate_ref[...] = jnp.zeros_like(grad_gate_ref)

    for head in range(heads):
        part = slice(head * HD, (head + 1) * HD)
        gate = gate_ref[part, 0:1]
        grad_wide = grad_ref[part, :].astype(f32)
        grad_crossed = (gate * grad_wide).astype(bf16)
        grad_gate_ref[part, 0:1] += jnp.sum(
            grad_wide * crossed_ref[part, :], axis=1, keepdims=True
        ) * (1.0 - gate * gate)
        scores = tn(caption_key_ref[part, :], cross_ref[part, :])
        weights = jnp.exp(scores - stats_ref[heads + head : heads + head + 1, :])
        grad_weights = tn(caption_value_ref[part, :], grad_crossed)
        delta = jnp.sum(weights * grad_weights, axis=0, keepdims=True)
        grad_scores = (weights * (grad_weights - delta)).astype(bf16)
        grad_cross_ref[part, :] = (
            nn(caption_key_ref[part, :], grad_scores) * (1.0 / math.sqrt(HD))
        ).astype(bf16)
        grad_key_ref[part, :] += nt(cross_ref[part, :], grad_scores)
        grad_value_ref[part, :] += nt(grad_crossed, weights.astype(bf16))


def attend_back_kernel(
    heads,
    key_rows,
    key_width,
    items_ref,
    low_ref,
    high_ref,
    item_query_ref,
    query_ref,
    above_ref,
    both_ref,
    below_ref,
    grad_ref,
    self_ref,
    stats_ref,
    grad_query_ref,
    grad_both_ref,
    delta_ref,
    near_ref,
):
    block = pl.program_id(0)
    head_width = heads * HD
    lay_out(block, near_ref, above_ref, both_ref, below_ref)

    @pl.when(block == 0)
    def _():
        grad_both_ref[...] = jnp.zeros_like(grad_both_ref)

    item_query = item_query_ref[0:1, :]
    grad_query_ref[...] = jnp.zeros_like(grad_query_ref)
    for head in range(heads):
        part = slice(head * HD, (head + 1) * HD)
        delta_ref[head : head + 1, :] = jnp.sum(
            grad_ref[part, :].astype(f32) * self_ref[part, :], axis=0, keepdims=True
        )

    def chunk_step(chunk, carry):
        lanes = pl.ds(pl.multiple_of(chunk * LANES, LANES), LANES)
        bias = block_bias(items_ref, item_query, chunk, key_rows, key_width)
        for head in range(heads):
            part = slice(head * HD, (head + 1) * HD)
            value_part = slice(head_width + head * HD, head_width + (head + 1) * HD)
            key_block = near_ref[part, lanes]
            query_block = query_ref[part, :]
            grad_block = grad_ref[part, :]
            scores = masked_scores(key_block, query_block, bias)
            weights = jnp.exp(scores - stats_ref[head : head + 1, :])
            grad_weights = tn(near_ref[value_part, lanes], grad_block)
            grad_scores = (weights * (grad_weights - delta_ref[head : head + 1, :])).astype(bf16)
            grad_query_ref[part, :] += nn(key_block, grad_scores)
            grad_both_ref[part, lanes] += nt(query_block, grad_scores)
            grad_both_ref[value_part, lanes] += nt(grad_block, weights.astype(bf16))
        return carry

    lax.fori_loop(low_ref[block], high_ref[block], chunk_step, 0)


def turn(values, tables):
    quarter = HD // 4
    first, second, third, fourth = (values[i * quarter : (i + 1) * quarter] for i in range(4))
    cos_rows, sin_rows, cos_cols, sin_cols = (
        tables[i * quarter : (i + 1) * quarter] for i in range(4)
    )
    return jnp.concatenate(
        [
            first * cos_rows - second * sin_rows,
            first * sin_rows + second * cos_rows,
            third * cos_cols - fourth * sin_cols,
            third * sin_cols + fourth * cos_cols,
        ],
        axis=0,
    )


def turn_back(values, tables):
    quarter = HD // 4
    first, second, third, fourth = (values[i * quarter : (i + 1) * quarter] for i in range(4))
    cos_rows, sin_rows, cos_cols, sin_cols = (
        tables[i * quarter : (i + 1) * quarter] for i in range(4)
    )
    return jnp.concatenate(
        [
            first * cos_rows + second * sin_rows,
            second * cos_rows - first * sin_rows,
            third * cos_cols + fourth * sin_cols,
            fourth * cos_cols - third * sin_cols,
        ],
        axis=0,
    )


def mean_inverse(values, axis):
    return lax.rsqrt(jnp.mean(values * values, axis=axis, keepdims=True) + EPS)


def project_kernel(
    heads,
    span,
    near_ref,
    embed_ref,
    vector_ref,
    mod_ref,
    weight_ref,
    table_ref,
    gain_ref,
    embedded_ref,
    normed_ref,
    raw_ref,
    query_ref,
    both_ref,
    cross_ref,
):
    block = pl.program_id(0)
    model = embed_ref.shape[0]
    head_width = heads * HD
    embedded_ref[...] = nt(near_ref[...], embed_ref[...]) + vector_ref[0:1, :]
    for j in range(LANES // span):
        rows = slice(j * span, (j + 1) * span)
        embedded = embedded_ref[rows, :]
        scale = mod_ref[pl.ds(block * (LANES // span) + j, 1), 0:model]
        factor = vector_ref[1:2, :] * (1.0 + scale)
        normed_ref[rows, :] = (embedded * mean_inverse(embedded, -1) * factor).astype(bf16)
    raw = nn(normed_ref[...], weight_ref[...]).astype(bf16).astype(f32).T
    tables = table_ref[...]
    score_scale = 1.0 / math.sqrt(HD)
    raw_ref[...] = raw[0 : 2 * head_width].astype(bf16)
    for head in range(heads):
        part = slice(head * HD, (head + 1) * HD)
        query = raw[part]
        query = turn(query * mean_inverse(query, 0) * gain_ref[part, 0:1], tables)
        query_ref[part, :] = (query.astype(bf16).astype(f32) * score_scale).astype(bf16)
        key = raw[head_width + head * HD : head_width + (head + 1) * HD]
        key = turn(key * mean_inverse(key, 0) * gain_ref[part, 1:2], tables)
        both_ref[part, :] = key.astype(bf16)
    both_ref[head_width:, :] = raw[2 * head_width : 3 * head_width].astype(bf16)
    cross_ref[...] = (raw[3 * head_width :] * score_scale).astype(bf16)


def middle_kernel(
    pieces,
    span,
    own_ref,
    place_ref,
    *refs,
):
    mixed_refs, refs = refs[:pieces], refs[pieces:]
    (
        embedded_ref,
        patch_ref,
        vector_ref,
        mod_ref,
        output_ref,
        gu_ref,
        down_ref,
        unpatch_ref,
        mixed_ref,
        residual_ref,
        inner_ref,
        hidden_ref,
        grad_feed_ref,
        grad_gu_ref,
        part_residual_ref,
        part_branch_ref,
        grad_mixed_ref,
        scale_rows_ref,
        gate_rows_ref,
        gain_ref,
        branch_ref,
        grad_inner_ref,
    ) = refs
    block = pl.program_id(0)
    row_count = LANES // span
    model = embedded_ref.shape[1]
    groups = output_ref.shape[0]
    group = model // groups
    ff_mine = down_ref.shape[0]

    @pl.when(block == 0)
    def _():
        gain_ref[...] = jnp.zeros_like(gain_ref)

    for i, ref in enumerate(mixed_refs):
        size = ref.shape[0]
        mixed_ref[pl.ds(pl.multiple_of(place_ref[i], 32), size), :] = ref[...]
    for g in range(groups):
        branch_ref[:, g * group : (g + 1) * group] = tn(mixed_ref[...], output_ref[g])
    ff_gain = vector_ref[2:3, :]

    def mods(j, which):
        return mod_ref[
            pl.ds(block * row_count + j, 1), which * model : (which + 1) * model
        ]

    for j in range(row_count):
        rows = slice(j * span, (j + 1) * span)
        residual = embedded_ref[rows, :] + jnp.tanh(mods(j, 1)) * branch_ref[rows, :]
        residual_ref[rows, :] = residual
        factor = ff_gain * (1.0 + mods(j, 2))
        inner_ref[rows, :] = (residual * mean_inverse(residual, -1) * factor).astype(bf16)
    inner = inner_ref[...]
    ff_groups = gu_ref.shape[0]
    ff_group = 2 * ff_mine // ff_groups
    half = ff_groups // 2
    grad_inner_ref[...] = nt(patch_ref[...], unpatch_ref[...])
    for j in range(row_count):
        rows = slice(j * span, (j + 1) * span)
        grad_feed_ref[rows, :] = (jnp.tanh(mods(j, 3)) * grad_inner_ref[rows, :]).astype(bf16)
    grad_hidden = nt(grad_feed_ref[...], down_ref[...])
    for g in range(half):
        gate = nn(inner, gu_ref[g])
        upward = nn(inner, gu_ref[half + g])
        sigmoid = jax.nn.sigmoid(gate)
        silu = gate * sigmoid
        cols = slice(g * ff_group, (g + 1) * ff_group)
        hidden_ref[:, cols] = (silu * upward).astype(bf16)
        grad = grad_hidden[:, cols]
        grad_gu_ref[:, cols] = (
            grad * upward * (sigmoid * (1.0 + gate * (1.0 - sigmoid)))
        ).astype(bf16)
        grad_gu_ref[:, ff_mine + g * ff_group : ff_mine + (g + 1) * ff_group] = (
            grad * silu
        ).astype(bf16)
    own_column = lax.broadcasted_iota(jnp.int32, (span, 1), 0)
    mine = (own_column >= own_ref[0]) & (own_column < own_ref[1])
    for j in range(row_count):
        rows = slice(j * span, (j + 1) * span)
        part_residual_ref[rows, :] = jnp.where(mine, grad_inner_ref[rows, :], 0.0)
    total = nt(grad_gu_ref[:, 0:ff_group], gu_ref[0])
    for g in range(1, ff_groups):
        total = total + nt(grad_gu_ref[:, g * ff_group : (g + 1) * ff_group], gu_ref[g])
    grad_inner_ref[...] = total
    for j in range(row_count):
        rows = slice(j * span, (j + 1) * span)
        tanh_one = jnp.tanh(mods(j, 1))
        second_scale = mods(j, 2)
        residual = residual_ref[rows, :]
        inverse = mean_inverse(residual, -1)
        unit = residual * inverse
        grad_inner = grad_inner_ref[rows, :]
        summed = jnp.sum(grad_inner * unit, axis=0, keepdims=True)
        scale_rows_ref[pl.ds(block * row_count + j, 1), :] = summed * ff_gain
        gain_ref[0:1, :] += summed * (1.0 + second_scale)
        grad_unit = grad_inner * (ff_gain * (1.0 + second_scale))
        part = part_residual_ref[rows, :] + inverse * (
            grad_unit - unit * jnp.mean(grad_unit * unit, axis=-1, keepdims=True)
        )
        part_residual_ref[rows, :] = part
        part_branch_ref[rows, :] = (tanh_one * part).astype(bf16)
        gate_rows_ref[pl.ds(block * row_count + j, 1), :] = jnp.sum(
            part * branch_ref[rows, :], axis=0, keepdims=True
        ) * (1.0 - tanh_one * tanh_one)
    total = nt(output_ref[0], part_branch_ref[:, 0:group])
    for g in range(1, groups):
        total = total + nt(output_ref[g], part_branch_ref[:, g * group : (g + 1) * group])
    grad_mixed_ref[...] = total.astype(bf16)


def result_kernel(
    span,
    own_ref,
    hidden_ref,
    residual_ref,
    patch_ref,
    mod_ref,
    down_ref,
    unpatch_ref,
    cells_ref,
    grad_unpatch_ref,
    gate_rows_ref,
    feed_ref,
    grad_ref,
    result_ref,
):
    block = pl.program_id(0)
    row_count = LANES // span
    model = residual_ref.shape[1]

    @pl.when(block == 0)
    def _():
        grad_unpatch_ref[...] = jnp.zeros_like(grad_unpatch_ref)

    feed_ref[...] = nn(hidden_ref[...], down_ref[...])
    grad_ref[...] = nt(patch_ref[...], unpatch_ref[...])
    own_column = lax.broadcasted_iota(jnp.int32, (span, 1), 0)
    mine = (own_column >= own_ref[0]) & (own_column < own_ref[1])
    for j in range(row_count):
        rows = slice(j * span, (j + 1) * span)
        tanh_two = jnp.tanh(mod_ref[pl.ds(block * row_count + j, 1), 3 * model : 4 * model])
        feed = feed_ref[rows, :]
        result_ref[rows, :] = (
            jnp.where(mine, residual_ref[rows, :], 0.0) + tanh_two * feed
        ).astype(bf16)
        gate_rows_ref[pl.ds(block * row_count + j, 1), :] = jnp.sum(
            grad_ref[rows, :] * feed, axis=0, keepdims=True
        ) * (1.0 - tanh_two * tanh_two)
    cells_ref[...] = nn(result_ref[...], unpatch_ref[...])
    grad_unpatch_ref[...] += tn(patch_ref[...], result_ref[...])


def finish_kernel(
    heads,
    span,
    grad_query_ref,
    grad_key_ref,
    grad_value_ref,
    grad_cross_ref,
    raw_ref,
    table_ref,
    gain_ref,
    embedded_ref,
    part_residual_ref,
    near_ref,
    vector_ref,
    mod_ref,
    weight_ref,
    embed_ref,
    grad_raw_ref,
    cells_ref,
    grad_embed_ref,
    scale_rows_ref,
    sums_ref,
    head_sums_ref,
    turned_ref,
    grad_normed_ref,
    part_ref,
):
    block = pl.program_id(0)
    row_count = LANES // span
    model = embedded_ref.shape[1]
    head_width = heads * HD
    score_scale = 1.0 / math.sqrt(HD)

    @pl.when(block == 0)
    def _():
        grad_embed_ref[...] = jnp.zeros_like(grad_embed_ref)
        sums_ref[...] = jnp.zeros_like(sums_ref)
        head_sums_ref[...] = jnp.zeros_like(head_sums_ref)

    tables = table_ref[...]
    for which in range(2):
        for head in range(heads):
            part = slice(head * HD, (head + 1) * HD)
            if which == 0:
                grad = (grad_query_ref[part, :] * score_scale).astype(bf16).astype(f32)
            else:
                grad = grad_key_ref[part, :].astype(bf16).astype(f32)
            at = which * head_width + head * HD
            raw = raw_ref[at : at + HD, :].astype(f32)
            grad = turn_back(grad, tables)
            inverse = mean_inverse(raw, 0)
            unit = raw * inverse
            head_sums_ref[part, which : which + 1] += jnp.sum(grad * unit, axis=1, keepdims=True)
            grad = grad * gain_ref[part, which : which + 1]
            turned_ref[at : at + HD, :] = inverse * (
                grad - unit * jnp.mean(grad * unit, axis=0, keepdims=True)
            )
    turned_ref[2 * head_width : 3 * head_width, :] = grad_value_ref[...].astype(f32)
    turned_ref[3 * head_width :, :] = grad_cross_ref[...].astype(f32)
    grad_raw_ref[...] = turned_ref[...].T.astype(bf16)
    grad_normed_ref[...] = nt(grad_raw_ref[...], weight_ref[...])
    gain = vector_ref[1:2, :]
    for j in range(row_count):
        rows = slice(j * span, (j + 1) * span)
        scale = mod_ref[pl.ds(block * row_count + j, 1), 0:model]
        embedded = embedded_ref[rows, :]
        inverse = mean_inverse(embedded, -1)
        unit = embedded * inverse
        grad_normed = grad_normed_ref[rows, :]
        summed = jnp.sum(grad_normed * unit, axis=0, keepdims=True)
        scale_rows_ref[pl.ds(block * row_count + j, 1), :] = summed * gain
        sums_ref[0:1, :] += summed * (1.0 + scale)
        grad_unit = grad_normed * (gain * (1.0 + scale))
        part = part_residual_ref[rows, :] + inverse * (
            grad_unit - unit * jnp.mean(grad_unit * unit, axis=-1, keepdims=True)
        )
        part = part.astype(bf16)
        part_ref[rows, :] = part
        sums_ref[1:2, :] += jnp.sum(part.astype(f32), axis=0, keepdims=True)
    cells_ref[...] = nn(part_ref[...], embed_ref[...])
    grad_embed_ref[...] += tn(near_ref[...], part_ref[...])


def on_device(
    latents,
    captions,
    item_heights,
    item_bands,
    embedding,
    embed_bias,
    band_table,
    adaptive,
    adaptive_bias,
    attention_gain,
    projection,
    query_gain,
    key_gain,
    cross_query,
    caption_weight,
    cross_gate,
    output_weight,
    feedforward_gain,
    gate_weight,
    up_weight,
    down_weight,
    unpatch_weight,
    cotangent,
):
    rows_n, sub_n, tp_n = (lax.axis_size(a) for a in ALL)
    col_n = sub_n * tp_n
    all_n = rows_n * col_n
    row = lax.axis_index("row")
    sub = lax.axis_index("sub")
    tp = lax.axis_index("tp")
    tile_rows, tile_cols, channels = latents.shape
    grid_rows = tile_rows * rows_n
    grid_cols = tile_cols * col_n
    span = tile_cols * tp_n
    tokens = tile_rows * span
    own = tile_rows * tile_cols
    width = embed_bias.shape[0]
    model = width * col_n
    head_width = model // tp_n
    heads = head_width // HD
    owned = model // all_n
    quarter = width // rows_n
    ff = gate_weight.shape[1]
    ff_part = ff // col_n
    ff_mine = ff // tp_n
    text = captions.shape[0]
    patch = 9 * channels

    index = (row * sub_n + sub) * tp_n + tp
    col = sub * tp_n + tp

    def to_peers(piece):
        spread = jnp.broadcast_to(piece[None], (sub_n,) + piece.shape)
        return spread.reshape((col_n,) + piece.shape[1:])

    def share(pieces):
        whole = row_gather(pieces)
        return whole.transpose(1, 0, 2, 3).reshape(model, pieces.shape[2])

    def my_quarter(weight):
        return lax.dynamic_slice_in_dim(weight, row * quarter, quarter, 0)

    copies = []
    for t in range(tp_n):
        for i in range(3):
            copies.append((0, None, i * model + t * head_width, 2, t, i * head_width, head_width))
        copies.append((1, None, t * head_width, 2, t, 3 * head_width, head_width))
    qkvc_piece = pack(
        copies,
        jax.ShapeDtypeStruct((tp_n, quarter, 4 * head_width), bf16),
        my_quarter(projection),
        my_quarter(cross_query),
    )
    tiles = jnp.concatenate([latents, cotangent], axis=-1).reshape(-1, 128)
    tiles_width = -(-tiles.shape[0] // quarter) * 128
    tiles = jnp.pad(tiles, ((0, quarter * tiles_width // 128 - tiles.shape[0]), (0, 0)))
    tiles = tiles.reshape(tiles_width // 128, quarter, 128).transpose(1, 0, 2)
    tiles = jnp.broadcast_to(tiles.reshape(1, quarter, tiles_width), (tp_n, quarter, tiles_width))
    qkvc_pieces = swap(to_peers(jnp.concatenate([qkvc_piece, tiles], axis=2)), COL)
    weight_qkvc = share(qkvc_pieces[:, :, : 4 * head_width])
    tiles = qkvc_pieces[:, :, 4 * head_width :].reshape(col_n, quarter, tiles_width // 128, 128)
    tiles = tiles.transpose(0, 2, 1, 3).reshape(col_n, -1, 128)
    tiles = tiles[:, : own * 2 * channels // 128].reshape(
        col_n, tile_rows, tile_cols, 2 * channels
    )
    grid = tiles.transpose(1, 0, 2, 3).reshape(tile_rows, grid_cols, 2 * channels)
    grid = jnp.concatenate(
        [
            shift(grid[tile_rows - 1 :], "row", True),
            grid,
            shift(grid[:1], "row", False),
        ],
        axis=0,
    )
    grid = jnp.pad(grid, ((0, 0), (1, 1), (0, 0)))
    bordered = lax.dynamic_slice_in_dim(grid, sub * span, span + 2, 1)
    neighbours = gather_cells(bordered[..., 0:channels], tile_rows, span).reshape(tokens, patch)
    patch_grads = gather_cells(bordered[..., channels : 2 * channels], tile_rows, span)
    patch_grads = patch_grads.reshape(tokens, patch)

    mod_width = adaptive.shape[1] // rows_n
    mod_bias = lax.dynamic_update_slice_in_dim(
        jnp.zeros((adaptive.shape[1],), f32), adaptive_bias.astype(f32), col * adaptive_bias.shape[0], 0
    )
    silu_band = jax.nn.silu(band_table.astype(f32))

    def mod_columns(start, count):
        return (
            jnp.dot(
                silu_band,
                lax.dynamic_slice_in_dim(adaptive, start, count, 1).astype(f32),
                precision=HIGH,
            )
            + lax.dynamic_slice_in_dim(mod_bias, start, count, 0)
        ).astype(bf16)

    columns = jnp.concatenate(
        [
            embedding.T,
            embed_bias[:, None],
            attention_gain[:, None],
            feedforward_gain[:, None],
            band_table.T,
            mod_columns(row * mod_width, mod_width).T.reshape(width, -1),
        ],
        axis=1,
    )
    columns_n = columns.shape[1]
    wide = -(-columns_n // 128) * 128
    columns = jnp.pad(columns, ((0, 0), (0, wide - columns_n)))

    def in_quarters(array):
        parts = array.reshape(-1, quarter, array.shape[1])
        return parts.transpose(1, 0, 2).reshape(quarter, -1)

    def from_quarters(array, columns_each):
        parts = array.reshape(array.shape[:-1] + (-1, columns_each))
        parts = jnp.moveaxis(parts, -2, -3)
        return parts.reshape(parts.shape[:-3] + (-1, columns_each))

    text_part = text // rows_n
    cap_part = jnp.dot(
        lax.dynamic_slice(
            captions,
            (row * text_part, col * caption_weight.shape[0]),
            (text_part, caption_weight.shape[0]),
        ),
        caption_weight,
        preferred_element_type=f32,
    )
    copies = []
    for t in range(tp_n):
        for i in range(2):
            copies.append((0, None, i * model + t * head_width, 1, t, i * head_width, head_width))
    cap_part = pack(
        copies, jax.ShapeDtypeStruct((tp_n, text_part, 2 * head_width), bf16), cap_part
    )
    cap_lanes = 2 * head_width // 128
    cap_part = (
        cap_part.reshape(tp_n, text_part, cap_lanes, 128)
        .transpose(0, 2, 1, 3)
        .reshape(tp_n, -1, quarter, 128)
        .transpose(0, 2, 1, 3)
        .reshape(tp_n, quarter, -1)
    )
    same = jnp.concatenate(
        [in_quarters(columns), in_quarters(mod_columns(0, model).reshape(-1, 256))], axis=1
    )
    same_width = same.shape[1]
    sent = jnp.concatenate(
        [jnp.broadcast_to(same[None], (tp_n,) + same.shape), cap_part], axis=2
    )
    got = swap(to_peers(after(sent, qkvc_pieces)), COL)
    columns = from_quarters(got[:, :, : rows_n * wide], wide).reshape(model, wide)
    embedding_t = columns[:, 0:patch]
    at = patch + 3 + NBAND
    vectors = columns[:, patch:at].T.astype(f32)
    full_band = vectors[3:]
    first_scale = jnp.sum(got[:, :, rows_n * wide : same_width].astype(f32), axis=0)
    first_scale = from_quarters(first_scale, 256).reshape(NBAND, model)
    item_of_row, row_place, band_onehot = row_items(item_heights, item_bands, grid_rows)
    tile_onehot = lax.dynamic_slice_in_dim(band_onehot, row * tile_rows, tile_rows, 0)
    first_mods = jnp.dot(
        tile_onehot, after(first_scale, weight_qkvc, neighbours), precision=HIGH
    )
    mod_part = columns[:, at:columns_n].reshape(col_n, width, -1)
    mod_part = jnp.sum(mod_part.astype(f32), axis=0).reshape(mod_width, NBAND).T
    cap_part = jnp.sum(got[:, :, same_width:].astype(f32), axis=0).astype(bf16)

    output_width = model // rows_n
    output_piece = lax.dynamic_slice_in_dim(output_weight, row * output_width, output_width, 1)
    output_piece = lax.all_gather(output_piece, COL, axis=0, tiled=True)
    full_output = lax.all_gather(output_piece, "row", axis=0)

    shared_mods = NBAND * mod_width // quarter
    shared = row_gather(
        jnp.concatenate([in_quarters(mod_part.reshape(-1, 256).astype(bf16)), cap_part], axis=1)
    )
    caption_heads = (
        from_quarters(shared[:, :, shared_mods:], 128)
        .reshape(rows_n, cap_lanes, text_part, 128)
        .transpose(1, 3, 0, 2)
        .reshape(2 * head_width, text)
    )
    caption_keys = caption_heads[:head_width]
    caption_values = caption_heads[head_width:]

    frequency = THETA ** (-jnp.arange(HD // 4, dtype=f32) / (HD // 4))
    tile_place = lax.dynamic_slice_in_dim(row_place, row * tile_rows, tile_rows, 0)
    row_angles = frequency[:, None] * jnp.repeat(tile_place, span).astype(f32)[None, :]
    col_place = sub * span + jnp.tile(jnp.arange(span), tile_rows)
    col_angles = frequency[:, None] * col_place.astype(f32)[None, :]
    tables = jnp.concatenate(
        [jnp.cos(row_angles), jnp.sin(row_angles), jnp.cos(col_angles), jnp.sin(col_angles)],
        axis=0,
    )
    gate_column = jnp.tanh(_mine(cross_gate, tp, sub_n).astype(f32))[:, None]
    gains = jnp.stack(
        [_mine(query_gain, tp, sub_n).astype(f32), _mine(key_gain, tp, sub_n).astype(f32)], axis=1
    )
    blocks = tokens // LANES

    def by_block(count):
        return pl.BlockSpec((count, LANES), lambda i, *_: (0, i))

    def by_rows(count):
        return pl.BlockSpec((LANES, count), lambda i, *_: (i, 0))

    def whole(*shape):
        return pl.BlockSpec(shape, lambda i, *_: (0,) * len(shape))

    def struct(shape, dtype=f32):
        return jax.ShapeDtypeStruct(shape, dtype)

    vmem = pltpu.CompilerParams(vmem_limit_bytes=56 * 2**20)
    embedded, normed, raw, queries, both, raw_cross = pl.pallas_call(
        functools.partial(project_kernel, heads, span),
        grid=(blocks,),
        in_specs=[
            by_rows(patch),
            whole(model, patch),
            whole(*vectors.shape),
            whole(*first_mods.shape),
            whole(model, 4 * head_width),
            by_block(HD),
            whole(head_width, 2),
        ],
        out_specs=[
            by_rows(model),
            by_rows(model),
            by_block(2 * head_width),
            by_block(head_width),
            by_block(2 * head_width),
            by_block(head_width),
        ],
        out_shape=[
            struct((tokens, model)),
            struct((tokens, model), bf16),
            struct((2 * head_width, tokens), bf16),
            struct((head_width, tokens), bf16),
            struct((2 * head_width, tokens), bf16),
            struct((head_width, tokens), bf16),
        ],
        compiler_params=vmem,
        name="project",
        cost_estimate=cost(10),
    )(neighbours, embedding_t, vectors, first_mods, weight_qkvc, tables, gains)
    modulations = (
        from_quarters(shared[:, :, :shared_mods], 256)
        .reshape(rows_n, NBAND, mod_width)
        .transpose(1, 0, 2)
        .reshape(NBAND, adaptive.shape[1])
        .astype(f32)
    )
    mods = jnp.dot(tile_onehot, modulations, precision=HIGH)

    gu_width = 2 * ff_mine // rows_n
    which_half = rows_n // 2
    gu_source = jnp.where(row < which_half, gate_weight, up_weight)
    gu_piece = lax.dynamic_slice_in_dim(
        gu_source.reshape(width, sub_n, tp_n, which_half, ff_part // which_half),
        lax.rem(row, which_half),
        1,
        3,
    )
    gu_piece = gu_piece.transpose(2, 0, 1, 3, 4).reshape(tp_n, width, gu_width)
    unpatch_piece = jnp.pad(my_quarter(unpatch_weight), ((0, 0), (0, gu_width - patch)))
    gu_piece = jnp.concatenate(
        [gu_piece, jnp.broadcast_to(unpatch_piece[None], (tp_n,) + unpatch_piece.shape)], axis=1
    )
    gu_pieces = swap(to_peers(after(gu_piece, queries)), COL)
    down_mine = down_weight
    if sub_n > 1:
        down_mine = lax.all_gather(down_weight, "sub", axis=0, tiled=True)

    if sub_n > 1:
        both = (
            lax.all_gather(both, "sub", axis=0)
            .reshape(sub_n, 2 * head_width, tile_rows, span)
            .transpose(1, 2, 0, 3)
            .reshape(2 * head_width, tile_rows * grid_cols)
        )
    edge = HALO * grid_cols
    middle_cols = both.shape[1]
    above = shift(both[:, middle_cols - edge :], "row", True)
    below = shift(both[:, :edge], "row", False)

    near_rows = tile_rows + 2 * HALO
    key_rows = max(1, LANES // grid_cols)
    key_width = LANES // key_rows
    block_rows = LANES // span
    items_padded = jnp.concatenate(
        [
            jnp.full((HALO,), -1, jnp.int32),
            item_of_row.astype(jnp.int32),
            jnp.full((HALO,), item_heights.shape[0] + 1, jnp.int32),
        ]
    )
    items_near = lax.dynamic_slice_in_dim(items_padded, row * tile_rows, near_rows, 0)
    item_query = jnp.repeat(items_near[HALO : HALO + tile_rows], span)[None, :]
    chunk_items = jnp.repeat(items_near, grid_cols // (key_width)).reshape(-1, key_rows)
    query_items = items_near[HALO : HALO + tile_rows].reshape(blocks, block_rows)
    before = chunk_items[None, :, -1] < query_items[:, None, 0]
    reached = chunk_items[None, :, 0] <= query_items[:, None, -1]
    low = jnp.sum(before.astype(jnp.int32), axis=1)
    high = jnp.sum(reached.astype(jnp.int32), axis=1)
    chunk_items = chunk_items.reshape(-1)
    near = near_rows * grid_cols

    mixed, self_out, crossed, stats = pl.pallas_call(
        waits_for(functools.partial(attend_kernel, heads, key_rows, key_width), 12, 2),
        grid_spec=pltpu.PrefetchScalarGridSpec(
            num_scalar_prefetch=3,
            grid=(blocks,),
            in_specs=[
                by_block(1),
                by_block(head_width),
                whole(2 * head_width, edge),
                whole(2 * head_width, middle_cols),
                whole(2 * head_width, edge),
                by_block(head_width),
                whole(head_width, text),
                whole(head_width, text),
                whole(head_width, 1),
                ANYWHERE,
                ANYWHERE,
            ],
            out_specs=[by_block(head_width), by_block(head_width), by_block(head_width), by_block(8)],
            scratch_shapes=[
                pltpu.VMEM((8, LANES), f32),
                pltpu.VMEM((2 * head_width, near), bf16),
            ],
        ),
        out_shape=[
            jax.ShapeDtypeStruct((head_width, tokens), bf16),
            jax.ShapeDtypeStruct((head_width, tokens), f32),
            jax.ShapeDtypeStruct((head_width, tokens), f32),
            jax.ShapeDtypeStruct((8, tokens), f32),
        ],
        compiler_params=vmem,
        name="attend",
        cost_estimate=cost(14),
    )(
        chunk_items,
        low,
        high,
        item_query,
        queries,
        above,
        both,
        below,
        raw_cross,
        caption_keys,
        caption_values,
        gate_column,
        mods,
        patch_grads,
    )

    weight_gu = lax.all_gather(after(gu_pieces, mixed, full_output), "row", axis=0)
    full_unpatch = weight_gu[:, :, width:, :patch].transpose(1, 0, 2, 3).reshape(model, patch)
    weight_gu = weight_gu[:, :, :width].reshape(rows_n, model, gu_width)
    pieces, starts = ring_gather(mixed, "tp")
    own_span = jnp.stack([tp * tile_cols, (tp + 1) * tile_cols]).astype(jnp.int32)
    (
        mixed_all,
        residual,
        inner,
        hidden,
        grad_feed,
        grad_gu,
        part_residual,
        part_branch,
        grad_mixed,
        rows_second_scale,
        rows_first_gate,
        grad_ff_gain,
    ) = pl.pallas_call(
        functools.partial(middle_kernel, len(pieces), span),
        grid_spec=pltpu.PrefetchScalarGridSpec(
            num_scalar_prefetch=2,
            grid=(blocks,),
            in_specs=[by_block(piece.shape[0]) for piece in pieces]
            + [
                by_rows(model),
                by_rows(patch),
                whole(*vectors.shape),
                whole(*mods.shape),
                whole(*full_output.shape),
                whole(*weight_gu.shape),
                whole(*down_mine.shape),
                whole(model, patch),
            ],
            out_specs=[
                by_block(model),
                by_rows(model),
                by_rows(model),
                by_rows(ff_mine),
                by_rows(model),
                by_rows(2 * ff_mine),
                by_rows(model),
                by_rows(model),
                by_block(model),
                whole(tile_rows, model),
                whole(tile_rows, model),
                whole(8, model),
            ],
            scratch_shapes=[pltpu.VMEM((LANES, model), f32), pltpu.VMEM((LANES, model), f32)],
        ),
        out_shape=[
            struct((model, tokens), bf16),
            struct((tokens, model)),
            struct((tokens, model), bf16),
            struct((tokens, ff_mine), bf16),
            struct((tokens, model), bf16),
            struct((tokens, 2 * ff_mine), bf16),
            struct((tokens, model)),
            struct((tokens, model), bf16),
            struct((model, tokens), bf16),
            struct((tile_rows, model)),
            struct((tile_rows, model)),
            struct((8, model)),
        ],
        compiler_params=vmem,
        name="middle",
        cost_estimate=cost(35),
    )(
        own_span,
        starts,
        *pieces,
        embedded,
        patch_grads,
        vectors,
        mods,
        full_output,
        weight_gu,
        down_mine,
        full_unpatch,
    )

    def result_part(held):
        return pl.pallas_call(
            waits_for(functools.partial(result_kernel, span), 7, 2),
            grid_spec=pltpu.PrefetchScalarGridSpec(
                num_scalar_prefetch=1,
                grid=(blocks,),
                in_specs=[
                    by_rows(ff_mine),
                    by_rows(model),
                    by_rows(patch),
                    whole(*mods.shape),
                    whole(*down_mine.shape),
                    whole(model, patch),
                    ANYWHERE,
                    ANYWHERE,
                ],
                out_specs=[by_rows(patch), whole(patch, model), whole(tile_rows, model)],
                scratch_shapes=[
                    pltpu.VMEM((LANES, model), f32),
                    pltpu.VMEM((LANES, model), f32),
                    pltpu.VMEM((LANES, model), bf16),
                ],
            ),
            out_shape=[struct((tokens, patch)), struct((patch, model)), struct((tile_rows, model))],
            compiler_params=vmem,
            name="result",
        cost_estimate=cost(9),
        )(own_span, hidden, residual, patch_grads, mods, down_mine, full_unpatch, *held)

    def mixed_block(which):
        return lax.dynamic_slice_in_dim(
            grad_mixed, which * head_width, head_width, 0
        ).astype(f32)

    def gu_part(held):
        return (dot(inner, after(grad_gu, *held), 0, 0).astype(bf16),)

    def output_part(held):
        return (dot(mixed_all, after(part_branch, *held), 1, 0).astype(bf16),)

    grad_mixed, done = ring_scatter(mixed_block, "tp", [gu_part, output_part, result_part])
    grad_mixed = grad_mixed.astype(bf16)
    (grad_gu_part,), (grad_output_part,), (cells, grad_unpatch, rows_second_gate) = done

    def cells_out(*parts):
        around = jnp.concatenate(
            [
                spread_cells(
                    jnp.pad(part.reshape(tile_rows, span, patch), ((2, 2), (2, 2), (0, 0))),
                    tile_rows + 2,
                    span + 2,
                    channels,
                )
                for part in parts
            ],
            axis=-1,
        )
        inside = around[:, 1 : span + 1]
        if sub_n > 1:
            from_left = shift(around[:, span + 1 :].astype(bf16), "sub", True).astype(f32)
            from_right = shift(around[:, :1].astype(bf16), "sub", False).astype(f32)
            inside = (
                inside
                + jnp.pad(from_left, ((0, 0), (0, span - 1), (0, 0)))
                + jnp.pad(from_right, ((0, 0), (span - 1, 0), (0, 0)))
            )
        from_above = shift(inside[tile_rows + 1 :].astype(bf16), "row", True).astype(f32)
        from_below = shift(inside[:1].astype(bf16), "row", False).astype(f32)
        inside = (
            inside[1 : tile_rows + 1]
            + jnp.pad(from_above, ((0, tile_rows - 1), (0, 0), (0, 0)))
            + jnp.pad(from_below, ((tile_rows - 1, 0), (0, 0), (0, 0)))
        )
        inside = (
            inside.astype(bf16)
            .reshape(tile_rows, tp_n, tile_cols, -1)
            .transpose(1, 0, 2, 3)
            .reshape(tp_n, -1, 128)
        )
        rows = -(-inside.shape[1] // owned) * owned
        inside = jnp.pad(inside, ((0, 0), (0, rows - inside.shape[1]), (0, 0)))
        return inside.reshape(tp_n, rows // owned, owned, 128).transpose(0, 2, 1, 3).reshape(
            tp_n, owned, -1
        )

    def cells_in(got):
        inside = jnp.sum(got.astype(f32), axis=0).reshape(owned, -1, 128).transpose(1, 0, 2)
        inside = inside.reshape(-1, 128)[: own * 2 * channels // 128]
        return inside.reshape(tile_rows, tile_cols, 2 * channels).astype(bf16)

    def to_chunks(partial):
        summed = lax.psum_scatter(partial.astype(bf16), "row", scatter_dimension=0, tiled=True)
        if sub_n > 1:
            summed = lax.psum_scatter(summed, "sub", scatter_dimension=0, tiled=True)
        return summed

    def scatter_rows(partial):
        if sub_n > 1:
            return to_chunks(partial)
        return row_scatter(partial).astype(bf16)

    def bands(rows):
        return dot(tile_onehot, rows, 0, 0, HIGH)

    first_cells = cells
    grad_gu_sum = to_chunks(grad_gu_part)
    grad_cross, grad_cap_keys, grad_cap_values, grad_gate_part = pl.pallas_call(
        functools.partial(cross_back_kernel, heads),
        grid=(blocks,),
        in_specs=[
            by_block(head_width),
            whole(head_width, text),
            whole(head_width, text),
            whole(head_width, 1),
            by_block(head_width),
            by_block(head_width),
            by_block(8),
        ],
        out_specs=[
            by_block(head_width),
            whole(head_width, text),
            whole(head_width, text),
            whole(head_width, 128),
        ],
        out_shape=[
            jax.ShapeDtypeStruct((head_width, tokens), bf16),
            jax.ShapeDtypeStruct((head_width, text), f32),
            jax.ShapeDtypeStruct((head_width, text), f32),
            jax.ShapeDtypeStruct((head_width, 128), f32),
        ],
        compiler_params=vmem,
        name="cross_back",
        cost_estimate=cost(7),
    )(raw_cross, caption_keys, caption_values, gate_column, grad_mixed, crossed, stats)

    grad_queries, grad_both = pl.pallas_call(
        functools.partial(attend_back_kernel, heads, key_rows, key_width),
        grid_spec=pltpu.PrefetchScalarGridSpec(
            num_scalar_prefetch=3,
            grid=(blocks,),
            in_specs=[
                by_block(1),
                by_block(head_width),
                whole(2 * head_width, edge),
                whole(2 * head_width, middle_cols),
                whole(2 * head_width, edge),
                by_block(head_width),
                by_block(head_width),
                by_block(8),
            ],
            out_specs=[by_block(head_width), whole(2 * head_width, near)],
            scratch_shapes=[
                pltpu.VMEM((8, LANES), f32),
                pltpu.VMEM((2 * head_width, near), bf16),
            ],
        ),
        out_shape=[
            jax.ShapeDtypeStruct((head_width, tokens), f32),
            jax.ShapeDtypeStruct((2 * head_width, near), f32),
        ],
        compiler_params=vmem,
        name="attend_back",
        cost_estimate=cost(14),
    )(chunk_items, low, high, item_query, queries, above, both, below, grad_mixed, self_out, stats)

    moves = []
    for source in range(all_n):
        source_row, rest = divmod(source, col_n)
        moves.append((source, rest * rows_n + source_row))
    output_sum = to_chunks(grad_output_part)
    got_gu = swap(
        jnp.concatenate(
            [
                after(grad_gu_sum, grad_mixed).reshape(tp_n, owned, -1),
                output_sum.reshape(tp_n, owned, model),
            ],
            axis=2,
        ),
        "tp",
    )
    grad_output = jnp.sum(got_gu[:, :, 2 * ff_mine :].astype(f32), axis=0)
    grad_down_part = dot(hidden, after(grad_feed, grad_queries), 0, 0).astype(bf16)
    grad_down = (
        grad_down_part.reshape(sub_n, rows_n, ff // all_n, model)
        .transpose(1, 0, 2, 3)
        .reshape(-1, model)
    )
    copies = []
    for t in range(tp_n):
        for i in range(2):
            for s in range(sub_n):
                copies.append(
                    (0, t, i * ff_mine + s * ff_part, 1 + i, None, (s * tp_n + t) * ff_part, ff_part)
                )
    grad_gate_weight, grad_up_weight = pack(
        copies, [jax.ShapeDtypeStruct((owned, ff), f32)] * 2, got_gu
    )

    grad_down_sum = to_chunks(grad_down)

    def in_lanes(rows, lanes):
        return rows.reshape(rows.shape[0], -1, lanes).transpose(1, 0, 2).reshape(-1, lanes)

    def from_lanes(rows, count):
        return rows.reshape(-1, count, rows.shape[-1]).transpose(1, 0, 2).reshape(count, -1)

    upper = grad_both[:, :edge].astype(bf16)
    lower = grad_both[:, near - edge :].astype(bf16)
    middle = grad_both[:, edge : near - edge]
    from_above = shift(lower, "row", True).astype(f32)
    from_below = shift(upper, "row", False).astype(f32)
    side = middle.shape[1] - edge
    middle = (
        middle
        + jnp.pad(from_above, ((0, 0), (0, side)))
        + jnp.pad(from_below, ((0, 0), (side, 0)))
    )
    if sub_n > 1:
        middle = (
            middle.astype(bf16)
            .reshape(2 * head_width, tile_rows, sub_n, span)
            .transpose(2, 0, 1, 3)
            .reshape(sub_n, 2 * head_width, tokens)
        )
        middle = jnp.sum(swap(middle, "sub").astype(f32), axis=0)
    grad_keys, grad_values = middle[:head_width], middle[head_width:]

    grad_raw, cells, grad_embedding, rows_first_scale, sums, head_sums = pl.pallas_call(
        functools.partial(finish_kernel, heads, span),
        grid=(blocks,),
        in_specs=[
            by_block(head_width),
            by_block(head_width),
            by_block(head_width),
            by_block(head_width),
            by_block(2 * head_width),
            by_block(HD),
            whole(head_width, 2),
            by_rows(model),
            by_rows(model),
            by_rows(patch),
            whole(*vectors.shape),
            whole(*first_mods.shape),
            whole(model, 4 * head_width),
            whole(model, patch),
        ],
        out_specs=[
            by_rows(4 * head_width),
            by_rows(patch),
            whole(patch, model),
            whole(tile_rows, model),
            whole(8, model),
            whole(head_width, 128),
        ],
        out_shape=[
            struct((tokens, 4 * head_width), bf16),
            struct((tokens, patch)),
            struct((patch, model)),
            struct((tile_rows, model)),
            struct((8, model)),
            struct((head_width, 128)),
        ],
        scratch_shapes=[
            pltpu.VMEM((4 * head_width, LANES), f32),
            pltpu.VMEM((LANES, model), f32),
            pltpu.VMEM((LANES, model), bf16),
        ],
        compiler_params=vmem,
        name="finish",
        cost_estimate=cost(13),
    )(
        grad_queries,
        grad_keys,
        grad_values,
        grad_cross,
        raw,
        tables,
        gains,
        embedded,
        part_residual,
        neighbours,
        vectors,
        first_mods,
        weight_qkvc,
        embedding_t,
    )

    grad_qkvc = dot(normed, grad_raw, 0, 0).astype(bf16)

    def in_lanes(rows, lanes):
        return rows.reshape(rows.shape[0], -1, lanes).transpose(1, 0, 2).reshape(-1, lanes)

    def from_lanes(rows, count):
        return rows.reshape(-1, count, rows.shape[-1]).transpose(1, 0, 2).reshape(count, -1)

    grad_cap = row_scatter(
        after(jnp.concatenate([grad_cap_keys, grad_cap_values], axis=0), grad_qkvc)
    ).astype(bf16)
    if sub_n > 1:
        grad_cap = lax.psum_scatter(grad_cap, "sub", scatter_dimension=0, tiled=True)
    cap_rows = 2 * head_width // (rows_n * sub_n)
    grad_cap = lax.all_gather(grad_cap, ALL, axis=0)
    grad_cap = (
        grad_cap.reshape(rows_n, sub_n, tp_n, cap_rows, text)
        .transpose(2, 0, 1, 3, 4)
        .reshape(tp_n, 2, head_width, text)
        .transpose(1, 0, 2, 3)
        .reshape(2 * model, text)
    )


    def place(vectors):
        return lax.dynamic_update_slice_in_dim(
            jnp.zeros((vectors.shape[0], model), f32), vectors, tp * head_width, 1
        )

    head_vectors = jnp.concatenate(
        [head_sums[:, 0:2], grad_gate_part[:, 0:1], jnp.zeros((head_width, 5), f32)], axis=1
    )
    small = jnp.concatenate(
        [
            grad_embedding,
            grad_unpatch,
            sums,
            grad_ff_gain,
            place(head_vectors.T),
        ],
        axis=0,
    ).astype(bf16)
    small_width = small.shape[0]
    small = small.reshape(small_width, rows_n, model // rows_n).transpose(1, 0, 2)
    small = small.reshape(rows_n * small_width, model // rows_n)
    small, all_mods = row_sums(
        small,
        in_lanes(
            jnp.concatenate(
                [
                    bands(after(rows_first_scale, grad_qkvc, got_gu)),
                    bands(rows_first_gate),
                    bands(rows_second_scale),
                    bands(rows_second_gate),
                ],
                axis=0,
            ),
            model // rows_n,
        ),
    )
    all_mods = spread_all(after(all_mods, grad_down_sum).astype(bf16), COL)
    all_mods = from_lanes(jnp.sum(all_mods.astype(f32), axis=0), 4 * NBAND)
    small = small.astype(bf16).T
    if sub_n > 1:
        small = lax.psum_scatter(small, "sub", scatter_dimension=0, tiled=True)
    small = small.reshape(tp_n, owned, small_width)
    qkvc_width = 4 * head_width
    sent = scatter_rows(grad_qkvc).reshape(tp_n, owned, qkvc_width)
    sent = jnp.concatenate([sent, small, cells_out(first_cells, cells)], axis=2)
    got = swap(after(sent, all_mods), "tp")
    small = jnp.sum(got[:, :, qkvc_width : qkvc_width + small_width].astype(f32), axis=0)
    cells_at = qkvc_width + small_width
    both_cells = cells_in(got[:, :, cells_at:])
    prediction, latent_grad = both_cells[..., :channels], both_cells[..., channels:]
    copies = []
    for t in range(tp_n):
        for i in range(3):
            copies.append((0, t, i * head_width, 1, None, i * model + t * head_width, head_width))
        copies.append((0, t, 3 * head_width, 2, None, t * head_width, head_width))
    grad_projection, grad_cross_query = pack(
        copies,
        [
            jax.ShapeDtypeStruct((owned, 3 * model), f32),
            jax.ShapeDtypeStruct((owned, model), f32),
        ],
        got,
    )
    at = 2 * patch
    grad_embedding = small[:, :patch].T
    grad_unpatch = small[:, patch : 2 * patch]
    vectors = small[:, at:].T

    cap_own = captions.shape[1] // all_n
    own_captions = after(
        lax.dynamic_slice_in_dim(captions, index * cap_own, cap_own, 1), all_mods
    )
    grad_caption = dot(own_captions, grad_cap, 0, 1)

    grad_down = lax.ppermute(grad_down_sum, ALL, moves).astype(f32)
    own_band = lax.dynamic_slice_in_dim(full_band, index * owned, owned, 1)
    own_silu = jax.nn.silu(own_band)
    grad_adaptive = jnp.concatenate(
        [dot(own_silu, all_mods[i * NBAND : (i + 1) * NBAND], 0, 0, HIGH) for i in range(4)], axis=1
    )
    bias_own = 4 * owned
    totals = jnp.sum(all_mods.reshape(4, NBAND, model), axis=1).reshape(-1)
    grad_adaptive_bias = lax.dynamic_slice_in_dim(totals, index * bias_own, bias_own, 0)
    local_rows = my_quarter(adaptive)
    local_band = lax.dynamic_slice_in_dim(band_table, row * quarter, quarter, 1).astype(f32)
    grad_band = sum(
        dot(
            all_mods[i * NBAND : (i + 1) * NBAND],
            local_rows[:, i * model : (i + 1) * model].astype(f32),
            1,
            1,
            HIGH,
        )
        for i in range(4)
    ) * silu_slope(local_band)
    grad_band = lax.ppermute(grad_band, ALL, moves)

    return (
        prediction,
        latent_grad,
        grad_embedding,
        vectors[1],
        grad_band,
        grad_adaptive,
        grad_adaptive_bias,
        vectors[0],
        grad_projection,
        vectors[16],
        vectors[17],
        grad_cross_query,
        grad_caption,
        vectors[18],
        grad_output,
        vectors[8],
        grad_gate_weight,
        grad_up_weight,
        grad_down,
        grad_unpatch,
    )


def _mine(vector, tp, sub_n):
    if sub_n == 1:
        return vector
    size = vector.shape[0] * sub_n
    whole = lax.all_gather(vector, COL, axis=0, tiled=True)
    return lax.dynamic_slice_in_dim(whole, tp * size, size, 0)


def solution(mesh):
    rows_n, col_n = mesh.shape["row"], mesh.shape["col"]

    def run(*args):
        heads = args[5].shape[0] // HD
        tp_n = math.gcd(heads, col_n)
        split = Mesh(mesh.devices.reshape(rows_n, col_n // tp_n, tp_n), ALL)
        in_specs = (
            P("row", COL, None),
            P(),
            P(),
            P(),
            P(None, COL),
            P(COL),
            P(None, COL),
            P(COL, None),
            P(COL),
            P(COL),
            P(COL, None),
            P(COL),
            P(COL),
            P(COL, None),
            P(COL, None),
            P(COL),
            P(COL, None),
            P(COL),
            P(COL, None),
            P(COL, None),
            P(COL, None),
            P(COL, None),
            P("row", COL, None),
        )
        out_specs = (
            P("row", COL, None),
            P("row", COL, None),
            P(None, ALL),
            P(ALL),
            P(None, ALL),
            P(ALL, None),
            P(ALL),
            P(ALL),
            P(ALL, None),
            P(ALL),
            P(ALL),
            P(ALL, None),
            P(ALL, None),
            P(ALL),
            P(ALL, None),
            P(ALL),
            P(ALL, None),
            P(ALL, None),
            P(ALL, None),
            P(ALL, None),
        )
        return jax.shard_map(
            on_device, mesh=split, in_specs=in_specs, out_specs=out_specs, check_vma=False
        )(*args)

    return run
```

time: 863 us -> 568 us (0.66)
  waiting for transfers between devices: 331 us -> 99.1 us
  local copies, waits for them, and re-layouts: 173 us -> 95.6 us
  Pallas kernels: 38 us -> 110 us
  blocking collectives: 46.6 us -> 0 us
  matrix products: 94.3 us -> 48.5 us
  between operations: 16.9 us -> 40.6 us
    reduce_scatter x6 -> x3, waiting for transfers between devices: 162 us -> 0.02 us  [to_chunks(): lax.psum_scatter(partial.astype(bf16), 'row', scatter_dimension=0, tiled=...]
    all_to_all x6 -> x1, waiting for transfers between devices: 82.5 us -> 4.66 us  [spread_all(): lax.all_to_all(jnp.broadcast_to(value[None], (count,) + value.shape), axe...]
    pallas_call x1 -> x9, Pallas kernels: 16.1 us -> 87.1 us  [the longest x1 34.7 us: on_device(): pl.pallas_call(functools.partial(middle_kernel, len(pieces), span), grid_...]
    all_to_all x2 -> x0, blocking collectives: 46.6 us -> none  [swap(): return lax.all_to_all(value, axes, 0, 0, tiled=True)]
    ppermute x1 -> x27, waiting for transfers between devices: 0.01 us -> 41.2 us  [the longest x8 24.4 us: onward(): lax.ppermute(value, axis, [(ring[i], ring[(i + 1) % count]) for i in rang...]
    dot_general x23 -> x17, matrix products: 80.3 us -> 42.3 us  [dot(): lax.dot_general(left, right, (((left_dim,), (right_dim,)), ((), ())), pre...]
    ppermute x1 -> x27, starting transfers between devices: 4.48 us -> 33.7 us  [the longest x10 11.7 us: pairwise(): return lax.ppermute(value, 'row', [(i, i ^ flip) for i in range(4)])]
    all_gather x6 -> x4, waiting for transfers between devices: 49.2 us -> 21.5 us  [the longest x1 21.4 us: on_device(): output_piece = lax.all_gather(output_piece, COL, axis=0, tiled=True)]
  transfers between devices with their start and end apart: 38 -> 49, of which waited for: 17 -> 18; matrix products, arithmetic and copies ran while one was open for 29% -> 32% of each run, Pallas kernels for 4% -> 13%
where the time goes in v2:
time: 568 us; the launch traced here: 557 us
  Pallas kernels  110 us (19%)
  starting transfers between devices  100 us (18%)
  waiting for transfers between devices  99.1 us (17%)
  local copies, waits for them, and re-layouts  95.6 us (17%)
  other arithmetic  64 us (11%)
  matrix products  48.5 us (9%)
  between operations  40.6 us (7%)
    all_to_all x5, starting transfers between devices, swap(): return lax.all_to_all(value, axes, 0, 0, tiled=True)  47.1 us
    dot_general x17, matrix products, dot(): lax.dot_general(left, right, (((left_dim,), (right_dim,)), ((), ())), pre...  42.3 us
    pallas_call x1, Pallas kernels, on_device(): pl.pallas_call(functools.partial(middle_kernel, len(pieces), span), grid_...  34.7 us
    all_to_all x5, waiting for transfers between devices, swap(): return lax.all_to_all(value, axes, 0, 0, tiled=True)  31.7 us
    ppermute x8, waiting for transfers between devices, onward(): lax.ppermute(value, axis, [(ring[i], ring[(i + 1) % count]) for i in rang...  24.4 us
    all_gather x1, waiting for transfers between devices, on_device(): output_piece = lax.all_gather(output_piece, COL, axis=0, tiled=True)  21.4 us
    slice x21, local copies, waits for them, and re-layouts, nothing(): return sum((other[(0,) * other.ndim].astype(f32) * 0.0 for other in others))  19 us
    pallas_call x1, Pallas kernels, on_device(): pl.pallas_call(waits_for(functools.partial(attend_kernel, heads, key_rows...  15.4 us
  transfers between devices with their start and end apart: 49, of which 18 were waited for; matrix products, arithmetic and copies ran while one was open for 32% of the time, Pallas kernels for 13%

profile of v2, /device:TPU:0, one launch (start us, length us, event | category | flops | bytes accessed | tf_op | source)
XLA Modules:
  0.0 557.5 jit_solution(15942951833699645618)
XLA Ops:
  13.2 7.3 %all-to-all-start = ((bf16[8,48,896]{2,1,0:T(8,128)(2,1)}), bf16[8,48,896]{2,1,0:T(8,128)(2,1)}, u32[]{:S(2)}, u32[]{:S(2)}) async-start(bf16[8,48,896]{2,1,0:T(8,128)(2,1)} %pad_maximum_fusion.4), calls=%async_computation | async-start | bytes 1376256 | tf_op jit(solution)/shard_map/all_to_all | solution.py:37
  25.7 2.7 broadcast_select_fusion
  32.5 2.4 reshape.336
  37.2 3.0 all-to-all-done
  46.1 4.4 all-to-all-start.1
  50.7 2.7 collective-permute-done.2
  54.7 21.4 %all-gather.8.cloned.1.call-done = bf16[1536,384]{1,0:T(8,128)(2,1)} async-done(((bf16[192,384]{1,0:T(8,128)(2,1)}), bf16[1536,384]{1,0:T(8,128)(2,1)}) %all-gather.8.cloned.1.call-update) | async-done | bytes 1179664 | tf_op jit(solution)/shard_map/all_gather | solution.py:976
  80.0 2.4 collective-permute-start
  90.3 3.8 concatenate.100
  95.3 4.1 concatenate.107
  108.6 3.1 collective-permute-start.6
  114.7 10.0 %project.1 = (f32[1024,1536]{1,0:T(8,128)}, bf16[1024,1536]{1,0:T(8,128)(2,1)}, bf16[384,1024]{1,0:T(8,128)(2,1)}, bf16[192,1024]{1,0:T(8,128)(2,1)}, bf16[384,1...) custom-call(bf16[1024,144]{1,0:T(8,128)(2,1)} %bitcast.272, bf16[1536,144]{1,0:T(8,128)(2,1)} %bitcast.233, ...), custom_call_target="tpu_custom_call" | custom-call | flops 10000000000 | bytes 30000000 | tf_op jit(solution)/shard_map/project/pallas_call | solution.py:1020
  126.1 2.3 collective-permute-start.4
  132.7 7.5 %all-to-all-start.2 = ((bf16[8,240,256]{2,1,0:T(8,128)(2,1)}), bf16[8,240,256]{2,1,0:T(8,128)(2,1)S(1)}, u32[]{:S(2)}, u32[]{:S(2)}) async-start(bf16[8,240,256]{2,1,0:T(8,128)(2,1)} %maximum_add_fusion.1), calls=%async_computation.2 | async-start | bytes 1966080 | tf_op jit(solution)/shard_map/all_to_all | solution.py:37
  143.5 15.4 %attend.1 = (bf16[192,1024]{1,0:T(8,128)(2,1)}, f32[192,1024]{1,0:T(8,128)}, f32[192,1024]{1,0:T(8,128)}, f32[8,1024]{1,0:T(8,128)}) custom-call(s32[32]{0:T(128)} %copy-done.51, s32[4]{0:T(128)} %get-tuple-element.319.refs_1_.low_ref, s32[4]{0:T(128)} %get-tuple-element.318.refs_2_.high_ref, s32[1,1024]{1,0:T(1,128)} %broadcast_in_dim_reshape.3.refs_3_.item_query_ref, ...), custom_call_target="tpu_custom_call" | custom-call | flops 14000000000 | bytes 42000000 | tf_op jit(solution)/shard_map/attend/pallas_call | solution.py:1114
  162.7 3.4 all-to-all-done.2
  169.3 9.0 %collective-permute-done.8.refs_1_ = bf16[192,1024]{1,0:T(8,128)(2,1)S(1)} collective-permute-done((bf16[192,1024]{1,0:T(8,128)(2,1)S(1)}, bf16[192,1024]{1,0:T(8,128)(2,1)S(1)}, u32[]{:S(2)}, u32[]{:S(2)}) %collective-permute-start.8) | collective-permute-done | bytes 393248 | tf_op jit(solution)/shard_map/ppermute | solution.py:136
  180.3 8.2 %collective-permute-done.10.refs_3_ = bf16[192,1024]{1,0:T(8,128)(2,1)S(1)} collective-permute-done((bf16[192,1024]{1,0:T(8,128)(2,1)S(1)}, bf16[192,1024]{1,0:T(8,128)(2,1)S(1)}, u32[]{:S(2)}, u32[]{:S(2)}) %collective-permute-start.10) | collective-permute-done | bytes 393248 | tf_op jit(solution)/shard_map/ppermute | solution.py:136
  206.0 3.9 slice.631
  212.0 34.7 %middle.1 = (bf16[1536,1024]{1,0:T(8,128)(2,1)}, f32[1024,1536]{1,0:T(8,128)}, bf16[1024,1536]{1,0:T(8,128)(2,1)}, bf16[1024,512]{1,0:T(8,128)(2,1)}, bf16[1024,...) custom-call(s32[2]{0:T(128)} %pad_add_fusion.1.own_ref.refs_0_, ...), custom_call_target="tpu_custom_call" | custom-call | flops 35000000512 | bytes 105000000 | tf_op jit(solution)/shard_map/middle/pallas_call | solution.py:1182
  246.7 2.1 constant_dynamic-slice_fusion.4
  251.9 2.6 collective-permute-done.16
  258.0 6.5 %convolution_convert_fusion.1 = bf16[1536,1024]{1,0:T(8,128)(2,1)} fusion(bf16[1024,1536]{1,0:T(8,128)(2,1)S(1)} %copy-done.65, bf16[1024,1024]{1,0:T(8,128)(2,1)} %get-tuple-element.69, bf16[]{:T(256)} %bitcast.61), kind=kOutput, calls=%fused_computation.1 | convolution fusion | flops 3223846912 | bytes 8388610 | tf_op jit(solution)/shard_map/dot_general | solution.py:213
  265.8 4.7 collective-permute-done.19
  277.9 2.5 collective-permute-done.20
  280.4 2.8 collective-permute-done.17
  284.0 2.4 fusion.102
  288.7 8.6 %convolution_convert_fusion = bf16[1536,1536]{1,0:T(8,128)(2,1)} fusion(bf16[1536,1024]{1,0:T(8,128)(2,1)S(1)} %copy-done.66, bf16[1024,1536]{1,0:T(8,128)(2,1)} %get-tuple-element.71, bf16[]{:T(256)} %bitcast.63), kind=kOutput, calls=%fused_computation | convolution fusion | flops 4835770368 | bytes 11010050 | tf_op jit(solution)/shard_map/dot_general | solution.py:213
  312.0 10.6 %result.1 = (f32[1024,144]{1,0:T(8,128)}, f32[144,1536]{1,0:T(8,128)}, f32[16,1536]{1,0:T(8,128)}) custom-call(s32[2]{0:T(128)} %pad_add_fusion.1.own_ref.refs_0_, bf16[1024,512]{1,0:T(8,128)(2,1)} %get-tuple-element.72.refs_1_, f32[1024,1536]{1,0:T(8,128)} %get-tuple-element.73.refs_2_, bf16[1024,144]{1,0:T(8,128)(2,1)} %bitcast.276, ...), custom_call_target="tpu_custom_call" | custom-call | flops 8999999488 | bytes 27000000 | tf_op jit(solution)/shard_map/result/pallas_call | solution.py:1246
  323.7 2.2 convert.78
  333.0 15.4 %attend_back.1 = (f32[192,1024]{1,0:T(8,128)}, f32[384,2048]{1,0:T(8,128)}) custom-call(s32[32]{0:T(128)} %copy-done.51, s32[4]{0:T(128)} %get-tuple-element.319.refs_1_.low_ref, s32[4]{0:T(128)} %get-tuple-element.318.refs_2_.high_ref, s32[1,1024]{1,0:T(1,128)} %broadcast_in_dim_reshape.3.refs_3_.item_query_ref, ...), custom_call_target="tpu_custom_call" | custom-call | flops 14000000000 | bytes 42000000 | tf_op jit(solution)/shard_map/attend_back/pallas_call | solution.py:1380
  348.4 2.1 convert.76
  356.6 7.2 %cross_back.1 = (bf16[192,1024]{1,0:T(8,128)(2,1)}, f32[192,256]{1,0:T(8,128)}, f32[192,256]{1,0:T(8,128)}, f32[192,128]{1,0:T(8,128)}) custom-call(bf16[192,1024]{1,0:T(8,128)(2,1)} %get-tuple-element.64.refs_8_.cross_ref, bf16[192,256]{1,0:T(8,128)(2,1)} %get-tuple-element.303.refs_9_.caption_key_ref, ...), custom_call_target="tpu_custom_call" | custom-call | flops 7000000000 | bytes 21000000 | tf_op jit(solution)/shard_map/cross_back/pallas_call | solution.py:1351
  365.4 5.4 fusion.3
  374.6 2.7 pad_maximum_fusion.1
  377.3 5.9 %all-to-all-start.3 = ((bf16[8,48,2560]{2,1,0:T(8,128)(2,1)}), bf16[8,48,2560]{2,1,0:T(8,128)(2,1)S(1)}, u32[]{:S(2)}, u32[]{:S(2)}) async-start(bf16[8,48,2560]{2,1,0:T(8,128)(2,1)} %pad_maximum_fusion.1), calls=%async_computation.5 | async-start | bytes 3932160 | tf_op jit(solution)/shard_map/all_to_all | solution.py:37
  383.5 13.6 %finish.1 = (bf16[1024,768]{1,0:T(8,128)(2,1)}, f32[1024,144]{1,0:T(8,128)}, f32[144,1536]{1,0:T(8,128)}, f32[16,1536]{1,0:T(8,128)}, f32[8,1536]{1,0:T(8,128)}, /*index=5*/f32[192,128]{1,0:T(8,128)}) custom-call(f32[192,1024]{1,0:T(8,128)} %get-tuple-element.79.grad_query_ref, f32[192,1024]{1,0:T(8,128)} %get-tuple-element.263.grad_key_ref, ...), custom_call_target="tpu_custom_call" | custom-call | flops 12999999488 | bytes 39000000 | tf_op jit(solution)/shard_map/finish/pallas_call | solution.py:1472
  397.2 4.5 convolution_convert_fusion.2
  415.0 15.3 %all-to-all-done.3.refs_0_ = bf16[8,48,2560]{2,1,0:T(8,128)(2,1)S(1)} async-done(((bf16[8,48,2560]{2,1,0:T(8,128)(2,1)}), bf16[8,48,2560]{2,1,0:T(8,128)(2,1)S(1)}, u32[]{:S(2)}, u32[]{:S(2)}) %all-to-all-start.3) | async-done | bytes 1966112 | tf_op jit(solution)/shard_map/all_to_all | solution.py:37
  434.8 2.4 dynamic-slice_bitcast_fusion.1
  447.0 2.6 fusion.6
  451.4 3.4 collective-permute-done.29
  457.0 4.2 all-to-all-start.4
  470.7 4.6 collective-permute-start.35
  488.7 4.7 all-to-all-done.4
  496.9 22.0 %all-to-all-start.5 = ((bf16[8,48,1208]{2,1,0:T(8,128)(2,1)}), bf16[8,48,1208]{2,1,0:T(8,128)(2,1)S(1)}, u32[]{:S(2)}, u32[]{:S(2)}) async-start(bf16[8,48,1208]{2,1,0:T(8,128)(2,1)} %broadcast_add_fusion), calls=%async_computation.8 | async-start | bytes 1966080 | tf_op jit(solution)/shard_map/all_to_all | solution.py:37
  530.0 2.6 fusion.60
  534.3 10.0 %all-to-all-done.5.refs_0_ = bf16[8,48,1208]{2,1,0:T(8,128)(2,1)S(1)} async-done(((bf16[8,48,1208]{2,1,0:T(8,128)(2,1)}), bf16[8,48,1208]{2,1,0:T(8,128)(2,1)S(1)}, u32[]{:S(2)}, u32[]{:S(2)}) %all-to-all-start.5) | async-done | bytes 927776 | tf_op jit(solution)/shard_map/all_to_all | solution.py:37
  (462 shorter events, 191.6 us)
Async XLA Ops:
  13.2 27.0 %all-to-all-start = ((bf16[8,48,896]{2,1,0:T(8,128)(2,1)}), bf16[8,48,896]{2,1,0:T(8,128)(2,1)}, u32[]{:S(2)}, u32[]{:S(2)}) async-start(bf16[8,48,896]{2,1,0:T(8,128)(2,1)} %pad_maximum_fusion.4), calls=%async_computation | async-start | bytes 1376256 | tf_op jit(solution)/shard_map/all_to_all | solution.py:37
  20.5 55.6 %all-gather.8.cloned.1.call-start = ((), (), s32[]{:S(2)}) async-start(), calls=%async_computation.9 | async-start | bytes 1327104 | tf_op jit(solution)/shard_map/all_gather | solution.py:976
  41.4 12.1 %collective-permute-start.2 = (bf16[8,48,768]{2,1,0:T(8,128)(2,1)S(1)}, bf16[8,48,768]{2,1,0:T(8,128)(2,1)S(1)}, u32[]{:S(2)}, u32[]{:S(2)}) collective-permute-start(bf16[8,48,768]{2,1,0:T(8,128)(2,1)S(1)} %slice.612), channel_id=1, source_target_pairs={{0,16},{8,24},{16,0},{24,8},{1,17},{9,25},{17,1},{25,9},{2,18},{10... | collective-permute-start | bytes 1769480 | tf_op jit(solution)/shard_map/ppermute | solution.py:65
  46.1 58.7 %all-to-all-start.1 = ((bf16[8,48,1792]{2,1,0:T(8,128)(2,1)}), bf16[8,48,1792]{2,1,0:T(8,128)(2,1)}, u32[]{:S(2)}, u32[]{:S(2)}) async-start(bf16[8,48,1792]{2,1,0:T(8,128)(2,1)} %maximum_add_fusion), calls=%async_computation.1 | async-start | bytes 2752512 | tf_op jit(solution)/shard_map/all_to_all | solution.py:37
  50.6 110.3 %all-gather.10.cloned.1.call-start = ((), (), s32[]{:S(2)}) async-start(), calls=%async_computation.13 | async-start | bytes 5898240 | tf_op jit(solution)/shard_map/all_gather | solution.py:977
  77.2 22.2 %collective-permute-start.3 = (bf16[2,8,48,768]{3,2,1,0:T(8,128)(2,1)}, bf16[2,8,48,768]{3,2,1,0:T(8,128)(2,1)}, u32[]{:S(2)}, u32[]{:S(2)}) collective-permute-start(bf16[2,8,48,768]{3,2,1,0:T(8,128)(2,1)} %pad_maximum_fusion.2), channel_id=1, source_target_pairs={{0,8},{8,0},{16,24},{24,16},{1,9},{9,1},{17,25},{25,17},{2,10},{10... | collective-permute-start | bytes 3538952 | tf_op jit(solution)/shard_map/ppermute | solution.py:65
  80.0 8.0 %collective-permute-start = (bf16[1,64,32]{2,1,0:T(8,128)(2,1)S(1)}, bf16[1,64,32]{2,1,0:T(8,128)(2,1)S(1)}, u32[]{:S(2)}, u32[]{:S(2)}) collective-permute-start(bf16[1,64,32]{2,1,0:T(8,128)(2,1)S(1)} %get-tuple-element.294), channel_id=1, source_target_pairs={{0,8},{8,16},{16,24},{1,9},{9,17},{17,25},{2,10},{10,18},{18,26},{... | collective-permute-start | bytes 12296 | tf_op jit(solution)/shard_map/ppermute | solution.py:225
  82.4 5.6 %collective-permute-start.1 = (bf16[1,64,32]{2,1,0:T(8,128)(2,1)S(1)}, bf16[1,64,32]{2,1,0:T(8,128)(2,1)S(1)}, u32[]{:S(2)}, u32[]{:S(2)}) collective-permute-start(bf16[1,64,32]{2,1,0:T(8,128)(2,1)S(1)} %get-tuple-element.295), channel_id=1, source_target_pairs={{8,0},{16,8},{24,16},{9,1},{17,9},{25,17},{10,2},{18,10},{26,18},{... | collective-permute-start | bytes 12296 | tf_op jit(solution)/shard_map/ppermute | solution.py:225
  108.6 16.2 %collective-permute-start.6 = (bf16[48,768]{1,0:T(8,128)(2,1)S(1)}, bf16[48,768]{1,0:T(8,128)(2,1)S(1)}, u32[]{:S(2)}, u32[]{:S(2)}) collective-permute-start(bf16[48,768]{1,0:T(8,128)(2,1)S(1)} %pad_maximum_fusion.17), channel_id=1, source_target_pairs={{0,16},{8,24},{16,0},{24,8},{1,17},{9,25},{17,1},{25,9},{2,18},{10... | collective-permute-start | bytes 221192 | tf_op jit(solution)/shard_map/ppermute | solution.py:65
  124.8 15.5 %collective-permute-start.7 = (bf16[2,48,768]{2,1,0:T(8,128)(2,1)S(1)}, bf16[2,48,768]{2,1,0:T(8,128)(2,1)S(1)}, u32[]{:S(2)}, u32[]{:S(2)}) collective-permute-start(bf16[2,48,768]{2,1,0:T(8,128)(2,1)S(1)} %pad_maximum_fusion.14), channel_id=1, source_target_pairs={{0,8},{8,0},{16,24},{24,16},{1,9},{9,1},{17,25},{25,17},{2,10},{10... | collective-permute-start | bytes 442376 | tf_op jit(solution)/shard_map/ppermute | solution.py:65
  126.1 16.6 %collective-permute-start.4 = (bf16[384,512]{1,0:T(8,128)(2,1)S(1)}, bf16[384,512]{1,0:T(8,128)(2,1)S(1)}, u32[]{:S(2)}, u32[]{:S(2)}) collective-permute-start(bf16[384,512]{1,0:T(8,128)(2,1)S(1)} %get-tuple-element.269), channel_id=1, source_target_pairs={{0,8},{8,16},{16,24},{1,9},{9,17},{17,25},{2,10},{10,18},{18,26},{... | collective-permute-start | bytes 1179656 | tf_op jit(solution)/shard_map/ppermute | solution.py:225
  128.5 14.3 %collective-permute-start.5 = (bf16[384,512]{1,0:T(8,128)(2,1)S(1)}, bf16[384,512]{1,0:T(8,128)(2,1)}, u32[]{:S(2)}, u32[]{:S(2)}) collective-permute-start(bf16[384,512]{1,0:T(8,128)(2,1)S(1)} %get-tuple-element.268), channel_id=1, source_target_pairs={{8,0},{16,8},{24,16},{9,1},{17,9},{25,17},{10,2},{18,10},{26,18},{... | collective-permute-start | bytes 1179656 | tf_op jit(solution)/shard_map/ppermute | solution.py:225
  132.7 33.4 %all-to-all-start.2 = ((bf16[8,240,256]{2,1,0:T(8,128)(2,1)}), bf16[8,240,256]{2,1,0:T(8,128)(2,1)S(1)}, u32[]{:S(2)}, u32[]{:S(2)}) async-start(bf16[8,240,256]{2,1,0:T(8,128)(2,1)} %maximum_add_fusion.1), calls=%async_computation.2 | async-start | bytes 1966080 | tf_op jit(solution)/shard_map/all_to_all | solution.py:37
  140.2 65.7 %all-gather.12.cloned.1.call-start = ((), (), s32[]{:S(2)}) async-start(), calls=%async_computation.14 | async-start | bytes 4915200 | tf_op jit(solution)/shard_map/all_gather | solution.py:1164
  167.2 206.2 %reduce-scatter.4.cloned.1.call-start = ((), (), s32[]{:S(2)}) async-start(), calls=%async_computation.10 | async-start | bytes 3932160 | tf_op jit(solution)/shard_map/reduce_scatter | solution.py:1336
  167.2 11.1 %collective-permute-start.8 = (bf16[192,1024]{1,0:T(8,128)(2,1)S(1)}, bf16[192,1024]{1,0:T(8,128)(2,1)S(1)}, u32[]{:S(2)}, u32[]{:S(2)}) collective-permute-start(bf16[192,1024]{1,0:T(8,128)(2,1)S(1)} %copy-done.54), channel_id=1, source_target_pairs={{0,2},{2,4},{4,6},{6,7},{7,5},{5,3},{3,1},{1,0},{8,10},{10,12},{12... | collective-permute-start | bytes 1179656 | tf_op jit(solution)/shard_map/ppermute | solution.py:136
  167.3 11.7 %collective-permute-start.9 = (bf16[192,1024]{1,0:T(8,128)(2,1)S(1)}, bf16[192,1024]{1,0:T(8,128)(2,1)S(1)}, u32[]{:S(2)}, u32[]{:S(2)}) collective-permute-start(bf16[192,1024]{1,0:T(8,128)(2,1)S(1)} %copy-done.54), channel_id=1, source_target_pairs={{2,0},{4,2},{6,4},{7,6},{5,7},{3,5},{1,3},{0,1},{10,8},{12,10},{14... | collective-permute-start | bytes 1179656 | tf_op jit(solution)/shard_map/ppermute | solution.py:139
  178.3 10.3 %collective-permute-start.10 = (bf16[192,1024]{1,0:T(8,128)(2,1)S(1)}, bf16[192,1024]{1,0:T(8,128)(2,1)S(1)}, u32[]{:S(2)}, u32[]{:S(2)}) collective-permute-start(bf16[192,1024]{1,0:T(8,128)(2,1)S(1)} %collective-permute-done.8.refs_1_), channel_id=1, source_target_pairs={{0,2},{2,4},{4,6},{6,7},{7,5},{5,3},{3,1},{1,0},{8,10},{10,12},{12... | collective-permute-start | bytes 1179656 | tf_op jit(solution)/shard_map/ppermute | solution.py:136
  179.0 11.0 %collective-permute-start.11 = (bf16[192,1024]{1,0:T(8,128)(2,1)S(1)}, bf16[192,1024]{1,0:T(8,128)(2,1)S(1)}, u32[]{:S(2)}, u32[]{:S(2)}) collective-permute-start(bf16[192,1024]{1,0:T(8,128)(2,1)S(1)} %collective-permute-done.9.refs_2_), channel_id=1, source_target_pairs={{2,0},{4,2},{6,4},{7,6},{5,7},{3,5},{1,3},{0,1},{10,8},{12,10},{14... | collective-permute-start | bytes 1179656 | tf_op jit(solution)/shard_map/ppermute | solution.py:139
  188.6 15.0 %collective-permute-start.12 = (bf16[192,1024]{1,0:T(8,128)(2,1)S(1)}, bf16[192,1024]{1,0:T(8,128)(2,1)S(1)}, u32[]{:S(2)}, u32[]{:S(2)}) collective-permute-start(bf16[192,1024]{1,0:T(8,128)(2,1)S(1)} %collective-permute-done.10.refs_3_), channel_id=1, source_target_pairs={{0,2},{2,4},{4,6},{6,7},{7,5},{5,3},{3,1},{1,0},{8,10},{10,12},{12... | collective-permute-start | bytes 1179656 | tf_op jit(solution)/shard_map/ppermute | solution.py:136
  190.0 15.1 %collective-permute-start.13 = (bf16[192,1024]{1,0:T(8,128)(2,1)S(1)}, bf16[192,1024]{1,0:T(8,128)(2,1)S(1)}, u32[]{:S(2)}, u32[]{:S(2)}) collective-permute-start(bf16[192,1024]{1,0:T(8,128)(2,1)S(1)} %collective-permute-done.11.refs_4_), channel_id=1, source_target_pairs={{2,0},{4,2},{6,4},{7,6},{5,7},{3,5},{1,3},{0,1},{10,8},{12,10},{14... | collective-permute-start | bytes 1179656 | tf_op jit(solution)/shard_map/ppermute | solution.py:139
  203.6 8.4 %collective-permute-start.14 = (bf16[96,1024]{1,0:T(8,128)(2,1)S(1)}, bf16[96,1024]{1,0:T(8,128)(2,1)}, u32[]{:S(2)}, u32[]{:S(2)}) collective-permute-start(bf16[96,1024]{1,0:T(8,128)(2,1)S(1)} %slice.628), channel_id=1, source_target_pairs={{0,2},{2,4},{4,6},{6,7},{7,5},{5,3},{3,1},{1,0},{8,10},{10,12},{12... | collective-permute-start | bytes 589832 | tf_op jit(solution)/shard_map/ppermute | solution.py:136
  205.1 6.9 %collective-permute-start.15 = (bf16[96,1024]{1,0:T(8,128)(2,1)S(1)}, bf16[96,1024]{1,0:T(8,128)(2,1)}, u32[]{:S(2)}, u32[]{:S(2)}) collective-permute-start(bf16[96,1024]{1,0:T(8,128)(2,1)S(1)} %slice.629), channel_id=1, source_target_pairs={{2,0},{4,2},{6,4},{7,6},{5,7},{3,5},{1,3},{0,1},{10,8},{12,10},{14... | collective-permute-start | bytes 589832 | tf_op jit(solution)/shard_map/ppermute | solution.py:139
  248.8 5.7 %collective-permute-start.16 = (bf16[96,1024]{1,0:T(8,128)(2,1)S(1)}, bf16[96,1024]{1,0:T(8,128)(2,1)S(1)}, u32[]{:S(2)}, u32[]{:S(2)}) collective-permute-start(bf16[96,1024]{1,0:T(8,128)(2,1)S(1)} %get-tuple-element.258), channel_id=1, source_target_pairs={{0,2},{2,4},{4,6},{6,7},{7,5},{5,3},{3,1},{1,0},{8,10},{10,12},{12... | collective-permute-start | bytes 589832 | tf_op jit(solution)/shard_map/ppermute | solution.py:136
  264.5 110.1 %reduce-scatter.6.cloned.1.call-start = ((), (), s32[]{:S(2)}) async-start(), calls=%async_computation.11 | async-start | bytes 5898240 | tf_op jit(solution)/shard_map/reduce_scatter | solution.py:1336
  264.5 5.9 %collective-permute-start.19 = (bf16[96,1024]{1,0:T(8,128)(2,1)}, bf16[96,1024]{1,0:T(8,128)(2,1)S(1)}, u32[]{:S(2)}, u32[]{:S(2)}) collective-permute-start(bf16[96,1024]{1,0:T(8,128)(2,1)} %get-tuple-element.259), channel_id=1, source_target_pairs={{2,0},{4,2},{6,4},{7,6},{5,7},{3,5},{1,3},{0,1},{10,8},{12,10},{14... | collective-permute-start | bytes 589832 | tf_op jit(solution)/shard_map/ppermute | solution.py:139
  272.3 8.1 %collective-permute-start.20 = (bf16[192,1024]{1,0:T(8,128)(2,1)}, bf16[192,1024]{1,0:T(8,128)(2,1)}, u32[]{:S(2)}, u32[]{:S(2)}) collective-permute-start(bf16[192,1024]{1,0:T(8,128)(2,1)} %pad_maximum_fusion.7), channel_id=1, source_target_pairs={{2,0},{4,2},{6,4},{7,6},{5,7},{3,5},{1,3},{0,1},{10,8},{12,10},{14... | collective-permute-start | bytes 1179656 | tf_op jit(solution)/shard_map/ppermute | solution.py:139
  275.2 8.0 %collective-permute-start.17 = (bf16[192,1024]{1,0:T(8,128)(2,1)}, bf16[192,1024]{1,0:T(8,128)(2,1)S(1)}, u32[]{:S(2)}, u32[]{:S(2)}) collective-permute-start(bf16[192,1024]{1,0:T(8,128)(2,1)} %pad_maximum_fusion.6), channel_id=1, source_target_pairs={{0,2},{2,4},{4,6},{6,7},{7,5},{5,3},{3,1},{1,0},{8,10},{10,12},{12... | collective-permute-start | bytes 1179656 | tf_op jit(solution)/shard_map/ppermute | solution.py:136
  297.3 152.3 %reduce-scatter.8.cloned.1.call-start = ((), (), s32[]{:S(2)}) async-start(), calls=%async_computation.12 | async-start | bytes 1966080 | tf_op jit(solution)/shard_map/reduce_scatter | solution.py:1336
  298.9 9.4 %collective-permute-start.18 = (bf16[192,1024]{1,0:T(8,128)(2,1)}, bf16[192,1024]{1,0:T(8,128)(2,1)S(1)}, u32[]{:S(2)}, u32[]{:S(2)}) collective-permute-start(bf16[192,1024]{1,0:T(8,128)(2,1)} %get-tuple-element.244), channel_id=1, source_target_pairs={{0,2},{2,4},{4,6},{6,7},{7,5},{5,3},{3,1},{1,0},{8,10},{10,12},{12... | collective-permute-start | bytes 1179656 | tf_op jit(solution)/shard_map/ppermute | solution.py:136
  299.6 8.8 %collective-permute-start.22 = (bf16[192,1024]{1,0:T(8,128)(2,1)S(1)}, bf16[192,1024]{1,0:T(8,128)(2,1)S(1)}, u32[]{:S(2)}, u32[]{:S(2)}) collective-permute-start(bf16[192,1024]{1,0:T(8,128)(2,1)S(1)} %get-tuple-element.254), channel_id=1, source_target_pairs={{2,0},{4,2},{6,4},{7,6},{5,7},{3,5},{1,3},{0,1},{10,8},{12,10},{14... | collective-permute-start | bytes 1179656 | tf_op jit(solution)/shard_map/ppermute | solution.py:139
  309.9 22.2 %collective-permute-start.21 = (bf16[192,1024]{1,0:T(8,128)(2,1)S(1)}, bf16[192,1024]{1,0:T(8,128)(2,1)S(1)}, u32[]{:S(2)}, u32[]{:S(2)}) collective-permute-start(bf16[192,1024]{1,0:T(8,128)(2,1)S(1)} %get-tuple-element.242), channel_id=1, source_target_pairs={{0,2},{2,4},{4,6},{6,7},{7,5},{5,3},{3,1},{1,0},{8,10},{10,12},{12... | collective-permute-start | bytes 1179656 | tf_op jit(solution)/shard_map/ppermute | solution.py:136
  311.2 20.8 %collective-permute-start.23 = (bf16[192,1024]{1,0:T(8,128)(2,1)S(1)}, bf16[192,1024]{1,0:T(8,128)(2,1)S(1)}, u32[]{:S(2)}, u32[]{:S(2)}) collective-permute-start(bf16[192,1024]{1,0:T(8,128)(2,1)S(1)} %get-tuple-element.252), channel_id=1, source_target_pairs={{2,0},{4,2},{6,4},{7,6},{5,7},{3,5},{1,3},{0,1},{10,8},{12,10},{14... | collective-permute-start | bytes 1179656 | tf_op jit(solution)/shard_map/ppermute | solution.py:139
  351.4 19.4 %collective-permute-start.24 = (bf16[384,512]{1,0:T(8,128)(2,1)}, bf16[384,512]{1,0:T(8,128)(2,1)}, u32[]{:S(2)}, u32[]{:S(2)}) collective-permute-start(bf16[384,512]{1,0:T(8,128)(2,1)} %get-tuple-element.264), channel_id=1, source_target_pairs={{0,8},{8,16},{16,24},{1,9},{9,17},{17,25},{2,10},{10,18},{18,26},{... | collective-permute-start | bytes 1179656 | tf_op jit(solution)/shard_map/ppermute | solution.py:225
  353.4 17.4 %collective-permute-start.25 = (bf16[384,512]{1,0:T(8,128)(2,1)S(1)}, bf16[384,512]{1,0:T(8,128)(2,1)}, u32[]{:S(2)}, u32[]{:S(2)}) collective-permute-start(bf16[384,512]{1,0:T(8,128)(2,1)S(1)} %get-tuple-element.265), channel_id=1, source_target_pairs={{8,0},{16,8},{24,16},{9,1},{17,9},{25,17},{10,2},{18,10},{26,18},{... | collective-permute-start | bytes 1179656 | tf_op jit(solution)/shard_map/ppermute | solution.py:225
  377.3 53.0 %all-to-all-start.3 = ((bf16[8,48,2560]{2,1,0:T(8,128)(2,1)}), bf16[8,48,2560]{2,1,0:T(8,128)(2,1)S(1)}, u32[]{:S(2)}, u32[]{:S(2)}) async-start(bf16[8,48,2560]{2,1,0:T(8,128)(2,1)} %pad_maximum_fusion.1), calls=%async_computation.5 | async-start | bytes 3932160 | tf_op jit(solution)/shard_map/all_to_all | solution.py:37
  383.2 99.1 %all-gather.14.cloned.1.call-start = ((), (), s32[]{:S(2)}) async-start(), calls=%async_computation.15 | async-start | bytes 1622016 | tf_op jit(solution)/shard_map/all_gather | solution.py:1546
  404.3 5.6 collective-permute-start.33
  434.4 6.6 %collective-permute-start.28 = (bf16[752,384]{1,0:T(8,128)(2,1)}, bf16[752,384]{1,0:T(8,128)(2,1)}, u32[]{:S(2)}, u32[]{:S(2)}) collective-permute-start(bf16[752,384]{1,0:T(8,128)(2,1)} %pad_maximum_fusion.5), channel_id=1, source_target_pairs={{0,8},{8,0},{16,24},{24,16},{1,9},{9,1},{17,25},{25,17},{2,10},{10... | collective-permute-start | bytes 1732616 | tf_op jit(solution)/shard_map/ppermute | solution.py:65
  437.2 9.8 %collective-permute-start.26 = (bf16[2,384,768]{2,1,0:T(8,128)(2,1)}, bf16[2,384,768]{2,1,0:T(8,128)(2,1)}, u32[]{:S(2)}, u32[]{:S(2)}) collective-permute-start(bf16[2,384,768]{2,1,0:T(8,128)(2,1)} %dynamic-slice_bitcast_fusion.1), channel_id=1, source_target_pairs={{0,8},{8,0},{16,24},{24,16},{1,9},{9,1},{17,25},{25,17},{2,10},{10... | collective-permute-start | bytes 3538952 | tf_op jit(solution)/shard_map/ppermute | solution.py:65
  444.3 10.5 %collective-permute-start.29 = (bf16[440,384]{1,0:T(8,128)(2,1)}, bf16[440,384]{1,0:T(8,128)(2,1)}, u32[]{:S(2)}, u32[]{:S(2)}) collective-permute-start(bf16[440,384]{1,0:T(8,128)(2,1)} %pad_maximum_fusion.8), channel_id=1, source_target_pairs={{0,16},{8,24},{16,0},{24,8},{1,17},{9,25},{17,1},{25,9},{2,18},{10... | collective-permute-start | bytes 1013768 | tf_op jit(solution)/shard_map/ppermute | solution.py:65
  457.0 36.4 %all-to-all-start.4 = ((bf16[8,128,384]{2,1,0:T(8,128)(2,1)}), bf16[8,128,384]{2,1,0:T(8,128)(2,1)}, u32[]{:S(2)}, u32[]{:S(2)}) async-start(bf16[8,128,384]{2,1,0:T(8,128)(2,1)} %broadcast_in_dim.136), calls=%async_computation.7 | async-start | bytes 1572864 | tf_op jit(solution)/shard_map/all_to_all | solution.py:31
  463.2 15.1 %collective-permute-start.27 = (bf16[384,768]{1,0:T(8,128)(2,1)}, bf16[384,768]{1,0:T(8,128)(2,1)}, u32[]{:S(2)}, u32[]{:S(2)}) collective-permute-start(bf16[384,768]{1,0:T(8,128)(2,1)} %dynamic-slice_bitcast_fusion.2), channel_id=1, source_target_pairs={{0,16},{8,24},{16,0},{24,8},{1,17},{9,25},{17,1},{25,9},{2,18},{10... | collective-permute-start | bytes 1769480 | tf_op jit(solution)/shard_map/ppermute | solution.py:65
  466.9 8.4 %collective-permute-start.30 = (bf16[1,64,32]{2,1,0:T(8,128)(2,1)S(1)}, bf16[1,64,32]{2,1,0:T(8,128)(2,1)S(1)}, u32[]{:S(2)}, u32[]{:S(2)}) collective-permute-start(bf16[1,64,32]{2,1,0:T(8,128)(2,1)S(1)} %get-tuple-element.270), channel_id=1, source_target_pairs={{0,8},{8,16},{16,24},{1,9},{9,17},{17,25},{2,10},{10,18},{18,26},{... | collective-permute-start | bytes 12296 | tf_op jit(solution)/shard_map/ppermute | solution.py:225
  468.2 7.1 %collective-permute-start.31 = (bf16[1,64,32]{2,1,0:T(8,128)(2,1)S(1)}, bf16[1,64,32]{2,1,0:T(8,128)(2,1)S(1)}, u32[]{:S(2)}, u32[]{:S(2)}) collective-permute-start(bf16[1,64,32]{2,1,0:T(8,128)(2,1)S(1)} %get-tuple-element.271), channel_id=1, source_target_pairs={{8,0},{16,8},{24,16},{9,1},{17,9},{25,17},{10,2},{18,10},{26,18},{... | collective-permute-start | bytes 12296 | tf_op jit(solution)/shard_map/ppermute | solution.py:225
  470.7 9.7 %collective-permute-start.35 = (bf16[128,1536]{1,0:T(8,128)(2,1)}, bf16[128,1536]{1,0:T(8,128)(2,1)}, u32[]{:S(2)}, u32[]{:S(2)}) collective-permute-start(bf16[128,1536]{1,0:T(8,128)(2,1)} %reduce-scatter.8.cloned.1.call-done), channel_id=1, source_target_pairs={{0,0},{1,4},{2,8},{3,12},{4,16},{5,20},{6,24},{7,28},{8,1},{9,5},{... | collective-permute-start | bytes 1179656 | tf_op jit(solution)/shard_map/ppermute | solution.py:1630
  496.9 47.4 %all-to-all-start.5 = ((bf16[8,48,1208]{2,1,0:T(8,128)(2,1)}), bf16[8,48,1208]{2,1,0:T(8,128)(2,1)S(1)}, u32[]{:S(2)}, u32[]{:S(2)}) async-start(bf16[8,48,1208]{2,1,0:T(8,128)(2,1)} %broadcast_add_fusion), calls=%async_computation.8 | async-start | bytes 1966080 | tf_op jit(solution)/shard_map/all_to_all | solution.py:37
  523.6 10.0 %collective-permute-start.32 = (f32[8,48]{0,1:T(8,128)S(1)}, f32[8,48]{0,1:T(8,128)S(1)}, u32[]{:S(2)}, u32[]{:S(2)}) collective-permute-start(f32[8,48]{0,1:T(8,128)S(1)} %fusion.13), channel_id=1, source_target_pairs={{0,0},{1,4},{2,8},{3,12},{4,16},{5,20},{6,24},{7,28},{8,1},{9,5},{... | collective-permute-start | bytes 4616 | tf_op jit(solution)/shard_map/ppermute | solution.py:1651
  (68 other events, 651.0 us)
Sparse Core Ops, SparseCore 0:
  24.1 51.9 all-gather.7
  77.7 41.7 all-gather.9
  167.3 31.8 all-gather.11
  264.6 37.7 reduce-scatter.3
  304.9 47.8 reduce-scatter.5
  370.9 31.3 reduce-scatter.7
  415.1 58.5 all-gather.13

commit v3 on v2

--- a/solution.py
+++ b/solution.py
@@ -92,27 +92,6 @@
     kept = (pick(parts, core, 1).astype(f32) + near.astype(f32)).astype(bf16)
     far = pairwise(pick(kept, 1 - chip, 0), 2)
     return pick(kept, chip, 0).astype(f32) + far.astype(f32)
-
-
-def row_sums(value, rows):
-    if lax.axis_size("row") != 4:
-        return row_scatter(value), lax.psum(rows.astype(bf16), "row").astype(f32)
-    row = lax.axis_index("row")
-    chip, core = row // 2, row % 2
-    size = value.shape[0] // 4
-    parts = value.astype(bf16).reshape((2, 2, size) + value.shape[1:])
-    rows = rows.astype(bf16)
-
-    def pick(array, which, axis):
-        return lax.dynamic_index_in_dim(array, which, axis, keepdims=False)
-
-    sent = pick(parts, 1 - core, 1).reshape((2 * size,) + value.shape[1:])
-    near = pairwise(jnp.concatenate([sent, rows], axis=0), 1).astype(f32)
-    kept = pick(parts, core, 1).astype(f32) + near[: 2 * size].reshape((2, size) + value.shape[1:])
-    kept = kept.astype(bf16)
-    rows = (rows.astype(f32) + near[2 * size :]).astype(bf16)
-    far = pairwise(jnp.concatenate([pick(kept, 1 - chip, 0), rows], axis=0), 2).astype(f32)
-    return pick(kept, chip, 0).astype(f32) + far[:size], rows.astype(f32) + far[size:]
 
 
 def ring_of(count):
@@ -1412,17 +1391,7 @@
         source_row, rest = divmod(source, col_n)
         moves.append((source, rest * rows_n + source_row))
     output_sum = to_chunks(grad_output_part)
-    got_gu = swap(
-        jnp.concatenate(
-            [
-                after(grad_gu_sum, grad_mixed).reshape(tp_n, owned, -1),
-                output_sum.reshape(tp_n, owned, model),
-            ],
-            axis=2,
-        ),
-        "tp",
-    )
-    grad_output = jnp.sum(got_gu[:, :, 2 * ff_mine :].astype(f32), axis=0)
+    got_gu = swap(after(grad_gu_sum, grad_mixed).reshape(tp_n, owned, -1), "tp")
     grad_down_part = dot(hidden, after(grad_feed, grad_queries), 0, 0).astype(bf16)
     grad_down = (
         grad_down_part.reshape(sub_n, rows_n, ff // all_n, model)
@@ -1441,12 +1410,6 @@
     )
 
     grad_down_sum = to_chunks(grad_down)
-
-    def in_lanes(rows, lanes):
-        return rows.reshape(rows.shape[0], -1, lanes).transpose(1, 0, 2).reshape(-1, lanes)
-
-    def from_lanes(rows, count):
-        return rows.reshape(-1, count, rows.shape[-1]).transpose(1, 0, 2).reshape(count, -1)
 
     upper = grad_both[:, :edge].astype(bf16)
     lower = grad_both[:, near - edge :].astype(bf16)
@@ -1470,7 +1433,7 @@
     grad_keys, grad_values = middle[:head_width], middle[head_width:]
 
     grad_raw, cells, grad_embedding, rows_first_scale, sums, head_sums = pl.pallas_call(
-        functools.partial(finish_kernel, heads, span),
+        waits_for(functools.partial(finish_kernel, heads, span), 14, 2),
         grid=(blocks,),
         in_specs=[
             by_block(head_width),
@@ -1487,6 +1450,8 @@
             whole(*first_mods.shape),
             whole(model, 4 * head_width),
             whole(model, patch),
+            ANYWHERE,
+            ANYWHERE,
         ],
         out_specs=[
             by_rows(4 * head_width),
@@ -1527,30 +1492,18 @@
         first_mods,
         weight_qkvc,
         embedding_t,
+        output_sum,
+        got_gu,
     )
 
     grad_qkvc = dot(normed, grad_raw, 0, 0).astype(bf16)
 
-    def in_lanes(rows, lanes):
-        return rows.reshape(rows.shape[0], -1, lanes).transpose(1, 0, 2).reshape(-1, lanes)
-
-    def from_lanes(rows, count):
-        return rows.reshape(-1, count, rows.shape[-1]).transpose(1, 0, 2).reshape(count, -1)
-
     grad_cap = row_scatter(
-        after(jnp.concatenate([grad_cap_keys, grad_cap_values], axis=0), grad_qkvc)
+        after(jnp.concatenate([grad_cap_keys, grad_cap_values], axis=0), grad_raw)
     ).astype(bf16)
     if sub_n > 1:
         grad_cap = lax.psum_scatter(grad_cap, "sub", scatter_dimension=0, tiled=True)
     cap_rows = 2 * head_width // (rows_n * sub_n)
-    grad_cap = lax.all_gather(grad_cap, ALL, axis=0)
-    grad_cap = (
-        grad_cap.reshape(rows_n, sub_n, tp_n, cap_rows, text)
-        .transpose(2, 0, 1, 3, 4)
-        .reshape(tp_n, 2, head_width, text)
-        .transpose(1, 0, 2, 3)
-        .reshape(2 * model, text)
-    )
 
 
     def place(vectors):
@@ -1563,6 +1516,10 @@
     )
     small = jnp.concatenate(
         [
+            bands(rows_first_scale),
+            bands(rows_first_gate),
+            bands(rows_second_scale),
+            bands(rows_second_gate),
             grad_embedding,
             grad_unpatch,
             sums,
@@ -1574,33 +1531,32 @@
     small_width = small.shape[0]
     small = small.reshape(small_width, rows_n, model // rows_n).transpose(1, 0, 2)
     small = small.reshape(rows_n * small_width, model // rows_n)
-    small, all_mods = row_sums(
-        small,
-        in_lanes(
-            jnp.concatenate(
-                [
-                    bands(after(rows_first_scale, grad_qkvc, got_gu)),
-                    bands(rows_first_gate),
-                    bands(rows_second_scale),
-                    bands(rows_second_gate),
-                ],
-                axis=0,
-            ),
-            model // rows_n,
-        ),
-    )
-    all_mods = spread_all(after(all_mods, grad_down_sum).astype(bf16), COL)
-    all_mods = from_lanes(jnp.sum(all_mods.astype(f32), axis=0), 4 * NBAND)
-    small = small.astype(bf16).T
+    small = row_scatter(small).astype(bf16)
+    mods_rows = 4 * NBAND
+    lanes = model // rows_n
+    joint = jnp.concatenate(
+        [grad_cap, small[:mods_rows].reshape(-1, text)], axis=0
+    )
+    joint = lax.all_gather(after(joint, grad_down_sum), ALL, axis=0)
+    all_mods = joint[:, cap_rows:].astype(f32).reshape(rows_n, col_n, mods_rows, lanes)
+    all_mods = jnp.sum(all_mods, axis=1).transpose(1, 0, 2).reshape(mods_rows, model)
+    grad_cap = joint[:, :cap_rows]
+    small = small[mods_rows:]
+    small_width = small_width - mods_rows
+    small = small.T
     if sub_n > 1:
         small = lax.psum_scatter(small, "sub", scatter_dimension=0, tiled=True)
     small = small.reshape(tp_n, owned, small_width)
     qkvc_width = 4 * head_width
     sent = scatter_rows(grad_qkvc).reshape(tp_n, owned, qkvc_width)
-    sent = jnp.concatenate([sent, small, cells_out(first_cells, cells)], axis=2)
-    got = swap(after(sent, all_mods), "tp")
-    small = jnp.sum(got[:, :, qkvc_width : qkvc_width + small_width].astype(f32), axis=0)
-    cells_at = qkvc_width + small_width
+    sent = jnp.concatenate(
+        [sent, output_sum.reshape(tp_n, owned, model), small, cells_out(first_cells, cells)], axis=2
+    )
+    got = swap(sent, "tp")
+    grad_output = jnp.sum(got[:, :, qkvc_width : qkvc_width + model].astype(f32), axis=0)
+    small_at = qkvc_width + model
+    cells_at = small_at + small_width
+    small = jnp.sum(got[:, :, small_at:cells_at].astype(f32), axis=0)
     both_cells = cells_in(got[:, :, cells_at:])
     prediction, latent_grad = both_cells[..., :channels], both_cells[..., channels:]
     copies = []
@@ -1621,10 +1577,15 @@
     grad_unpatch = small[:, patch : 2 * patch]
     vectors = small[:, at:].T
 
+    grad_cap = (
+        grad_cap.reshape(rows_n, sub_n, tp_n, cap_rows, text)
+        .transpose(2, 0, 1, 3, 4)
+        .reshape(tp_n, 2, head_width, text)
+        .transpose(1, 0, 2, 3)
+        .reshape(2 * model, text)
+    )
     cap_own = captions.shape[1] // all_n
-    own_captions = after(
-        lax.dynamic_slice_in_dim(captions, index * cap_own, cap_own, 1), all_mods
-    )
+    own_captions = lax.dynamic_slice_in_dim(captions, index * cap_own, cap_own, 1)
     grad_caption = dot(own_captions, grad_cap, 0, 1)
 
     grad_down = lax.ppermute(grad_down_sum, ALL, moves).astype(f32)

time: 568 us -> 571 us (level)
  the two profiles are of different devices: /device:TPU:0 before, /device:TPU:7 now
where the time goes in v3:
time: 571 us; the launch traced here: 560 us
  starting transfers between devices  124 us (22%)
  Pallas kernels  107 us (19%)
  local copies, waits for them, and re-layouts  97.4 us (17%)
  waiting for transfers between devices  89.6 us (16%)
  other arithmetic  53.8 us (9%)
  matrix products  49 us (9%)
  between operations  39.2 us (7%)
    all_to_all x5, starting transfers between devices, swap(): return lax.all_to_all(value, axes, 0, 0, tiled=True)  46.3 us
    dot_general x17, matrix products, dot(): lax.dot_general(left, right, (((left_dim,), (right_dim,)), ((), ())), pre...  42.8 us
    ppermute x8, starting transfers between devices, shift(): return lax.ppermute(cells, axis, pairs)  39.4 us
    pallas_call x1, Pallas kernels, on_device(): pl.pallas_call(functools.partial(middle_kernel, len(pieces), span), grid_...  34.6 us
    all_gather x1, waiting for transfers between devices, on_device(): joint = lax.all_gather(after(joint, grad_down_sum), ALL, axis=0)  27.4 us
    slice x19, local copies, waits for them, and re-layouts, nothing(): return sum((other[(0,) * other.ndim].astype(f32) * 0.0 for other in others))  18.8 us
    ppermute x8, waiting for transfers between devices, onward(): lax.ppermute(value, axis, [(ring[i], ring[(i + 1) % count]) for i in rang...  16.7 us
    all_gather x1, waiting for transfers between devices, on_device(): output_piece = lax.all_gather(output_piece, COL, axis=0, tiled=True)  16.7 us
  transfers between devices with their start and end apart: 48, of which 18 were waited for; matrix products, arithmetic and copies ran while one was open for 30% of the time, Pallas kernels for 13%

profile of v3, /device:TPU:7, one launch (start us, length us, event | category | flops | bytes accessed | tf_op | source)
XLA Modules:
  0.0 559.7 jit_solution(12596996380314807528)
XLA Ops:
  13.2 5.9 %all-to-all-start = ((bf16[8,48,896]{2,1,0:T(8,128)(2,1)}), bf16[8,48,896]{2,1,0:T(8,128)(2,1)}, u32[]{:S(2)}, u32[]{:S(2)}) async-start(bf16[8,48,896]{2,1,0:T(8,128)(2,1)} %pad_maximum_fusion.3), calls=%async_computation | async-start | bytes 1376256 | tf_op jit(solution)/shard_map/all_to_all | solution.py:37
  24.3 2.7 broadcast_select_fusion
  31.7 2.4 reshape.359
  36.4 3.1 dynamic-slice_bitcast_fusion
  45.0 5.6 all-to-all-start.1
  50.6 4.7 collective-permute-done.2
  57.7 2.2 collective-permute-start.3
  59.9 16.7 %all-gather.7.cloned.1.call-done = bf16[1536,384]{1,0:T(8,128)(2,1)} async-done(((bf16[192,384]{1,0:T(8,128)(2,1)}), bf16[1536,384]{1,0:T(8,128)(2,1)}) %all-gather.7.cloned.1.call-update) | async-done | bytes 1179664 | tf_op jit(solution)/shard_map/all_gather | solution.py:955
  82.7 4.5 collective-permute-start.1
  88.7 2.3 fusion.103
  91.0 4.2 concatenate.109
  96.3 3.8 concatenate.116
  109.1 3.9 collective-permute-start.6
  116.1 10.0 %project.1 = (f32[1024,1536]{1,0:T(8,128)}, bf16[1024,1536]{1,0:T(8,128)(2,1)}, bf16[384,1024]{1,0:T(8,128)(2,1)}, bf16[192,1024]{1,0:T(8,128)(2,1)}, bf16[384,1...) custom-call(bf16[1024,144]{1,0:T(8,128)(2,1)} %bitcast.256, bf16[1536,144]{1,0:T(8,128)(2,1)} %bitcast.222, ...), custom_call_target="tpu_custom_call" | custom-call | flops 10000000000 | bytes 30000000 | tf_op jit(solution)/shard_map/project/pallas_call | solution.py:999
  128.8 3.8 collective-permute-start.5
  135.6 6.5 %all-to-all-start.2 = ((bf16[8,240,256]{2,1,0:T(8,128)(2,1)}), bf16[8,240,256]{2,1,0:T(8,128)(2,1)S(1)}, u32[]{:S(2)}, u32[]{:S(2)}) async-start(bf16[8,240,256]{2,1,0:T(8,128)(2,1)} %maximum_add_fusion.1), calls=%async_computation.2 | async-start | bytes 1966080 | tf_op jit(solution)/shard_map/all_to_all | solution.py:37
  145.4 14.7 %attend.1 = (bf16[192,1024]{1,0:T(8,128)(2,1)}, f32[192,1024]{1,0:T(8,128)}, f32[192,1024]{1,0:T(8,128)}, f32[8,1024]{1,0:T(8,128)}) custom-call(s32[32]{0:T(128)} %copy-done.41, s32[4]{0:T(128)} %get-tuple-element.317.refs_1_.low_ref, s32[4]{0:T(128)} %get-tuple-element.316.refs_2_.high_ref, s32[1,1024]{1,0:T(1,128)} %broadcast_in_dim_reshape.3.refs_3_.item_query_ref, ...), custom_call_target="tpu_custom_call" | custom-call | flops 14000000000 | bytes 42000000 | tf_op jit(solution)/shard_map/attend/pallas_call | solution.py:1093
  168.3 6.4 %collective-permute-done.8.refs_1_ = bf16[192,1024]{1,0:T(8,128)(2,1)S(1)} collective-permute-done((bf16[192,1024]{1,0:T(8,128)(2,1)S(1)}, bf16[192,1024]{1,0:T(8,128)(2,1)S(1)}, u32[]{:S(2)}, u32[]{:S(2)}) %collective-permute-start.8) | collective-permute-done | bytes 393248 | tf_op jit(solution)/shard_map/ppermute | solution.py:115
  176.2 6.2 %collective-permute-done.10.refs_3_ = bf16[192,1024]{1,0:T(8,128)(2,1)S(1)} collective-permute-done((bf16[192,1024]{1,0:T(8,128)(2,1)S(1)}, bf16[192,1024]{1,0:T(8,128)(2,1)S(1)}, u32[]{:S(2)}, u32[]{:S(2)}) %collective-permute-start.10) | collective-permute-done | bytes 393248 | tf_op jit(solution)/shard_map/ppermute | solution.py:115
  198.7 3.7 all-gather.13.cloned.1.call-done
  202.3 3.8 slice.621
  208.4 34.6 %middle.1 = (bf16[1536,1024]{1,0:T(8,128)(2,1)}, f32[1024,1536]{1,0:T(8,128)}, bf16[1024,1536]{1,0:T(8,128)(2,1)}, bf16[1024,512]{1,0:T(8,128)(2,1)}, bf16[1024,...) custom-call(s32[2]{0:T(128)} %pad_add_fusion.1.own_ref.refs_0_, ...), custom_call_target="tpu_custom_call" | custom-call | flops 35000000512 | bytes 105000000 | tf_op jit(solution)/shard_map/middle/pallas_call | solution.py:1161
  246.8 2.8 collective-permute-done.16
  253.1 6.5 %convolution_convert_fusion.1 = bf16[1536,1024]{1,0:T(8,128)(2,1)} fusion(bf16[1024,1536]{1,0:T(8,128)(2,1)S(1)} %copy-done.54, bf16[1024,1024]{1,0:T(8,128)(2,1)} %get-tuple-element.69, bf16[]{:T(256)} %bitcast.60), kind=kOutput, calls=%fused_computation.1 | convolution fusion | flops 3223846912 | bytes 8388610 | tf_op jit(solution)/shard_map/dot_general | solution.py:192
  261.0 3.5 collective-permute-done.19
  270.4 3.7 collective-permute-done.20
  275.9 2.4 fusion.95
  280.6 8.6 %convolution_convert_fusion = bf16[1536,1536]{1,0:T(8,128)(2,1)} fusion(bf16[1536,1024]{1,0:T(8,128)(2,1)S(1)} %copy-done.55, bf16[1024,1536]{1,0:T(8,128)(2,1)} %get-tuple-element.71, bf16[]{:T(256)} %bitcast.62), kind=kOutput, calls=%fused_computation | convolution fusion | flops 4835770368 | bytes 11010050 | tf_op jit(solution)/shard_map/dot_general | solution.py:192
  301.2 9.6 %result.1 = (f32[1024,144]{1,0:T(8,128)}, f32[144,1536]{1,0:T(8,128)}, f32[16,1536]{1,0:T(8,128)}) custom-call(s32[2]{0:T(128)} %pad_add_fusion.1.own_ref.refs_0_, bf16[1024,512]{1,0:T(8,128)(2,1)} %get-tuple-element.72.refs_1_, f32[1024,1536]{1,0:T(8,128)} %get-tuple-element.73.refs_2_, bf16[1024,144]{1,0:T(8,128)(2,1)} %bitcast.260, ...), custom_call_target="tpu_custom_call" | custom-call | flops 8999999488 | bytes 27000000 | tf_op jit(solution)/shard_map/result/pallas_call | solution.py:1225
  321.2 14.3 %attend_back.1 = (f32[192,1024]{1,0:T(8,128)}, f32[384,2048]{1,0:T(8,128)}) custom-call(s32[32]{0:T(128)} %copy-done.41, s32[4]{0:T(128)} %get-tuple-element.317.refs_1_.low_ref, s32[4]{0:T(128)} %get-tuple-element.316.refs_2_.high_ref, s32[1,1024]{1,0:T(1,128)} %broadcast_in_dim_reshape.3.refs_3_.item_query_ref, ...), custom_call_target="tpu_custom_call" | custom-call | flops 14000000000 | bytes 42000000 | tf_op jit(solution)/shard_map/attend_back/pallas_call | solution.py:1359
  340.1 7.2 %cross_back.1 = (bf16[192,1024]{1,0:T(8,128)(2,1)}, f32[192,256]{1,0:T(8,128)}, f32[192,256]{1,0:T(8,128)}, f32[192,128]{1,0:T(8,128)}) custom-call(bf16[192,1024]{1,0:T(8,128)(2,1)} %get-tuple-element.64.refs_8_.cross_ref, bf16[192,256]{1,0:T(8,128)(2,1)} %get-tuple-element.301.refs_9_.caption_key_ref, ...), custom_call_target="tpu_custom_call" | custom-call | flops 7000000000 | bytes 21000000 | tf_op jit(solution)/shard_map/cross_back/pallas_call | solution.py:1330
  349.4 5.5 all-to-all-start.3
  356.3 22.5 %collective-permute-start.25 = (bf16[384,512]{1,0:T(8,128)(2,1)S(1)}, bf16[384,512]{1,0:T(8,128)(2,1)}, u32[]{:S(2)}, u32[]{:S(2)}) collective-permute-start(bf16[384,512]{1,0:T(8,128)(2,1)S(1)} %get-tuple-element.265), channel_id=1, source_target_pairs={{8,0},{16,8},{24,16},{9,1},{17,9},{25,17},{10,2},{18,10},{26,18},{... | collective-permute-start | bytes 1179656 | tf_op jit(solution)/shard_map/ppermute | solution.py:204
  379.8 5.2 fusion.3
  389.4 13.6 %finish.1 = (bf16[1024,768]{1,0:T(8,128)(2,1)}, f32[1024,144]{1,0:T(8,128)}, f32[144,1536]{1,0:T(8,128)}, f32[16,1536]{1,0:T(8,128)}, f32[8,1536]{1,0:T(8,128)}, /*index=5*/f32[192,128]{1,0:T(8,128)}) custom-call(f32[192,1024]{1,0:T(8,128)} %get-tuple-element.79.refs_0_, f32[192,1024]{1,0:T(8,128)} %get-tuple-element.263.refs_1_, ...), custom_call_target="tpu_custom_call" | custom-call | flops 12999999488 | bytes 39000000 | tf_op jit(solution)/shard_map/finish/pallas_call | solution.py:1435
  415.6 5.5 collective-permute-done.29
  421.8 5.0 convolution_convert_fusion.2
  436.9 3.4 collective-permute-start.31
  440.4 4.4 collective-permute-start.35
  445.4 4.3 collective-permute-done.27
  450.9 4.4 concatenate.132
  455.2 22.7 %all-to-all-start.4 = ((bf16[8,48,2744]{2,1,0:T(8,128)(2,1)}), bf16[8,48,2744]{2,1,0:T(8,128)(2,1)S(1)}, u32[]{:S(2)}, u32[]{:S(2)}) async-start(bf16[8,48,2744]{2,1,0:T(8,128)(2,1)} %concatenate.132), calls=%async_computation.6 | async-start | bytes 4325376 | tf_op jit(solution)/shard_map/all_to_all | solution.py:37
  478.0 2.4 slice.654
  482.5 27.4 %all-gather.9.cloned.1.call-done = bf16[32,144,256]{2,1,0:T(8,128)(2,1)} async-done(((bf16[1,144,256]{2,1,0:T(8,128)(2,1)}), bf16[32,144,256]{2,1,0:T(8,128)(2,1)}) %all-gather.9.cloned.1.call-update) | async-done | bytes 2359312 | tf_op jit(solution)/shard_map/all_gather | solution.py:1540
  510.0 2.5 slice_convert_fusion
  512.4 2.7 reshape.385
  524.2 10.3 %collective-permute-start.34 = (f32[8,48]{0,1:T(8,128)S(1)}, f32[8,48]{0,1:T(8,128)S(1)}, u32[]{:S(2)}, u32[]{:S(2)}) collective-permute-start(f32[8,48]{0,1:T(8,128)S(1)} %fusion.13), channel_id=1, source_target_pairs={{0,0},{1,4},{2,8},{3,12},{4,16},{5,20},{6,24},{7,28},{8,1},{9,5},{... | collective-permute-start | bytes 4616 | tf_op jit(solution)/shard_map/ppermute | solution.py:1612
  540.2 2.6 fusion.55
  (435 shorter events, 165.9 us)
Async XLA Ops:
  13.2 26.2 %all-to-all-start = ((bf16[8,48,896]{2,1,0:T(8,128)(2,1)}), bf16[8,48,896]{2,1,0:T(8,128)(2,1)}, u32[]{:S(2)}, u32[]{:S(2)}) async-start(bf16[8,48,896]{2,1,0:T(8,128)(2,1)} %pad_maximum_fusion.3), calls=%async_computation | async-start | bytes 1376256 | tf_op jit(solution)/shard_map/all_to_all | solution.py:37
  19.1 57.4 %all-gather.7.cloned.1.call-start = ((), (), s32[]{:S(2)}) async-start(), calls=%async_computation.8 | async-start | bytes 1327104 | tf_op jit(solution)/shard_map/all_gather | solution.py:955
  41.4 13.9 %collective-permute-start.2 = (bf16[8,48,768]{2,1,0:T(8,128)(2,1)}, bf16[8,48,768]{2,1,0:T(8,128)(2,1)}, u32[]{:S(2)}, u32[]{:S(2)}) collective-permute-start(bf16[8,48,768]{2,1,0:T(8,128)(2,1)} %slice.602), channel_id=1, source_target_pairs={{0,16},{8,24},{16,0},{24,8},{1,17},{9,25},{17,1},{25,9},{2,18},{10... | collective-permute-start | bytes 1769480 | tf_op jit(solution)/shard_map/ppermute | solution.py:65
  45.0 60.4 %all-to-all-start.1 = ((bf16[8,48,1792]{2,1,0:T(8,128)(2,1)}), bf16[8,48,1792]{2,1,0:T(8,128)(2,1)}, u32[]{:S(2)}, u32[]{:S(2)}) async-start(bf16[8,48,1792]{2,1,0:T(8,128)(2,1)} %maximum_add_fusion), calls=%async_computation.1 | async-start | bytes 2752512 | tf_op jit(solution)/shard_map/all_to_all | solution.py:37
  50.5 111.5 %all-gather.11.cloned.1.call-start = ((), (), s32[]{:S(2)}) async-start(), calls=%async_computation.13 | async-start | bytes 5898240 | tf_op jit(solution)/shard_map/all_gather | solution.py:956
  57.7 42.4 %collective-permute-start.3 = (bf16[2,8,48,768]{3,2,1,0:T(8,128)(2,1)}, bf16[2,8,48,768]{3,2,1,0:T(8,128)(2,1)}, u32[]{:S(2)}, u32[]{:S(2)}) collective-permute-start(bf16[2,8,48,768]{3,2,1,0:T(8,128)(2,1)} %pad_maximum_fusion.1), channel_id=1, source_target_pairs={{0,8},{8,0},{16,24},{24,16},{1,9},{9,1},{17,25},{25,17},{2,10},{10... | collective-permute-start | bytes 3538952 | tf_op jit(solution)/shard_map/ppermute | solution.py:65
  81.4 5.9 %collective-permute-start = (bf16[1,64,32]{2,1,0:T(8,128)(2,1)S(1)}, bf16[1,64,32]{2,1,0:T(8,128)(2,1)S(1)}, u32[]{:S(2)}, u32[]{:S(2)}) collective-permute-start(bf16[1,64,32]{2,1,0:T(8,128)(2,1)S(1)} %get-tuple-element.294), channel_id=1, source_target_pairs={{0,8},{8,16},{16,24},{1,9},{9,17},{17,25},{2,10},{10,18},{18,26},{... | collective-permute-start | bytes 12296 | tf_op jit(solution)/shard_map/ppermute | solution.py:204
  82.7 4.8 collective-permute-start.1
  109.1 17.0 %collective-permute-start.6 = (bf16[48,768]{1,0:T(8,128)(2,1)S(1)}, bf16[48,768]{1,0:T(8,128)(2,1)S(1)}, u32[]{:S(2)}, u32[]{:S(2)}) collective-permute-start(bf16[48,768]{1,0:T(8,128)(2,1)S(1)} %pad_maximum_fusion.13), channel_id=1, source_target_pairs={{0,16},{8,24},{16,0},{24,8},{1,17},{9,25},{17,1},{25,9},{2,18},{10... | collective-permute-start | bytes 221192 | tf_op jit(solution)/shard_map/ppermute | solution.py:65
  126.2 16.0 %collective-permute-start.7 = (bf16[2,48,768]{2,1,0:T(8,128)(2,1)S(1)}, bf16[2,48,768]{2,1,0:T(8,128)(2,1)S(1)}, u32[]{:S(2)}, u32[]{:S(2)}) collective-permute-start(bf16[2,48,768]{2,1,0:T(8,128)(2,1)S(1)} %pad_maximum_fusion.11), channel_id=1, source_target_pairs={{0,8},{8,0},{16,24},{24,16},{1,9},{9,1},{17,25},{25,17},{2,10},{10... | collective-permute-start | bytes 442376 | tf_op jit(solution)/shard_map/ppermute | solution.py:65
  127.5 17.1 %collective-permute-start.4 = (bf16[384,512]{1,0:T(8,128)(2,1)S(1)}, bf16[384,512]{1,0:T(8,128)(2,1)S(1)}, u32[]{:S(2)}, u32[]{:S(2)}) collective-permute-start(bf16[384,512]{1,0:T(8,128)(2,1)S(1)} %get-tuple-element.269), channel_id=1, source_target_pairs={{0,8},{8,16},{16,24},{1,9},{9,17},{17,25},{2,10},{10,18},{18,26},{... | collective-permute-start | bytes 1179656 | tf_op jit(solution)/shard_map/ppermute | solution.py:204
  128.8 15.8 %collective-permute-start.5 = (bf16[384,512]{1,0:T(8,128)(2,1)S(1)}, bf16[384,512]{1,0:T(8,128)(2,1)}, u32[]{:S(2)}, u32[]{:S(2)}) collective-permute-start(bf16[384,512]{1,0:T(8,128)(2,1)S(1)} %get-tuple-element.268), channel_id=1, source_target_pairs={{8,0},{16,8},{24,16},{9,1},{17,9},{25,17},{10,2},{18,10},{26,18},{... | collective-permute-start | bytes 1179656 | tf_op jit(solution)/shard_map/ppermute | solution.py:204
  135.6 30.1 %all-to-all-start.2 = ((bf16[8,240,256]{2,1,0:T(8,128)(2,1)}), bf16[8,240,256]{2,1,0:T(8,128)(2,1)S(1)}, u32[]{:S(2)}, u32[]{:S(2)}) async-start(bf16[8,240,256]{2,1,0:T(8,128)(2,1)} %maximum_add_fusion.1), calls=%async_computation.2 | async-start | bytes 1966080 | tf_op jit(solution)/shard_map/all_to_all | solution.py:37
  142.2 60.2 %all-gather.13.cloned.1.call-start = ((), (), s32[]{:S(2)}) async-start(), calls=%async_computation.14 | async-start | bytes 4915200 | tf_op jit(solution)/shard_map/all_gather | solution.py:1143
  166.7 180.6 %reduce-scatter.6.cloned.1.call-start = ((), (), s32[]{:S(2)}) async-start(), calls=%async_computation.10 | async-start | bytes 3932160 | tf_op jit(solution)/shard_map/reduce_scatter | solution.py:1315
  166.8 7.9 %collective-permute-start.8 = (bf16[192,1024]{1,0:T(8,128)(2,1)S(1)}, bf16[192,1024]{1,0:T(8,128)(2,1)S(1)}, u32[]{:S(2)}, u32[]{:S(2)}) collective-permute-start(bf16[192,1024]{1,0:T(8,128)(2,1)S(1)} %copy-done.44), channel_id=1, source_target_pairs={{0,2},{2,4},{4,6},{6,7},{7,5},{5,3},{3,1},{1,0},{8,10},{10,12},{12... | collective-permute-start | bytes 1179656 | tf_op jit(solution)/shard_map/ppermute | solution.py:115
  166.9 8.1 %collective-permute-start.9 = (bf16[192,1024]{1,0:T(8,128)(2,1)S(1)}, bf16[192,1024]{1,0:T(8,128)(2,1)S(1)}, u32[]{:S(2)}, u32[]{:S(2)}) collective-permute-start(bf16[192,1024]{1,0:T(8,128)(2,1)S(1)} %copy-done.44), channel_id=1, source_target_pairs={{2,0},{4,2},{6,4},{7,6},{5,7},{3,5},{1,3},{0,1},{10,8},{12,10},{14... | collective-permute-start | bytes 1179656 | tf_op jit(solution)/shard_map/ppermute | solution.py:118
  174.7 7.7 %collective-permute-start.10 = (bf16[192,1024]{1,0:T(8,128)(2,1)S(1)}, bf16[192,1024]{1,0:T(8,128)(2,1)S(1)}, u32[]{:S(2)}, u32[]{:S(2)}) collective-permute-start(bf16[192,1024]{1,0:T(8,128)(2,1)S(1)} %collective-permute-done.8.refs_1_), channel_id=1, source_target_pairs={{0,2},{2,4},{4,6},{6,7},{7,5},{5,3},{3,1},{1,0},{8,10},{10,12},{12... | collective-permute-start | bytes 1179656 | tf_op jit(solution)/shard_map/ppermute | solution.py:115
  174.9 7.7 %collective-permute-start.11 = (bf16[192,1024]{1,0:T(8,128)(2,1)S(1)}, bf16[192,1024]{1,0:T(8,128)(2,1)S(1)}, u32[]{:S(2)}, u32[]{:S(2)}) collective-permute-start(bf16[192,1024]{1,0:T(8,128)(2,1)S(1)} %collective-permute-done.9.refs_2_), channel_id=1, source_target_pairs={{2,0},{4,2},{6,4},{7,6},{5,7},{3,5},{1,3},{0,1},{10,8},{12,10},{14... | collective-permute-start | bytes 1179656 | tf_op jit(solution)/shard_map/ppermute | solution.py:118
  182.4 14.5 %collective-permute-start.12 = (bf16[192,1024]{1,0:T(8,128)(2,1)S(1)}, bf16[192,1024]{1,0:T(8,128)(2,1)S(1)}, u32[]{:S(2)}, u32[]{:S(2)}) collective-permute-start(bf16[192,1024]{1,0:T(8,128)(2,1)S(1)} %collective-permute-done.10.refs_3_), channel_id=1, source_target_pairs={{0,2},{2,4},{4,6},{6,7},{7,5},{5,3},{3,1},{1,0},{8,10},{10,12},{12... | collective-permute-start | bytes 1179656 | tf_op jit(solution)/shard_map/ppermute | solution.py:115
  182.6 14.6 %collective-permute-start.13 = (bf16[192,1024]{1,0:T(8,128)(2,1)S(1)}, bf16[192,1024]{1,0:T(8,128)(2,1)S(1)}, u32[]{:S(2)}, u32[]{:S(2)}) collective-permute-start(bf16[192,1024]{1,0:T(8,128)(2,1)S(1)} %collective-permute-done.11.refs_4_), channel_id=1, source_target_pairs={{2,0},{4,2},{6,4},{7,6},{5,7},{3,5},{1,3},{0,1},{10,8},{12,10},{14... | collective-permute-start | bytes 1179656 | tf_op jit(solution)/shard_map/ppermute | solution.py:118
  196.9 11.5 %collective-permute-start.14 = (bf16[96,1024]{1,0:T(8,128)(2,1)S(1)}, bf16[96,1024]{1,0:T(8,128)(2,1)}, u32[]{:S(2)}, u32[]{:S(2)}) collective-permute-start(bf16[96,1024]{1,0:T(8,128)(2,1)S(1)} %slice.618), channel_id=1, source_target_pairs={{0,2},{2,4},{4,6},{6,7},{7,5},{5,3},{3,1},{1,0},{8,10},{10,12},{12... | collective-permute-start | bytes 589832 | tf_op jit(solution)/shard_map/ppermute | solution.py:115
  197.2 11.1 %collective-permute-start.15 = (bf16[96,1024]{1,0:T(8,128)(2,1)S(1)}, bf16[96,1024]{1,0:T(8,128)(2,1)}, u32[]{:S(2)}, u32[]{:S(2)}) collective-permute-start(bf16[96,1024]{1,0:T(8,128)(2,1)S(1)} %slice.619), channel_id=1, source_target_pairs={{2,0},{4,2},{6,4},{7,6},{5,7},{3,5},{1,3},{0,1},{10,8},{12,10},{14... | collective-permute-start | bytes 589832 | tf_op jit(solution)/shard_map/ppermute | solution.py:118
  245.1 4.5 collective-permute-start.16
  259.6 128.9 %reduce-scatter.4.cloned.1.call-start = ((), (), s32[]{:S(2)}) async-start(), calls=%async_computation.9 | async-start | bytes 5898240 | tf_op jit(solution)/shard_map/reduce_scatter | solution.py:1315
  259.7 4.8 collective-permute-start.19
  266.3 7.8 %collective-permute-start.20 = (bf16[192,1024]{1,0:T(8,128)(2,1)}, bf16[192,1024]{1,0:T(8,128)(2,1)}, u32[]{:S(2)}, u32[]{:S(2)}) collective-permute-start(bf16[192,1024]{1,0:T(8,128)(2,1)} %pad_maximum_fusion.5), channel_id=1, source_target_pairs={{2,0},{4,2},{6,4},{7,6},{5,7},{3,5},{1,3},{0,1},{10,8},{12,10},{14... | collective-permute-start | bytes 1179656 | tf_op jit(solution)/shard_map/ppermute | solution.py:118
  268.3 6.8 %collective-permute-start.17 = (bf16[192,1024]{1,0:T(8,128)(2,1)}, bf16[192,1024]{1,0:T(8,128)(2,1)S(1)}, u32[]{:S(2)}, u32[]{:S(2)}) collective-permute-start(bf16[192,1024]{1,0:T(8,128)(2,1)} %pad_maximum_fusion.4), channel_id=1, source_target_pairs={{0,2},{2,4},{4,6},{6,7},{7,5},{5,3},{3,1},{1,0},{8,10},{10,12},{12... | collective-permute-start | bytes 1179656 | tf_op jit(solution)/shard_map/ppermute | solution.py:115
  290.8 7.2 %collective-permute-start.18 = (bf16[192,1024]{1,0:T(8,128)(2,1)}, bf16[192,1024]{1,0:T(8,128)(2,1)S(1)}, u32[]{:S(2)}, u32[]{:S(2)}) collective-permute-start(bf16[192,1024]{1,0:T(8,128)(2,1)} %get-tuple-element.244), channel_id=1, source_target_pairs={{0,2},{2,4},{4,6},{6,7},{7,5},{5,3},{3,1},{1,0},{8,10},{10,12},{12... | collective-permute-start | bytes 1179656 | tf_op jit(solution)/shard_map/ppermute | solution.py:115
  291.0 7.2 %collective-permute-start.22 = (bf16[192,1024]{1,0:T(8,128)(2,1)S(1)}, bf16[192,1024]{1,0:T(8,128)(2,1)S(1)}, u32[]{:S(2)}, u32[]{:S(2)}) collective-permute-start(bf16[192,1024]{1,0:T(8,128)(2,1)S(1)} %get-tuple-element.254), channel_id=1, source_target_pairs={{2,0},{4,2},{6,4},{7,6},{5,7},{3,5},{1,3},{0,1},{10,8},{12,10},{14... | collective-permute-start | bytes 1179656 | tf_op jit(solution)/shard_map/ppermute | solution.py:118
  299.7 20.5 %collective-permute-start.21 = (bf16[192,1024]{1,0:T(8,128)(2,1)S(1)}, bf16[192,1024]{1,0:T(8,128)(2,1)S(1)}, u32[]{:S(2)}, u32[]{:S(2)}) collective-permute-start(bf16[192,1024]{1,0:T(8,128)(2,1)S(1)} %get-tuple-element.242), channel_id=1, source_target_pairs={{0,2},{2,4},{4,6},{6,7},{7,5},{5,3},{3,1},{1,0},{8,10},{10,12},{12... | collective-permute-start | bytes 1179656 | tf_op jit(solution)/shard_map/ppermute | solution.py:115
  301.2 19.0 %collective-permute-start.23 = (bf16[192,1024]{1,0:T(8,128)(2,1)S(1)}, bf16[192,1024]{1,0:T(8,128)(2,1)S(1)}, u32[]{:S(2)}, u32[]{:S(2)}) collective-permute-start(bf16[192,1024]{1,0:T(8,128)(2,1)S(1)} %get-tuple-element.252), channel_id=1, source_target_pairs={{2,0},{4,2},{6,4},{7,6},{5,7},{3,5},{1,3},{0,1},{10,8},{12,10},{14... | collective-permute-start | bytes 1179656 | tf_op jit(solution)/shard_map/ppermute | solution.py:118
  349.4 39.1 %all-to-all-start.3 = ((bf16[8,48,1024]{2,1,0:T(8,128)(2,1)}), bf16[8,48,1024]{2,1,0:T(8,128)(2,1)S(1)}, u32[]{:S(2)}, u32[]{:S(2)}) async-start(bf16[8,48,1024]{2,1,0:T(8,128)(2,1)} %bitcast.66), calls=%async_computation.5 | async-start | bytes 1572864 | tf_op jit(solution)/shard_map/all_to_all | solution.py:37
  355.0 58.7 %reduce-scatter.8.cloned.1.call-start = ((), (), s32[]{:S(2)}) async-start(), calls=%async_computation.11 | async-start | bytes 1966080 | tf_op jit(solution)/shard_map/reduce_scatter | solution.py:1315
  355.0 30.3 %collective-permute-start.24 = (bf16[384,512]{1,0:T(8,128)(2,1)S(1)}, bf16[384,512]{1,0:T(8,128)(2,1)S(1)}, u32[]{:S(2)}, u32[]{:S(2)}) collective-permute-start(bf16[384,512]{1,0:T(8,128)(2,1)S(1)} %get-tuple-element.264), channel_id=1, source_target_pairs={{0,8},{8,16},{16,24},{1,9},{9,17},{17,25},{2,10},{10,18},{18,26},{... | collective-permute-start | bytes 1179656 | tf_op jit(solution)/shard_map/ppermute | solution.py:204
  356.3 29.1 %collective-permute-start.25 = (bf16[384,512]{1,0:T(8,128)(2,1)S(1)}, bf16[384,512]{1,0:T(8,128)(2,1)}, u32[]{:S(2)}, u32[]{:S(2)}) collective-permute-start(bf16[384,512]{1,0:T(8,128)(2,1)S(1)} %get-tuple-element.265), channel_id=1, source_target_pairs={{8,0},{16,8},{24,16},{9,1},{17,9},{25,17},{10,2},{18,10},{26,18},{... | collective-permute-start | bytes 1179656 | tf_op jit(solution)/shard_map/ppermute | solution.py:204
  385.1 124.9 %all-gather.9.cloned.1.call-start = ((), (), s32[]{:S(2)}) async-start(), calls=%async_computation.12 | async-start | bytes 2433024 | tf_op jit(solution)/shard_map/all_gather | solution.py:1540
  409.1 3.5 collective-permute-start.28
  410.1 1.6 collective-permute-start.32
  411.8 3.7 collective-permute-start.33
  412.9 8.2 %collective-permute-start.29 = (bf16[344,384]{1,0:T(8,128)(2,1)S(1)}, bf16[344,384]{1,0:T(8,128)(2,1)S(1)}, u32[]{:S(2)}, u32[]{:S(2)}) collective-permute-start(bf16[344,384]{1,0:T(8,128)(2,1)S(1)} %dynamic-slice_bitcast_fusion.4), channel_id=1, source_target_pairs={{0,16},{8,24},{16,0},{24,8},{1,17},{9,25},{17,1},{25,9},{2,18},{10... | collective-permute-start | bytes 792584 | tf_op jit(solution)/shard_map/ppermute | solution.py:65
  428.1 4.2 collective-permute-start.26
  435.1 14.6 %collective-permute-start.27 = (bf16[384,768]{1,0:T(8,128)(2,1)}, bf16[384,768]{1,0:T(8,128)(2,1)}, u32[]{:S(2)}, u32[]{:S(2)}) collective-permute-start(bf16[384,768]{1,0:T(8,128)(2,1)} %dynamic-slice_bitcast_fusion.2), channel_id=1, source_target_pairs={{0,16},{8,24},{16,0},{24,8},{1,17},{9,25},{17,1},{25,9},{2,18},{10... | collective-permute-start | bytes 1769480 | tf_op jit(solution)/shard_map/ppermute | solution.py:65
  435.6 9.1 %collective-permute-start.30 = (bf16[1,64,32]{2,1,0:T(8,128)(2,1)S(1)}, bf16[1,64,32]{2,1,0:T(8,128)(2,1)S(1)}, u32[]{:S(2)}, u32[]{:S(2)}) collective-permute-start(bf16[1,64,32]{2,1,0:T(8,128)(2,1)S(1)} %get-tuple-element.270), channel_id=1, source_target_pairs={{0,8},{8,16},{16,24},{1,9},{9,17},{17,25},{2,10},{10,18},{18,26},{... | collective-permute-start | bytes 12296 | tf_op jit(solution)/shard_map/ppermute | solution.py:204
  436.9 7.8 %collective-permute-start.31 = (bf16[1,64,32]{2,1,0:T(8,128)(2,1)S(1)}, bf16[1,64,32]{2,1,0:T(8,128)(2,1)S(1)}, u32[]{:S(2)}, u32[]{:S(2)}) collective-permute-start(bf16[1,64,32]{2,1,0:T(8,128)(2,1)S(1)} %get-tuple-element.271), channel_id=1, source_target_pairs={{8,0},{16,8},{24,16},{9,1},{17,9},{25,17},{10,2},{18,10},{26,18},{... | collective-permute-start | bytes 12296 | tf_op jit(solution)/shard_map/ppermute | solution.py:204
  440.4 40.0 %collective-permute-start.35 = (bf16[128,1536]{1,0:T(8,128)(2,1)}, bf16[128,1536]{1,0:T(8,128)(2,1)S(1)}, u32[]{:S(2)}, u32[]{:S(2)}) collective-permute-start(bf16[128,1536]{1,0:T(8,128)(2,1)} %reduce-scatter.8.cloned.1.call-done), channel_id=1, source_target_pairs={{0,0},{1,4},{2,8},{3,12},{4,16},{5,20},{6,24},{7,28},{8,1},{9,5},{... | collective-permute-start | bytes 1179656 | tf_op jit(solution)/shard_map/ppermute | solution.py:1591
  455.2 89.2 %all-to-all-start.4 = ((bf16[8,48,2744]{2,1,0:T(8,128)(2,1)}), bf16[8,48,2744]{2,1,0:T(8,128)(2,1)S(1)}, u32[]{:S(2)}, u32[]{:S(2)}) async-start(bf16[8,48,2744]{2,1,0:T(8,128)(2,1)} %concatenate.132), calls=%async_computation.6 | async-start | bytes 4325376 | tf_op jit(solution)/shard_map/all_to_all | solution.py:37
  524.2 19.6 %collective-permute-start.34 = (f32[8,48]{0,1:T(8,128)S(1)}, f32[8,48]{0,1:T(8,128)S(1)}, u32[]{:S(2)}, u32[]{:S(2)}) collective-permute-start(f32[8,48]{0,1:T(8,128)S(1)} %fusion.13), channel_id=1, source_target_pairs={{0,0},{1,4},{2,8},{3,12},{4,16},{5,20},{6,24},{7,28},{8,1},{9,5},{... | collective-permute-start | bytes 4616 | tf_op jit(solution)/shard_map/ppermute | solution.py:1612
  (57 other events, 411.3 us)
Sparse Core Ops, SparseCore 0:
  22.7 53.8 all-gather.6
  78.1 41.1 all-gather.10
  166.9 35.4 all-gather.12
  259.8 42.7 reduce-scatter.5
  305.1 47.8 reduce-scatter.3
  385.2 28.4 reduce-scatter.7
  422.0 87.9 all-gather.8

commit v4 on v3

--- a/solution.py
+++ b/solution.py
@@ -1433,7 +1433,7 @@
     grad_keys, grad_values = middle[:head_width], middle[head_width:]
 
     grad_raw, cells, grad_embedding, rows_first_scale, sums, head_sums = pl.pallas_call(
-        waits_for(functools.partial(finish_kernel, heads, span), 14, 2),
+        waits_for(functools.partial(finish_kernel, heads, span), 14, 1),
         grid=(blocks,),
         in_specs=[
             by_block(head_width),
@@ -1450,7 +1450,6 @@
             whole(*first_mods.shape),
             whole(model, 4 * head_width),
             whole(model, patch),
-            ANYWHERE,
             ANYWHERE,
         ],
         out_specs=[
@@ -1493,10 +1492,9 @@
         weight_qkvc,
         embedding_t,
         output_sum,
-        got_gu,
-    )
-
-    grad_qkvc = dot(normed, grad_raw, 0, 0).astype(bf16)
+    )
+
+    grad_qkvc = dot(normed, after(grad_raw, got_gu), 0, 0).astype(bf16)
 
     grad_cap = row_scatter(
         after(jnp.concatenate([grad_cap_keys, grad_cap_values], axis=0), grad_raw)

time: 571 us -> 575 us (level)
  the two profiles are of different devices: /device:TPU:7 before, /device:TPU:0 now
where the time goes in v4:
time: 575 us; the launch traced here: 566 us
  waiting for transfers between devices  139 us (24%)
  Pallas kernels  109 us (19%)
  local copies, waits for them, and re-layouts  98.7 us (17%)
  starting transfers between devices  82.6 us (14%)
  other arithmetic  52.6 us (9%)
  matrix products  44.4 us (8%)
  between operations  39.9 us (7%)
    all_to_all x5, waiting for transfers between devices, swap(): return lax.all_to_all(value, axes, 0, 0, tiled=True)  46.6 us
    dot_general x17, matrix products, dot(): lax.dot_general(left, right, (((left_dim,), (right_dim,)), ((), ())), pre...  38.2 us
    all_to_all x5, starting transfers between devices, swap(): return lax.all_to_all(value, axes, 0, 0, tiled=True)  37 us
    pallas_call x1, Pallas kernels, on_device(): pl.pallas_call(functools.partial(middle_kernel, len(pieces), span), grid_...  34.7 us
    reduce_scatter x3, waiting for transfers between devices, to_chunks(): lax.psum_scatter(partial.astype(bf16), 'row', scatter_dimension=0, tiled=...  25.2 us
    ppermute x10, waiting for transfers between devices, pairwise(): return lax.ppermute(value, 'row', [(i, i ^ flip) for i in range(4)])  21.8 us
    ppermute x8, waiting for transfers between devices, onward(): lax.ppermute(value, axis, [(ring[i], ring[(i + 1) % count]) for i in rang...  21.3 us
    all_gather x1, waiting for transfers between devices, on_device(): output_piece = lax.all_gather(output_piece, COL, axis=0, tiled=True)  21.2 us
  transfers between devices with their start and end apart: 48, of which 13 were waited for; matrix products, arithmetic and copies ran while one was open for 28% of the time, Pallas kernels for 13%

profile of v4, /device:TPU:0, one launch (start us, length us, event | category | flops | bytes accessed | tf_op | source)
XLA Modules:
  0.0 566.5 jit_solution(226127982148978278)
XLA Ops:
  13.2 7.4 %all-to-all-start = ((bf16[8,48,896]{2,1,0:T(8,128)(2,1)}), bf16[8,48,896]{2,1,0:T(8,128)(2,1)}, u32[]{:S(2)}, u32[]{:S(2)}) async-start(bf16[8,48,896]{2,1,0:T(8,128)(2,1)} %pad_maximum_fusion.3), calls=%async_computation | async-start | bytes 1376256 | tf_op jit(solution)/shard_map/all_to_all | solution.py:37
  25.9 2.7 broadcast_select_fusion
  33.2 2.4 reshape.363
  38.0 2.4 all-to-all-done
  46.3 4.4 all-to-all-start.1
  50.9 3.0 collective-permute-done.2
  55.1 21.2 %all-gather.7.cloned.1.call-done = bf16[1536,384]{1,0:T(8,128)(2,1)} async-done(((bf16[192,384]{1,0:T(8,128)(2,1)}), bf16[1536,384]{1,0:T(8,128)(2,1)}) %all-gather.7.cloned.1.call-update) | async-done | bytes 1179664 | tf_op jit(solution)/shard_map/all_gather | solution.py:955
  90.7 3.8 concatenate.109
  95.7 4.1 concatenate.116
  108.9 3.8 collective-permute-start.6
  115.7 10.0 %project.1 = (f32[1024,1536]{1,0:T(8,128)}, bf16[1024,1536]{1,0:T(8,128)(2,1)}, bf16[384,1024]{1,0:T(8,128)(2,1)}, bf16[192,1024]{1,0:T(8,128)(2,1)}, bf16[384,1...) custom-call(bf16[1024,144]{1,0:T(8,128)(2,1)} %bitcast.259, bf16[1536,144]{1,0:T(8,128)(2,1)} %bitcast.226, ...), custom_call_target="tpu_custom_call" | custom-call | flops 10000000000 | bytes 30000000 | tf_op jit(solution)/shard_map/project/pallas_call | solution.py:999
  127.1 2.3 collective-permute-start.4
  133.7 7.0 %all-to-all-start.2 = ((bf16[8,240,256]{2,1,0:T(8,128)(2,1)}), bf16[8,240,256]{2,1,0:T(8,128)(2,1)S(1)}, u32[]{:S(2)}, u32[]{:S(2)}) async-start(bf16[8,240,256]{2,1,0:T(8,128)(2,1)} %maximum_add_fusion.1), calls=%async_computation.2 | async-start | bytes 1966080 | tf_op jit(solution)/shard_map/all_to_all | solution.py:37
  144.0 15.4 %attend.1 = (bf16[192,1024]{1,0:T(8,128)(2,1)}, f32[192,1024]{1,0:T(8,128)}, f32[192,1024]{1,0:T(8,128)}, f32[8,1024]{1,0:T(8,128)}) custom-call(s32[32]{0:T(128)} %copy-done.44, s32[4]{0:T(128)} %get-tuple-element.319.refs_1_.low_ref, s32[4]{0:T(128)} %get-tuple-element.318.refs_2_.high_ref, s32[1,1024]{1,0:T(1,128)} %broadcast_in_dim_reshape.3.refs_3_.item_query_ref, ...), custom_call_target="tpu_custom_call" | custom-call | flops 14000000000 | bytes 42000000 | tf_op jit(solution)/shard_map/attend/pallas_call | solution.py:1093
  163.3 3.4 all-to-all-done.2
  167.8 2.0 collective-permute-start.9
  169.8 9.0 %collective-permute-done.8.refs_1_ = bf16[192,1024]{1,0:T(8,128)(2,1)S(1)} collective-permute-done((bf16[192,1024]{1,0:T(8,128)(2,1)S(1)}, bf16[192,1024]{1,0:T(8,128)(2,1)S(1)}, u32[]{:S(2)}, u32[]{:S(2)}) %collective-permute-start.8) | collective-permute-done | bytes 393248 | tf_op jit(solution)/shard_map/ppermute | solution.py:115
  180.8 8.2 %collective-permute-done.10.refs_3_ = bf16[192,1024]{1,0:T(8,128)(2,1)S(1)} collective-permute-done((bf16[192,1024]{1,0:T(8,128)(2,1)S(1)}, bf16[192,1024]{1,0:T(8,128)(2,1)S(1)}, u32[]{:S(2)}, u32[]{:S(2)}) %collective-permute-start.10) | collective-permute-done | bytes 393248 | tf_op jit(solution)/shard_map/ppermute | solution.py:115
  206.6 3.8 slice.625
  212.6 34.7 %middle.1 = (bf16[1536,1024]{1,0:T(8,128)(2,1)}, f32[1024,1536]{1,0:T(8,128)}, bf16[1024,1536]{1,0:T(8,128)(2,1)}, bf16[1024,512]{1,0:T(8,128)(2,1)}, bf16[1024,...) custom-call(s32[2]{0:T(128)} %pad_add_fusion.1.own_ref.refs_0_, ...), custom_call_target="tpu_custom_call" | custom-call | flops 35000000512 | bytes 105000000 | tf_op jit(solution)/shard_map/middle/pallas_call | solution.py:1161
  247.3 2.2 constant_dynamic-slice_fusion.3
  253.1 2.4 collective-permute-done.19
  261.9 6.8 %convolution_convert_fusion.1 = bf16[1536,1024]{1,0:T(8,128)(2,1)} fusion(bf16[1024,1536]{1,0:T(8,128)(2,1)} %get-tuple-element.68, bf16[1024,1024]{1,0:T(8,128)(2,1)S(1)} %copy-done.59, bf16[]{:T(256)} %bitcast.61), kind=kOutput, calls=%fused_computation.1 | convolution fusion | flops 3223846912 | bytes 8388610 | tf_op jit(solution)/shard_map/dot_general | solution.py:192
  271.4 2.4 fusion.97
  276.1 8.5 %convolution_convert_fusion = bf16[1536,1536]{1,0:T(8,128)(2,1)} fusion(bf16[1536,1024]{1,0:T(8,128)(2,1)S(1)} %copy-done.60, bf16[1024,1536]{1,0:T(8,128)(2,1)} %get-tuple-element.71, bf16[]{:T(256)} %bitcast.63), kind=kOutput, calls=%fused_computation | convolution fusion | flops 4835770368 | bytes 11010050 | tf_op jit(solution)/shard_map/dot_general | solution.py:192
  288.8 4.0 collective-permute-done.18
  293.4 2.6 fusion.96
  298.1 9.8 %result.1 = (f32[1024,144]{1,0:T(8,128)}, f32[144,1536]{1,0:T(8,128)}, f32[16,1536]{1,0:T(8,128)}) custom-call(s32[2]{0:T(128)} %pad_add_fusion.1.own_ref.refs_0_, bf16[1024,512]{1,0:T(8,128)(2,1)} %get-tuple-element.72.refs_1_, f32[1024,1536]{1,0:T(8,128)} %get-tuple-element.73.refs_2_, bf16[1024,144]{1,0:T(8,128)(2,1)} %bitcast.263, ...), custom_call_target="tpu_custom_call" | custom-call | flops 8999999488 | bytes 27000000 | tf_op jit(solution)/shard_map/result/pallas_call | solution.py:1225
  314.4 15.9 %attend_back.1 = (f32[192,1024]{1,0:T(8,128)}, f32[384,2048]{1,0:T(8,128)}) custom-call(s32[32]{0:T(128)} %copy-done.44, s32[4]{0:T(128)} %get-tuple-element.319.refs_1_.low_ref, s32[4]{0:T(128)} %get-tuple-element.318.refs_2_.high_ref, s32[1,1024]{1,0:T(1,128)} %broadcast_in_dim_reshape.3.refs_3_.item_query_ref, ...), custom_call_target="tpu_custom_call" | custom-call | flops 14000000000 | bytes 42000000 | tf_op jit(solution)/shard_map/attend_back/pallas_call | solution.py:1359
  332.2 3.0 fusion.3
  342.4 2.0 collective-permute-start.24
  345.7 7.2 %cross_back.1 = (bf16[192,1024]{1,0:T(8,128)(2,1)}, f32[192,256]{1,0:T(8,128)}, f32[192,256]{1,0:T(8,128)}, f32[192,128]{1,0:T(8,128)}) custom-call(bf16[192,1024]{1,0:T(8,128)(2,1)} %get-tuple-element.64.refs_8_.cross_ref, bf16[192,256]{1,0:T(8,128)(2,1)} %get-tuple-element.303.refs_9_.caption_key_ref, ...), custom_call_target="tpu_custom_call" | custom-call | flops 7000000000 | bytes 21000000 | tf_op jit(solution)/shard_map/cross_back/pallas_call | solution.py:1330
  357.9 13.3 %finish.1 = (bf16[1024,768]{1,0:T(8,128)(2,1)}, f32[1024,144]{1,0:T(8,128)}, f32[144,1536]{1,0:T(8,128)}, f32[16,1536]{1,0:T(8,128)}, f32[8,1536]{1,0:T(8,128)}, /*index=5*/f32[192,128]{1,0:T(8,128)}) custom-call(f32[192,1024]{1,0:T(8,128)} %get-tuple-element.79.refs_0_, f32[192,1024]{1,0:T(8,128)} %get-tuple-element.263.refs_1_, ...), custom_call_target="tpu_custom_call" | custom-call | flops 12999999488 | bytes 39000000 | tf_op jit(solution)/shard_map/finish/pallas_call | solution.py:1435
  383.2 2.1 collective-permute-start.29
  385.3 25.2 %reduce-scatter.6.cloned.1.call-done = bf16[384,1024]{1,0:T(8,128)(2,1)} async-done(((bf16[1536,1024]{1,0:T(8,128)(2,1)}), bf16[384,1024]{1,0:T(8,128)(2,1)}) %reduce-scatter.6.cloned.1.call-update) | async-done | bytes 786448 | tf_op jit(solution)/shard_map/reduce_scatter | solution.py:1315
  410.5 2.1 broadcast_add_fusion.1
  412.5 5.0 all-to-all-start.3
  418.7 19.9 %all-to-all-done.3.refs_0_ = bf16[8,48,1024]{2,1,0:T(8,128)(2,1)S(1)} async-done(((bf16[8,48,1024]{2,1,0:T(8,128)(2,1)}), bf16[8,48,1024]{2,1,0:T(8,128)(2,1)S(1)}, u32[]{:S(2)}, u32[]{:S(2)}) %all-to-all-start.3) | async-done | bytes 786464 | tf_op jit(solution)/shard_map/all_to_all | solution.py:37
  439.7 5.0 convolution_convert_fusion.2
  457.3 4.5 collective-permute-start.35
  462.4 18.8 %collective-permute-done.27 = bf16[384,768]{1,0:T(8,128)(2,1)} collective-permute-done((bf16[384,768]{1,0:T(8,128)(2,1)}, bf16[384,768]{1,0:T(8,128)(2,1)}, u32[]{:S(2)}, u32[]{:S(2)}) %collective-permute-start.27) | collective-permute-done | bytes 589856 | tf_op jit(solution)/shard_map/ppermute | solution.py:65
  482.4 4.4 concatenate.132
  486.8 13.1 %all-to-all-start.4 = ((bf16[8,48,2744]{2,1,0:T(8,128)(2,1)}), bf16[8,48,2744]{2,1,0:T(8,128)(2,1)S(1)}, u32[]{:S(2)}, u32[]{:S(2)}) async-start(bf16[8,48,2744]{2,1,0:T(8,128)(2,1)} %concatenate.132), calls=%async_computation.6 | async-start | bytes 4325376 | tf_op jit(solution)/shard_map/all_to_all | solution.py:37
  500.0 2.3 slice.659
  505.4 2.5 slice_convert_fusion
  507.9 2.7 reshape.389
  526.1 2.6 fusion.57
  530.4 21.0 %all-to-all-done.4.refs_0_ = bf16[8,48,2744]{2,1,0:T(8,128)(2,1)S(1)} async-done(((bf16[8,48,2744]{2,1,0:T(8,128)(2,1)}), bf16[8,48,2744]{2,1,0:T(8,128)(2,1)S(1)}, u32[]{:S(2)}, u32[]{:S(2)}) %all-to-all-start.4) | async-done | bytes 2107424 | tf_op jit(solution)/shard_map/all_to_all | solution.py:37
  (446 shorter events, 164.2 us)
Async XLA Ops:
  13.2 27.1 %all-to-all-start = ((bf16[8,48,896]{2,1,0:T(8,128)(2,1)}), bf16[8,48,896]{2,1,0:T(8,128)(2,1)}, u32[]{:S(2)}, u32[]{:S(2)}) async-start(bf16[8,48,896]{2,1,0:T(8,128)(2,1)} %pad_maximum_fusion.3), calls=%async_computation | async-start | bytes 1376256 | tf_op jit(solution)/shard_map/all_to_all | solution.py:37
  20.6 55.6 %all-gather.7.cloned.1.call-start = ((), (), s32[]{:S(2)}) async-start(), calls=%async_computation.8 | async-start | bytes 1327104 | tf_op jit(solution)/shard_map/all_gather | solution.py:955
  41.5 12.4 %collective-permute-start.2 = (bf16[8,48,768]{2,1,0:T(8,128)(2,1)S(1)}, bf16[8,48,768]{2,1,0:T(8,128)(2,1)S(1)}, u32[]{:S(2)}, u32[]{:S(2)}) collective-permute-start(bf16[8,48,768]{2,1,0:T(8,128)(2,1)S(1)} %slice.606), channel_id=1, source_target_pairs={{0,16},{8,24},{16,0},{24,8},{1,17},{9,25},{17,1},{25,9},{2,18},{10... | collective-permute-start | bytes 1769480 | tf_op jit(solution)/shard_map/ppermute | solution.py:65
  46.3 58.9 %all-to-all-start.1 = ((bf16[8,48,1792]{2,1,0:T(8,128)(2,1)}), bf16[8,48,1792]{2,1,0:T(8,128)(2,1)}, u32[]{:S(2)}, u32[]{:S(2)}) async-start(bf16[8,48,1792]{2,1,0:T(8,128)(2,1)} %maximum_add_fusion), calls=%async_computation.1 | async-start | bytes 2752512 | tf_op jit(solution)/shard_map/all_to_all | solution.py:37
  50.7 110.7 %all-gather.11.cloned.1.call-start = ((), (), s32[]{:S(2)}) async-start(), calls=%async_computation.13 | async-start | bytes 5898240 | tf_op jit(solution)/shard_map/all_gather | solution.py:956
  77.4 22.5 %collective-permute-start.3 = (bf16[2,8,48,768]{3,2,1,0:T(8,128)(2,1)}, bf16[2,8,48,768]{3,2,1,0:T(8,128)(2,1)}, u32[]{:S(2)}, u32[]{:S(2)}) collective-permute-start(bf16[2,8,48,768]{3,2,1,0:T(8,128)(2,1)} %pad_maximum_fusion.1), channel_id=1, source_target_pairs={{0,8},{8,0},{16,24},{24,16},{1,9},{9,1},{17,25},{25,17},{2,10},{10... | collective-permute-start | bytes 3538952 | tf_op jit(solution)/shard_map/ppermute | solution.py:65
  80.8 7.6 %collective-permute-start = (bf16[1,64,32]{2,1,0:T(8,128)(2,1)S(1)}, bf16[1,64,32]{2,1,0:T(8,128)(2,1)S(1)}, u32[]{:S(2)}, u32[]{:S(2)}) collective-permute-start(bf16[1,64,32]{2,1,0:T(8,128)(2,1)S(1)} %get-tuple-element.294), channel_id=1, source_target_pairs={{0,8},{8,16},{16,24},{1,9},{9,17},{17,25},{2,10},{10,18},{18,26},{... | collective-permute-start | bytes 12296 | tf_op jit(solution)/shard_map/ppermute | solution.py:204
  82.8 5.6 collective-permute-start.1
  108.9 16.8 %collective-permute-start.6 = (bf16[48,768]{1,0:T(8,128)(2,1)S(1)}, bf16[48,768]{1,0:T(8,128)(2,1)S(1)}, u32[]{:S(2)}, u32[]{:S(2)}) collective-permute-start(bf16[48,768]{1,0:T(8,128)(2,1)S(1)} %pad_maximum_fusion.13), channel_id=1, source_target_pairs={{0,16},{8,24},{16,0},{24,8},{1,17},{9,25},{17,1},{25,9},{2,18},{10... | collective-permute-start | bytes 221192 | tf_op jit(solution)/shard_map/ppermute | solution.py:65
  125.8 15.0 %collective-permute-start.7 = (bf16[2,48,768]{2,1,0:T(8,128)(2,1)S(1)}, bf16[2,48,768]{2,1,0:T(8,128)(2,1)S(1)}, u32[]{:S(2)}, u32[]{:S(2)}) collective-permute-start(bf16[2,48,768]{2,1,0:T(8,128)(2,1)S(1)} %pad_maximum_fusion.11), channel_id=1, source_target_pairs={{0,8},{8,0},{16,24},{24,16},{1,9},{9,1},{17,25},{25,17},{2,10},{10... | collective-permute-start | bytes 442376 | tf_op jit(solution)/shard_map/ppermute | solution.py:65
  127.1 16.2 %collective-permute-start.4 = (bf16[384,512]{1,0:T(8,128)(2,1)S(1)}, bf16[384,512]{1,0:T(8,128)(2,1)S(1)}, u32[]{:S(2)}, u32[]{:S(2)}) collective-permute-start(bf16[384,512]{1,0:T(8,128)(2,1)S(1)} %get-tuple-element.269), channel_id=1, source_target_pairs={{0,8},{8,16},{16,24},{1,9},{9,17},{17,25},{2,10},{10,18},{18,26},{... | collective-permute-start | bytes 1179656 | tf_op jit(solution)/shard_map/ppermute | solution.py:204
  129.5 13.8 %collective-permute-start.5 = (bf16[384,512]{1,0:T(8,128)(2,1)S(1)}, bf16[384,512]{1,0:T(8,128)(2,1)}, u32[]{:S(2)}, u32[]{:S(2)}) collective-permute-start(bf16[384,512]{1,0:T(8,128)(2,1)S(1)} %get-tuple-element.268), channel_id=1, source_target_pairs={{8,0},{16,8},{24,16},{9,1},{17,9},{25,17},{10,2},{18,10},{26,18},{... | collective-permute-start | bytes 1179656 | tf_op jit(solution)/shard_map/ppermute | solution.py:204
  133.7 32.9 %all-to-all-start.2 = ((bf16[8,240,256]{2,1,0:T(8,128)(2,1)}), bf16[8,240,256]{2,1,0:T(8,128)(2,1)S(1)}, u32[]{:S(2)}, u32[]{:S(2)}) async-start(bf16[8,240,256]{2,1,0:T(8,128)(2,1)} %maximum_add_fusion.1), calls=%async_computation.2 | async-start | bytes 1966080 | tf_op jit(solution)/shard_map/all_to_all | solution.py:37
  140.7 65.9 %all-gather.13.cloned.1.call-start = ((), (), s32[]{:S(2)}) async-start(), calls=%async_computation.14 | async-start | bytes 4915200 | tf_op jit(solution)/shard_map/all_gather | solution.py:1143
  167.7 190.2 %reduce-scatter.4.cloned.1.call-start = ((), (), s32[]{:S(2)}) async-start(), calls=%async_computation.9 | async-start | bytes 5898240 | tf_op jit(solution)/shard_map/reduce_scatter | solution.py:1315
  167.8 11.1 %collective-permute-start.8 = (bf16[192,1024]{1,0:T(8,128)(2,1)S(1)}, bf16[192,1024]{1,0:T(8,128)(2,1)S(1)}, u32[]{:S(2)}, u32[]{:S(2)}) collective-permute-start(bf16[192,1024]{1,0:T(8,128)(2,1)S(1)} %copy-done.47), channel_id=1, source_target_pairs={{0,2},{2,4},{4,6},{6,7},{7,5},{5,3},{3,1},{1,0},{8,10},{10,12},{12... | collective-permute-start | bytes 1179656 | tf_op jit(solution)/shard_map/ppermute | solution.py:115
  167.8 11.3 %collective-permute-start.9 = (bf16[192,1024]{1,0:T(8,128)(2,1)S(1)}, bf16[192,1024]{1,0:T(8,128)(2,1)S(1)}, u32[]{:S(2)}, u32[]{:S(2)}) collective-permute-start(bf16[192,1024]{1,0:T(8,128)(2,1)S(1)} %copy-done.47), channel_id=1, source_target_pairs={{2,0},{4,2},{6,4},{7,6},{5,7},{3,5},{1,3},{0,1},{10,8},{12,10},{14... | collective-permute-start | bytes 1179656 | tf_op jit(solution)/shard_map/ppermute | solution.py:118
  178.8 10.3 %collective-permute-start.10 = (bf16[192,1024]{1,0:T(8,128)(2,1)S(1)}, bf16[192,1024]{1,0:T(8,128)(2,1)S(1)}, u32[]{:S(2)}, u32[]{:S(2)}) collective-permute-start(bf16[192,1024]{1,0:T(8,128)(2,1)S(1)} %collective-permute-done.8.refs_1_), channel_id=1, source_target_pairs={{0,2},{2,4},{4,6},{6,7},{7,5},{5,3},{3,1},{1,0},{8,10},{10,12},{12... | collective-permute-start | bytes 1179656 | tf_op jit(solution)/shard_map/ppermute | solution.py:115
  179.1 10.6 %collective-permute-start.11 = (bf16[192,1024]{1,0:T(8,128)(2,1)S(1)}, bf16[192,1024]{1,0:T(8,128)(2,1)S(1)}, u32[]{:S(2)}, u32[]{:S(2)}) collective-permute-start(bf16[192,1024]{1,0:T(8,128)(2,1)S(1)} %collective-permute-done.9.refs_2_), channel_id=1, source_target_pairs={{2,0},{4,2},{6,4},{7,6},{5,7},{3,5},{1,3},{0,1},{10,8},{12,10},{14... | collective-permute-start | bytes 1179656 | tf_op jit(solution)/shard_map/ppermute | solution.py:118
  189.1 15.2 %collective-permute-start.12 = (bf16[192,1024]{1,0:T(8,128)(2,1)S(1)}, bf16[192,1024]{1,0:T(8,128)(2,1)S(1)}, u32[]{:S(2)}, u32[]{:S(2)}) collective-permute-start(bf16[192,1024]{1,0:T(8,128)(2,1)S(1)} %collective-permute-done.10.refs_3_), channel_id=1, source_target_pairs={{0,2},{2,4},{4,6},{6,7},{7,5},{5,3},{3,1},{1,0},{8,10},{10,12},{12... | collective-permute-start | bytes 1179656 | tf_op jit(solution)/shard_map/ppermute | solution.py:115
  189.7 15.2 %collective-permute-start.13 = (bf16[192,1024]{1,0:T(8,128)(2,1)S(1)}, bf16[192,1024]{1,0:T(8,128)(2,1)S(1)}, u32[]{:S(2)}, u32[]{:S(2)}) collective-permute-start(bf16[192,1024]{1,0:T(8,128)(2,1)S(1)} %collective-permute-done.11.refs_4_), channel_id=1, source_target_pairs={{2,0},{4,2},{6,4},{7,6},{5,7},{3,5},{1,3},{0,1},{10,8},{12,10},{14... | collective-permute-start | bytes 1179656 | tf_op jit(solution)/shard_map/ppermute | solution.py:118
  204.3 8.4 %collective-permute-start.14 = (bf16[96,1024]{1,0:T(8,128)(2,1)S(1)}, bf16[96,1024]{1,0:T(8,128)(2,1)}, u32[]{:S(2)}, u32[]{:S(2)}) collective-permute-start(bf16[96,1024]{1,0:T(8,128)(2,1)S(1)} %slice.622), channel_id=1, source_target_pairs={{0,2},{2,4},{4,6},{6,7},{7,5},{5,3},{3,1},{1,0},{8,10},{10,12},{12... | collective-permute-start | bytes 589832 | tf_op jit(solution)/shard_map/ppermute | solution.py:115
  204.9 7.7 %collective-permute-start.15 = (bf16[96,1024]{1,0:T(8,128)(2,1)S(1)}, bf16[96,1024]{1,0:T(8,128)(2,1)}, u32[]{:S(2)}, u32[]{:S(2)}) collective-permute-start(bf16[96,1024]{1,0:T(8,128)(2,1)S(1)} %slice.623), channel_id=1, source_target_pairs={{2,0},{4,2},{6,4},{7,6},{5,7},{3,5},{1,3},{0,1},{10,8},{12,10},{14... | collective-permute-start | bytes 589832 | tf_op jit(solution)/shard_map/ppermute | solution.py:118
  249.5 6.0 %collective-permute-start.19 = (bf16[96,1024]{1,0:T(8,128)(2,1)}, bf16[96,1024]{1,0:T(8,128)(2,1)}, u32[]{:S(2)}, u32[]{:S(2)}) collective-permute-start(bf16[96,1024]{1,0:T(8,128)(2,1)} %get-tuple-element.259), channel_id=1, source_target_pairs={{2,0},{4,2},{6,4},{7,6},{5,7},{3,5},{1,3},{0,1},{10,8},{12,10},{14... | collective-permute-start | bytes 589832 | tf_op jit(solution)/shard_map/ppermute | solution.py:118
  250.7 7.8 %collective-permute-start.16 = (bf16[96,1024]{1,0:T(8,128)(2,1)}, bf16[96,1024]{1,0:T(8,128)(2,1)S(1)}, u32[]{:S(2)}, u32[]{:S(2)}) collective-permute-start(bf16[96,1024]{1,0:T(8,128)(2,1)} %get-tuple-element.258), channel_id=1, source_target_pairs={{0,2},{2,4},{4,6},{6,7},{7,5},{5,3},{3,1},{1,0},{8,10},{10,12},{12... | collective-permute-start | bytes 589832 | tf_op jit(solution)/shard_map/ppermute | solution.py:115
  257.2 13.4 %collective-permute-start.20 = (bf16[192,1024]{1,0:T(8,128)(2,1)}, bf16[192,1024]{1,0:T(8,128)(2,1)}, u32[]{:S(2)}, u32[]{:S(2)}) collective-permute-start(bf16[192,1024]{1,0:T(8,128)(2,1)} %pad_maximum_fusion.5), channel_id=1, source_target_pairs={{2,0},{4,2},{6,4},{7,6},{5,7},{3,5},{1,3},{0,1},{10,8},{12,10},{14... | collective-permute-start | bytes 1179656 | tf_op jit(solution)/shard_map/ppermute | solution.py:118
  259.3 11.3 %collective-permute-start.17 = (bf16[192,1024]{1,0:T(8,128)(2,1)}, bf16[192,1024]{1,0:T(8,128)(2,1)S(1)}, u32[]{:S(2)}, u32[]{:S(2)}) collective-permute-start(bf16[192,1024]{1,0:T(8,128)(2,1)} %pad_maximum_fusion.4), channel_id=1, source_target_pairs={{0,2},{2,4},{4,6},{6,7},{7,5},{5,3},{3,1},{1,0},{8,10},{10,12},{12... | collective-permute-start | bytes 1179656 | tf_op jit(solution)/shard_map/ppermute | solution.py:115
  284.6 96.4 %reduce-scatter.8.cloned.1.call-start = ((), (), s32[]{:S(2)}) async-start(), calls=%async_computation.11 | async-start | bytes 1966080 | tf_op jit(solution)/shard_map/reduce_scatter | solution.py:1315
  284.7 8.1 %collective-permute-start.18 = (bf16[192,1024]{1,0:T(8,128)(2,1)}, bf16[192,1024]{1,0:T(8,128)(2,1)}, u32[]{:S(2)}, u32[]{:S(2)}) collective-permute-start(bf16[192,1024]{1,0:T(8,128)(2,1)} %get-tuple-element.244), channel_id=1, source_target_pairs={{0,2},{2,4},{4,6},{6,7},{7,5},{5,3},{3,1},{1,0},{8,10},{10,12},{12... | collective-permute-start | bytes 1179656 | tf_op jit(solution)/shard_map/ppermute | solution.py:115
  285.3 8.1 %collective-permute-start.22 = (bf16[192,1024]{1,0:T(8,128)(2,1)S(1)}, bf16[192,1024]{1,0:T(8,128)(2,1)}, u32[]{:S(2)}, u32[]{:S(2)}) collective-permute-start(bf16[192,1024]{1,0:T(8,128)(2,1)S(1)} %get-tuple-element.254), channel_id=1, source_target_pairs={{2,0},{4,2},{6,4},{7,6},{5,7},{3,5},{1,3},{0,1},{10,8},{12,10},{14... | collective-permute-start | bytes 1179656 | tf_op jit(solution)/shard_map/ppermute | solution.py:118
  296.1 17.3 %collective-permute-start.21 = (bf16[192,1024]{1,0:T(8,128)(2,1)S(1)}, bf16[192,1024]{1,0:T(8,128)(2,1)S(1)}, u32[]{:S(2)}, u32[]{:S(2)}) collective-permute-start(bf16[192,1024]{1,0:T(8,128)(2,1)S(1)} %get-tuple-element.242), channel_id=1, source_target_pairs={{0,2},{2,4},{4,6},{6,7},{7,5},{5,3},{3,1},{1,0},{8,10},{10,12},{12... | collective-permute-start | bytes 1179656 | tf_op jit(solution)/shard_map/ppermute | solution.py:115
  297.6 15.8 %collective-permute-start.23 = (bf16[192,1024]{1,0:T(8,128)(2,1)S(1)}, bf16[192,1024]{1,0:T(8,128)(2,1)S(1)}, u32[]{:S(2)}, u32[]{:S(2)}) collective-permute-start(bf16[192,1024]{1,0:T(8,128)(2,1)S(1)} %get-tuple-element.252), channel_id=1, source_target_pairs={{2,0},{4,2},{6,4},{7,6},{5,7},{3,5},{1,3},{0,1},{10,8},{12,10},{14... | collective-permute-start | bytes 1179656 | tf_op jit(solution)/shard_map/ppermute | solution.py:118
  335.2 75.2 %reduce-scatter.6.cloned.1.call-start = ((), (), s32[]{:S(2)}) async-start(), calls=%async_computation.10 | async-start | bytes 3932160 | tf_op jit(solution)/shard_map/reduce_scatter | solution.py:1315
  342.4 12.9 %collective-permute-start.24 = (bf16[384,512]{1,0:T(8,128)(2,1)}, bf16[384,512]{1,0:T(8,128)(2,1)}, u32[]{:S(2)}, u32[]{:S(2)}) collective-permute-start(bf16[384,512]{1,0:T(8,128)(2,1)} %get-tuple-element.264), channel_id=1, source_target_pairs={{0,8},{8,16},{16,24},{1,9},{9,17},{17,25},{2,10},{10,18},{18,26},{... | collective-permute-start | bytes 1179656 | tf_op jit(solution)/shard_map/ppermute | solution.py:204
  344.4 10.9 %collective-permute-start.25 = (bf16[384,512]{1,0:T(8,128)(2,1)S(1)}, bf16[384,512]{1,0:T(8,128)(2,1)}, u32[]{:S(2)}, u32[]{:S(2)}) collective-permute-start(bf16[384,512]{1,0:T(8,128)(2,1)S(1)} %get-tuple-element.265), channel_id=1, source_target_pairs={{8,0},{16,8},{24,16},{9,1},{17,9},{25,17},{10,2},{18,10},{26,18},{... | collective-permute-start | bytes 1179656 | tf_op jit(solution)/shard_map/ppermute | solution.py:204
  377.3 5.7 %collective-permute-start.28 = (bf16[2,344,384]{2,1,0:T(8,128)(2,1)S(1)}, bf16[2,344,384]{2,1,0:T(8,128)(2,1)S(1)}, u32[]{:S(2)}, u32[]{:S(2)}) collective-permute-start(bf16[2,344,384]{2,1,0:T(8,128)(2,1)S(1)} %dynamic-slice_bitcast_fusion.3), channel_id=1, source_target_pairs={{0,8},{8,0},{16,24},{24,16},{1,9},{9,1},{17,25},{25,17},{2,10},{10... | collective-permute-start | bytes 1585160 | tf_op jit(solution)/shard_map/ppermute | solution.py:65
  378.6 4.3 collective-permute-start.32
  382.9 34.9 %collective-permute-start.33 = (bf16[96,256]{1,0:T(8,128)(2,1)S(1)}, bf16[96,256]{1,0:T(8,128)(2,1)S(1)}, u32[]{:S(2)}, u32[]{:S(2)}) collective-permute-start(bf16[96,256]{1,0:T(8,128)(2,1)S(1)} %dynamic-slice_bitcast_fusion.6), channel_id=1, source_target_pairs={{0,16},{8,24},{16,0},{24,8},{1,17},{9,25},{17,1},{25,9},{2,18},{10... | collective-permute-start | bytes 147464 | tf_op jit(solution)/shard_map/ppermute | solution.py:65
  383.2 34.6 %collective-permute-start.29 = (bf16[344,384]{1,0:T(8,128)(2,1)S(1)}, bf16[344,384]{1,0:T(8,128)(2,1)S(1)}, u32[]{:S(2)}, u32[]{:S(2)}) collective-permute-start(bf16[344,384]{1,0:T(8,128)(2,1)S(1)} %dynamic-slice_bitcast_fusion.4), channel_id=1, source_target_pairs={{0,16},{8,24},{16,0},{24,8},{1,17},{9,25},{17,1},{25,9},{2,18},{10... | collective-permute-start | bytes 792584 | tf_op jit(solution)/shard_map/ppermute | solution.py:65
  412.5 26.0 %all-to-all-start.3 = ((bf16[8,48,1024]{2,1,0:T(8,128)(2,1)}), bf16[8,48,1024]{2,1,0:T(8,128)(2,1)S(1)}, u32[]{:S(2)}, u32[]{:S(2)}) async-start(bf16[8,48,1024]{2,1,0:T(8,128)(2,1)} %bitcast.67), calls=%async_computation.5 | async-start | bytes 1572864 | tf_op jit(solution)/shard_map/all_to_all | solution.py:37
  417.5 87.9 %all-gather.9.cloned.1.call-start = ((), (), s32[]{:S(2)}) async-start(), calls=%async_computation.12 | async-start | bytes 2433024 | tf_op jit(solution)/shard_map/all_gather | solution.py:1538
  446.0 5.5 collective-permute-start.26
  454.2 27.0 %collective-permute-start.27 = (bf16[384,768]{1,0:T(8,128)(2,1)}, bf16[384,768]{1,0:T(8,128)(2,1)}, u32[]{:S(2)}, u32[]{:S(2)}) collective-permute-start(bf16[384,768]{1,0:T(8,128)(2,1)} %dynamic-slice_bitcast_fusion.2), channel_id=1, source_target_pairs={{0,16},{8,24},{16,0},{24,8},{1,17},{9,25},{17,1},{25,9},{2,18},{10... | collective-permute-start | bytes 1769480 | tf_op jit(solution)/shard_map/ppermute | solution.py:65
  454.6 7.3 %collective-permute-start.30 = (bf16[1,64,32]{2,1,0:T(8,128)(2,1)S(1)}, bf16[1,64,32]{2,1,0:T(8,128)(2,1)S(1)}, u32[]{:S(2)}, u32[]{:S(2)}) collective-permute-start(bf16[1,64,32]{2,1,0:T(8,128)(2,1)S(1)} %get-tuple-element.270), channel_id=1, source_target_pairs={{0,8},{8,16},{16,24},{1,9},{9,17},{17,25},{2,10},{10,18},{18,26},{... | collective-permute-start | bytes 12296 | tf_op jit(solution)/shard_map/ppermute | solution.py:204
  456.0 5.8 %collective-permute-start.31 = (bf16[1,64,32]{2,1,0:T(8,128)(2,1)S(1)}, bf16[1,64,32]{2,1,0:T(8,128)(2,1)S(1)}, u32[]{:S(2)}, u32[]{:S(2)}) collective-permute-start(bf16[1,64,32]{2,1,0:T(8,128)(2,1)S(1)} %get-tuple-element.271), channel_id=1, source_target_pairs={{8,0},{16,8},{24,16},{9,1},{17,9},{25,17},{10,2},{18,10},{26,18},{... | collective-permute-start | bytes 12296 | tf_op jit(solution)/shard_map/ppermute | solution.py:204
  457.3 44.9 %collective-permute-start.35 = (bf16[128,1536]{1,0:T(8,128)(2,1)}, bf16[128,1536]{1,0:T(8,128)(2,1)}, u32[]{:S(2)}, u32[]{:S(2)}) collective-permute-start(bf16[128,1536]{1,0:T(8,128)(2,1)} %reduce-scatter.8.cloned.1.call-done), channel_id=1, source_target_pairs={{0,0},{1,4},{2,8},{3,12},{4,16},{5,20},{6,24},{7,28},{8,1},{9,5},{... | collective-permute-start | bytes 1179656 | tf_op jit(solution)/shard_map/ppermute | solution.py:1589
  486.8 64.5 %all-to-all-start.4 = ((bf16[8,48,2744]{2,1,0:T(8,128)(2,1)}), bf16[8,48,2744]{2,1,0:T(8,128)(2,1)S(1)}, u32[]{:S(2)}, u32[]{:S(2)}) async-start(bf16[8,48,2744]{2,1,0:T(8,128)(2,1)} %concatenate.132), calls=%async_computation.6 | async-start | bytes 4325376 | tf_op jit(solution)/shard_map/all_to_all | solution.py:37
  519.7 10.0 %collective-permute-start.34 = (f32[8,48]{0,1:T(8,128)S(1)}, f32[8,48]{0,1:T(8,128)S(1)}, u32[]{:S(2)}, u32[]{:S(2)}) collective-permute-start(f32[8,48]{0,1:T(8,128)S(1)} %fusion.14), channel_id=1, source_target_pairs={{0,0},{1,4},{2,8},{3,12},{4,16},{5,20},{6,24},{7,28},{8,1},{9,5},{... | collective-permute-start | bytes 4616 | tf_op jit(solution)/shard_map/ppermute | solution.py:1610
  (62 other events, 486.5 us)
Sparse Core Ops, SparseCore 0:
  24.2 51.9 all-gather.6
  77.8 41.6 all-gather.10
  167.8 31.0 all-gather.12
  284.7 46.9 reduce-scatter.3
  335.4 27.9 reduce-scatter.7
  365.8 44.6 reduce-scatter.5
  422.3 72.5 all-gather.8
